TPU v7x, 32 devices: a whole 2x2x4 slice. The times are simulated.
32 devices in a mesh: ctx: 8 (over y, x, core), tp: 4 (over z).
Axes of the slice: x: 2, y: 2, z: 4, core: 2. Of those that a mesh axis runs over, the one named last changes fastest.
Arguments:
- query_in: bfloat16 [1024, 4096], P('ctx', 'tp'), may hold values from -6 to 6
- key_in: bfloat16 [1024, 4096], P('ctx', 'tp'), may hold values from -6 to 6
- value_in: bfloat16 [1024, 4096], P('ctx', 'tp'), may hold values from -6 to 6
- long_filter: bfloat16 [1024, 4096], P('ctx', 'tp'), may hold values from -1.1 to 1.1
- short_taps: bfloat16 [3, 3, 4096], P(None, None, 'tp'), may hold values from -3.5 to 3.5
- out_grad: bfloat16 [1024, 4096], P('ctx', 'tp'), may hold values from -6 to 6
Outputs:
- output: bfloat16 [1024, 4096], P('ctx', 'tp')
- query_grad: bfloat16 [1024, 4096], P('ctx', 'tp')
- key_grad: bfloat16 [1024, 4096], P('ctx', 'tp')
- value_grad: bfloat16 [1024, 4096], P('ctx', 'tp')
- filter_grad: float32 [1024, 4096], P('ctx', 'tp')
- taps_grad: float32 [3, 3, 4096], P(None, None, 'tp')
All inputs are finite; a program needn't handle non-finite values.
Results may differ from a plain program's by a relative error of at most 0.001.
Values may be sent and summed in bfloat16 or wider, within the bound.
No kernel may reach another device: no remote copies, remote signals or barrier semaphores. Data moves between devices by JAX's collectives and lax.ppermute only.
A program may use at most 64 MiB of HBM per device.

v0:
```python
from functools import lru_cache, partial
import math

import jax
import jax.numpy as jnp
import ml_dtypes
import numpy as np
from jax import lax
from jax.experimental import pallas as pl
from jax.experimental.pallas import tpu as pltpu
from jax.sharding import PartitionSpec as P

HIGHEST_PREC = lax.Precision.HIGHEST
TWO_PI = 2.0 * math.pi


def passed_along(block, axis, distance):
    devices = range(lax.axis_size(axis))
    route = [(i - distance, i) for i in devices if i - distance in devices]
    return lax.ppermute(block, axis, route)


def phase_pair(count_a, count_b, period, direction):
    product = (
        jnp.arange(count_a, dtype=jnp.int32)[:, None]
        * jnp.arange(count_b, dtype=jnp.int32)[None, :]
    )
    phase_angle = direction * TWO_PI / period * (product % period).astype(jnp.float32)
    return (jnp.cos(phase_angle), jnp.sin(phase_angle))


def rotate_pair(real_part, imag_part, cosine, sine_part):
    return (real_part * cosine - imag_part * sine_part, real_part * sine_part + imag_part * cosine)


def times_pair(first_pair, second_pair, conj_second):
    factor = -1.0 if conj_second else 1.0
    real_part = first_pair[0] * second_pair[0] - factor * first_pair[1] * second_pair[1]
    imag_part = first_pair[1] * second_pair[0] + factor * first_pair[0] * second_pair[1]
    return (real_part, imag_part)


def unpack_fields(spectrum, comp_axis, field_axis):
    collected = []
    for partner_rank in range(spectrum.shape[field_axis]):
        single = lax.index_in_dim(spectrum, partner_rank, field_axis, keepdims=True)
        collected.append(
            (
                lax.index_in_dim(single, 0, comp_axis, keepdims=True),
                lax.index_in_dim(single, 1, comp_axis, keepdims=True),
            )
        )
    return collected


def pack_fields(pairs, comp_axis, field_axis):
    return jnp.concatenate(
        [jnp.concatenate([real_part, imag_part], axis=comp_axis) for real_part, imag_part in pairs],
        axis=field_axis,
    )


def spread_forward(regroup, fields):
    row_count, field_count, channels = fields.shape
    part_count = lax.axis_size("ctx")
    block_rows = row_count // part_count
    length = 2 * part_count * row_count
    my_index = lax.axis_index("ctx")
    gathered = regroup(fields.reshape(part_count, 1, block_rows, field_count, channels))
    cosine, sine_part = phase_pair(2 * part_count, part_count, 2 * part_count, -1.0)
    first_table = jnp.stack([cosine, sine_part], axis=1)
    first_pass = jnp.einsum("kda,arfc->kdrfc", first_table, gathered, precision=HIGHEST_PREC)
    row_index = my_index * block_rows + jnp.arange(block_rows, dtype=jnp.int32)
    twist_index = jnp.arange(2 * part_count, dtype=jnp.int32)[:, None] * row_index[None, :] % length
    phase_angle = -TWO_PI / length * twist_index.astype(jnp.float32)
    cos_twist = jnp.cos(phase_angle)[:, :, None, None]
    sin_twist = jnp.sin(phase_angle)[:, :, None, None]
    real_part, imag_part = rotate_pair(first_pass[:, 0], first_pass[:, 1], cos_twist, sin_twist)
    turned = jnp.stack([real_part, imag_part], axis=1)
    arrived = regroup(turned.reshape(part_count, 1, 2, 2, block_rows, field_count, channels))
    cosine, sine_part = phase_pair(row_count, row_count, row_count, -1.0)
    second_table = jnp.stack(
        [jnp.stack([cosine, sine_part], axis=-1), jnp.stack([-sine_part, cosine], axis=-1)], axis=0
    )
    second_table = second_table.reshape(2, part_count, block_rows, row_count, 2)
    return jnp.einsum("pqsrfc,sprkd->qkdfc", arrived, second_table, precision=HIGHEST_PREC)


def spread_inverse(regroup, spectrum):
    pair_count, row_count, _, field_count, channels = spectrum.shape
    part_count = lax.axis_size("ctx")
    block_rows = row_count // part_count
    length = 2 * part_count * row_count
    my_index = lax.axis_index("ctx")
    cosine, sine_part = phase_pair(row_count, row_count, row_count, 1.0)
    second_table = jnp.stack(
        [jnp.stack([cosine, sine_part], axis=-1), jnp.stack([-sine_part, cosine], axis=-1)], axis=0
    )
    second_table = second_table.reshape(2, row_count, part_count, block_rows, 2)
    row_parts = jnp.einsum("qkdfc,dkprs->pqsrfc", spectrum, second_table, precision=HIGHEST_PREC)
    freq_index = my_index * pair_count + jnp.arange(pair_count, dtype=jnp.int32)
    twist_index = freq_index[:, None] * jnp.arange(row_count, dtype=jnp.int32)[None, :] % length
    phase_angle = TWO_PI / length * twist_index.astype(jnp.float32)
    cos_twist = (
        jnp.cos(phase_angle)
        .reshape(pair_count, part_count, block_rows)
        .transpose(1, 0, 2)[:, :, :, None, None]
    )
    sin_twist = (
        jnp.sin(phase_angle)
        .reshape(pair_count, part_count, block_rows)
        .transpose(1, 0, 2)[:, :, :, None, None]
    )
    real_part, imag_part = rotate_pair(row_parts[:, :, 0], row_parts[:, :, 1], cos_twist, sin_twist)
    turned = jnp.stack([real_part, imag_part], axis=2)
    arrived = regroup(
        turned.reshape(part_count, 1, pair_count, 2, block_rows, field_count, channels)
    )
    cosine, sine_part = phase_pair(2 * part_count, part_count, 2 * part_count, 1.0)
    first_table = (jnp.stack([cosine, -sine_part], axis=1) / length).reshape(
        part_count, pair_count, 2, part_count
    )
    values = jnp.einsum("pqsrfc,pqsa->arfc", arrived, first_table, precision=HIGHEST_PREC)
    returned = regroup(values.reshape(part_count, 1, block_rows, field_count, channels))
    return returned.reshape(row_count, field_count, channels)


def local_general(query_in, key_in, value_in, long_filter, short_taps, out_grad):
    row_count = query_in.shape[0]
    tap_count = short_taps.shape[1]
    margin = tap_count - 1
    part_count = lax.axis_size("ctx")

    def regroup(blocks):
        return lax.all_to_all(blocks, "ctx", split_axis=0, concat_axis=1, tiled=True)[0]

    to_freq = partial(spread_forward, regroup)
    from_freq = partial(spread_inverse, regroup)
    comp_axis = 2
    field_axis = 3
    inputs = jnp.stack([query_in, key_in, value_in])
    earlier = passed_along(inputs[:, row_count - margin :], "ctx", 1)
    extended = jnp.concatenate([earlier, inputs], axis=1).astype(jnp.float32)
    tap_gain = short_taps.astype(jnp.float32)
    filtered = tap_gain[:, 0, None, :] * extended[:, margin:]
    for offset in range(1, tap_count):
        filtered = (
            filtered
            + tap_gain[:, offset, None, :]
            * extended[:, margin - offset : margin - offset + row_count]
        )
    query_filt = filtered[0]
    key_filt = filtered[1]
    value_filt = filtered[2]
    mixed_in = key_filt * value_filt
    spectra = to_freq(jnp.stack([mixed_in, long_filter.astype(jnp.float32)], axis=1))
    mixed_spec, filter_spec = unpack_fields(spectra, comp_axis, field_axis)
    convolved = from_freq(
        pack_fields([times_pair(mixed_spec, filter_spec, False)], comp_axis, field_axis)
    )[:, 0]
    output = (query_filt * convolved).astype(jnp.bfloat16)
    grad_in = out_grad.astype(jnp.float32)
    gate_grad = grad_in * convolved
    conv_grad = grad_in * query_filt
    grad_spec = unpack_fields(to_freq(conv_grad[:, None, :]), comp_axis, field_axis)[0]
    returned = from_freq(
        pack_fields(
            [times_pair(grad_spec, filter_spec, True), times_pair(grad_spec, mixed_spec, True)],
            comp_axis,
            field_axis,
        )
    )
    grad_scale = 1.0 / math.sqrt(part_count * row_count)
    mixed_grad = returned[:, 0]
    filter_grad = returned[:, 1] * grad_scale
    grad_stack = jnp.stack([gate_grad, mixed_grad * value_filt, mixed_grad * key_filt])
    later_rows = passed_along(grad_stack[:, :margin], "ctx", -1)
    padded_grad = jnp.concatenate([grad_stack, later_rows], axis=1)
    input_grads = tap_gain[:, 0, None, :] * grad_stack
    for offset in range(1, tap_count):
        input_grads = (
            input_grads + tap_gain[:, offset, None, :] * padded_grad[:, offset : offset + row_count]
        )
    partial_taps = jnp.stack(
        [
            jnp.sum(grad_stack * extended[:, margin - offset : margin - offset + row_count], axis=1)
            for offset in range(tap_count)
        ],
        axis=1,
    )
    taps_grad = lax.psum(partial_taps, "ctx") * grad_scale
    return (
        output,
        input_grads[0].astype(jnp.bfloat16),
        input_grads[1].astype(jnp.bfloat16),
        input_grads[2].astype(jnp.bfloat16),
        filter_grad,
        taps_grad,
    )


RADIX = 8
FIELD_NAMES = ("query", "key", "value", "filter", "out_grad")
CLASSES = (0, 8, 4, 2, 6, 1, 5, 9, 13)
LANES = 128
PAD = 8
CHUNK = 16


def split_pair(values):
    high = values.astype(jnp.bfloat16)
    low = (values - high.astype(jnp.float32)).astype(jnp.bfloat16)
    return high, low


@lru_cache(maxsize=None)
def class_tables(rows):
    length = 2 * RADIX * rows
    back = np.arange(rows)
    forward, inverse = [], []
    for residue in CLASSES:
        product = np.outer(2 * RADIX * back + residue, back) % length
        angle = -2.0 * np.pi * product / length
        cosine, sine = np.cos(angle), np.sin(angle)
        forward.append(np.block([[cosine, -sine], [sine, cosine]]))
        weight = (1.0 if residue in (0, RADIX) else 2.0) / length
        inverse.append(weight * np.block([[cosine.T, sine.T], [-sine.T, cosine.T]]))
    tables = []
    for table in (np.stack(forward), np.stack(inverse)):
        high = table.astype(ml_dtypes.bfloat16)
        low = (table - high.astype(np.float64)).astype(ml_dtypes.bfloat16)
        tables += [high, low]
    return tables


ROOT = math.sqrt(0.5)
COS1 = math.cos(math.pi / 8)
SIN1 = math.sin(math.pi / 8)


def forward_classes(x):
    u = [x[a] + x[a + 4] for a in range(4)]
    d = [x[a] - x[a + 4] for a in range(4)]
    even, odd = u[0] + u[2], u[1] + u[3]
    dif, tot = ROOT * (d[1] - d[3]), ROOT * (d[1] + d[3])
    found = [
        (even + odd, None),
        (even - odd, None),
        (u[0] - u[2], u[3] - u[1]),
        (d[0] + dif, -d[2] - tot),
        (d[0] - dif, d[2] - tot),
    ]
    w0 = (x[0], -x[4])
    w1 = (COS1 * x[1] - SIN1 * x[5], -SIN1 * x[1] - COS1 * x[5])
    w2 = (ROOT * (x[2] - x[6]), -ROOT * (x[2] + x[6]))
    w3 = (SIN1 * x[3] - COS1 * x[7], -COS1 * x[3] - SIN1 * x[7])
    s02 = (w0[0] + w2[0], w0[1] + w2[1])
    d02 = (w0[0] - w2[0], w0[1] - w2[1])
    s13 = (w1[0] + w3[0], w1[1] + w3[1])
    d13 = (w1[0] - w3[0], w1[1] - w3[1])
    found.append((s02[0] + s13[0], s02[1] + s13[1]))
    found.append((d02[0] + d13[1], d02[1] - d13[0]))
    found.append((s02[0] - s13[0], s02[1] - s13[1]))
    found.append((d02[0] - d13[1], d02[1] + d13[0]))
    return found


def inverse_classes(z):
    (z0, _), (z8, _), (r4, i4), (r2, i2), (r6, i6) = z[:5]
    up, down = z0 + z8, z0 - z8
    even = [up + r4, down - i4, up - r4, down + i4]
    gap, tot = ROOT * (r2 - r6), ROOT * (i2 + i6)
    turn = [r2 + r6, gap - tot, i6 - i2, -gap - tot]
    (r1, i1), (r5, i5), (r9, i9), (rd, id_) = z[5:]
    s = (r1 + r9, i1 + i9)
    d = (r1 - r9, i1 - i9)
    t = (r5 + rd, i5 + id_)
    e = (r5 - rd, i5 - id_)
    s0 = (s[0] + t[0], s[1] + t[1])
    s2 = (s[0] - t[0], s[1] - t[1])
    s1 = (d[0] - e[1], d[1] + e[0])
    s3 = (d[0] + e[1], d[1] - e[0])
    q = [
        s0,
        (COS1 * s1[0] - SIN1 * s1[1], SIN1 * s1[0] + COS1 * s1[1]),
        (ROOT * (s2[0] - s2[1]), ROOT * (s2[0] + s2[1])),
        (SIN1 * s3[0] - COS1 * s3[1], COS1 * s3[0] + SIN1 * s3[1]),
    ]
    return [even[a] + turn[a] + q[a][0] for a in range(4)] + [
        even[a] - turn[a] - q[a][1] for a in range(4)
    ]


def layer_kernel(
    taps_ref, got_ref, fh_ref, fl_ref, ih_ref, il_ref, out_ref,
    qp, kp, vp, qs, ks, vs, xh, xl, zs, g0, g1, g2, sums,
):
    blocks, height, _ = got_ref.shape
    rows = height // len(FIELD_NAMES)
    total = blocks * rows
    chunks = rows // CHUNK
    f32 = jnp.float32
    zero = jnp.zeros((PAD, LANES), f32)
    for ref in (qp, kp, vp):
        ref[pl.ds(0, PAD), :] = zero
    for ref in (g0, g1, g2):
        ref[pl.ds(total, PAD), :] = zero
    gain = [[taps_ref[3 * i + j : 3 * i + j + 1, :] for j in range(3)] for i in range(3)]

    def widen(step, carry):
        b0 = pl.multiple_of(step * CHUNK, CHUNK)
        for a in range(blocks):
            for field, ref in enumerate((qp, kp, vp)):
                ref[pl.ds(PAD + a * rows + b0, CHUNK), :] = got_ref[
                    a, pl.ds(field * rows + b0, CHUNK), :
                ].astype(f32)
        return carry

    lax.fori_loop(0, chunks, widen, 0)
    for f in (0, 1):
        xh[f, pl.ds(rows, rows), :] = jnp.zeros((rows, 3 * LANES), jnp.bfloat16)
        xl[f, pl.ds(rows, rows), :] = jnp.zeros((rows, 3 * LANES), jnp.bfloat16)

    def short(ref, i, at):
        return (
            gain[i][0] * ref[pl.ds(at, CHUNK), :]
            + gain[i][1] * ref[pl.ds(at - 1, CHUNK), :]
            + gain[i][2] * ref[pl.ds(at - 2, CHUNK), :]
        )

    def enter(step, carry):
        b0 = pl.multiple_of(step * CHUNK, CHUNK)

        def put(column, values):
            for f, (real, imag) in enumerate(forward_classes(values)):
                for part, value in ((0, real), (1, imag)):
                    if value is not None:
                        high, low = split_pair(value)
                        place = (f, pl.ds(part * rows + b0, CHUNK), pl.ds(column * LANES, LANES))
                        xh[place] = high
                        xl[place] = low

        mixed = []
        for a in range(blocks):
            at = a * rows + b0
            key_filt = short(kp, 1, PAD + at)
            value_filt = short(vp, 2, PAD + at)
            ks[pl.ds(at, CHUNK), :] = key_filt
            vs[pl.ds(at, CHUNK), :] = value_filt
            mixed.append(key_filt * value_filt)
        put(0, mixed)
        put(1, [got_ref[a, pl.ds(3 * rows + b0, CHUNK), :].astype(f32) for a in range(blocks)])
        conv_grad = []
        for a in range(blocks):
            at = a * rows + b0
            query_filt = short(qp, 0, PAD + at)
            qs[pl.ds(at, CHUNK), :] = query_filt
            conv_grad.append(
                query_filt * got_ref[a, pl.ds(4 * rows + b0, CHUNK), :].astype(f32)
            )
        put(2, conv_grad)
        return carry

    lax.fori_loop(0, chunks, enter, 0)

    def three(high_table, low_table, high, low):
        return (
            jnp.dot(high_table, high, preferred_element_type=f32)
            + jnp.dot(high_table, low, preferred_element_type=f32)
            + jnp.dot(low_table, high, preferred_element_type=f32)
        )

    def turn(f, carry):
        spec = three(fh_ref[f], fl_ref[f], xh[f], xl[f])
        (mr, hr, gr), (mi, hi, gi) = [
            [spec[p * rows : (p + 1) * rows, c * LANES : (c + 1) * LANES] for c in range(3)]
            for p in range(2)
        ]
        real = jnp.concatenate([mr * hr - mi * hi, gr * hr + gi * hi, gr * mr + gi * mi], axis=1)
        imag = jnp.concatenate([mr * hi + mi * hr, gi * hr - gr * hi, gi * mr - gr * mi], axis=1)
        high, low = split_pair(jnp.concatenate([real, imag], axis=0))
        zs[f] = three(ih_ref[f], il_ref[f], high, low)
        return carry

    lax.fori_loop(0, len(CLASSES), turn, 0)
    grad_scale = 1.0 / math.sqrt(total)

    def leave(step, carry):
        b0 = pl.multiple_of(step * CHUNK, CHUNK)

        def take(column):
            lanes = pl.ds(column * LANES, LANES)
            return inverse_classes(
                [
                    (zs[f, pl.ds(b0, CHUNK), lanes], zs[f, pl.ds(rows + b0, CHUNK), lanes])
                    for f in range(len(CLASSES))
                ]
            )

        for a, conv in enumerate(take(0)):
            at = a * rows + b0
            out_ref[a, pl.ds(b0, CHUNK), :] = (qs[pl.ds(at, CHUNK), :] * conv).astype(jnp.bfloat16)
            g0[pl.ds(at, CHUNK), :] = conv * got_ref[a, pl.ds(4 * rows + b0, CHUNK), :].astype(f32)
        for a, mixed_grad in enumerate(take(1)):
            at = a * rows + b0
            g1[pl.ds(at, CHUNK), :] = mixed_grad * vs[pl.ds(at, CHUNK), :]
            g2[pl.ds(at, CHUNK), :] = mixed_grad * ks[pl.ds(at, CHUNK), :]
        for a, value in enumerate(take(2)):
            high, low = split_pair(value * grad_scale)
            out_ref[a, pl.ds(4 * rows + b0, CHUNK), :] = high
            out_ref[a, pl.ds(5 * rows + b0, CHUNK), :] = low
        return carry

    lax.fori_loop(0, chunks, leave, 0)
    sums[...] = jnp.zeros_like(sums)

    def close(step, carry):
        b0 = pl.multiple_of(step * CHUNK, CHUNK)
        for i, (grad, source) in enumerate(((g0, qp), (g1, kp), (g2, vp))):
            found = [jnp.zeros((CHUNK, LANES), f32)] * 3
            for a in range(blocks):
                at = a * rows + b0
                now = grad[pl.ds(at, CHUNK), :]
                value = (
                    gain[i][0] * now
                    + gain[i][1] * grad[pl.ds(at + 1, CHUNK), :]
                    + gain[i][2] * grad[pl.ds(at + 2, CHUNK), :]
                )
                out_ref[a, pl.ds((1 + i) * rows + b0, CHUNK), :] = value.astype(jnp.bfloat16)
                for j in range(3):
                    found[j] = found[j] + now * source[pl.ds(PAD + at - j, CHUNK), :]
            for j in range(3):
                sums[3 * i + j] += found[j][:8] + found[j][8:]
        return carry

    lax.fori_loop(0, chunks, close, 0)
    place = lax.broadcasted_iota(jnp.int32, (CHUNK, LANES), 0)
    taps = jnp.zeros((CHUNK, LANES), f32)
    for n in range(9):
        line = jnp.sum(sums[n], axis=0, keepdims=True) * grad_scale
        taps = jnp.where(place == n, line, taps)
    high, low = split_pair(taps)
    for a in range(blocks):
        out_ref[a, pl.ds(6 * rows, CHUNK), :] = high
        out_ref[a, pl.ds(6 * rows + CHUNK, CHUNK), :] = low


def whole_vmem(count):
    return [pl.BlockSpec(memory_space=pltpu.VMEM)] * count


def pack_kernel(*refs):
    *sources, out_ref = refs
    rows = sources[0].shape[0]
    for a in range(out_ref.shape[0]):
        for field, ref in enumerate(sources):
            out_ref[a, pl.ds(field * rows, rows), :] = ref[:, a * LANES : (a + 1) * LANES]


def unpack_kernel(got_ref, output, query_grad, key_grad, value_grad, filter_grad, taps_grad):
    rows = output.shape[0]
    for a in range(got_ref.shape[0]):
        lanes = slice(a * LANES, (a + 1) * LANES)
        for field, ref in enumerate((output, query_grad, key_grad, value_grad)):
            ref[:, lanes] = got_ref[a, pl.ds(field * rows, rows), :]
        high, low = [got_ref[a, pl.ds(n * rows, rows), :].astype(jnp.float32) for n in (4, 5)]
        filter_grad[:, lanes] = high + low
        high, low = [
            got_ref[a, pl.ds(6 * rows + n * CHUNK, CHUNK), :].astype(jnp.float32) for n in (0, 1)
        ]
        taps_grad[:, lanes] = high + low


def local_fast(query_in, key_in, value_in, long_filter, short_taps, out_grad):
    rows, channels = query_in.shape
    blocks = lax.axis_size("ctx")
    total = blocks * rows
    f32, bf16 = jnp.float32, jnp.bfloat16
    shape = jax.ShapeDtypeStruct
    packed = pl.pallas_call(
        pack_kernel,
        out_shape=shape((blocks, 5 * rows, LANES), bf16),
        in_specs=whole_vmem(5),
        out_specs=whole_vmem(1)[0],
        name="pack",
    )(query_in, key_in, value_in, long_filter, out_grad)
    got = lax.all_to_all(packed, "ctx", 0, 0)
    gain = lax.dynamic_slice_in_dim(
        short_taps.reshape(9, channels), lax.axis_index("ctx") * LANES, LANES, 1
    ).astype(f32)
    tables = class_tables(rows)
    count = len(CLASSES)
    height = 6 * rows + 2 * CHUNK
    done = pl.pallas_call(
        layer_kernel,
        out_shape=shape((blocks, height, LANES), bf16),
        in_specs=whole_vmem(6),
        out_specs=whole_vmem(1)[0],
        scratch_shapes=[pltpu.VMEM((total + PAD, LANES), f32)] * 3
        + [pltpu.VMEM((total, LANES), f32)] * 3
        + [pltpu.VMEM((count, 2 * rows, 3 * LANES), bf16)] * 2
        + [pltpu.VMEM((count, 2 * rows, 3 * LANES), f32)]
        + [pltpu.VMEM((total + PAD, LANES), f32)] * 3
        + [pltpu.VMEM((9, 8, LANES), f32)],
        compiler_params=pltpu.CompilerParams(vmem_limit_bytes=40 * 1024 * 1024),
        name="layer",
    )(gain, got, *tables)
    back = lax.all_to_all(done, "ctx", 0, 0)
    result = pl.pallas_call(
        unpack_kernel,
        out_shape=[shape((rows, channels), bf16)] * 4
        + [shape((rows, channels), f32), shape((CHUNK, channels), f32)],
        in_specs=whole_vmem(1),
        out_specs=whole_vmem(6),
        name="unpack",
    )(back)
    return (*result[:5], result[5][:9].reshape(3, 3, channels))


def local(query_in, key_in, value_in, long_filter, short_taps, out_grad):
    rows, channels = query_in.shape
    blocks = lax.axis_size("ctx")
    taps = short_taps.shape[:2]
    if blocks == RADIX and channels == blocks * LANES and rows == LANES and taps == (3, 3):
        return local_fast(query_in, key_in, value_in, long_filter, short_taps, out_grad)
    return local_general(query_in, key_in, value_in, long_filter, short_taps, out_grad)


def solution(mesh):
    placed = (
        P("ctx", "tp"),
        P("ctx", "tp"),
        P("ctx", "tp"),
        P("ctx", "tp"),
        P(None, None, "tp"),
        P("ctx", "tp"),
    )
    return jax.shard_map(
        local,
        mesh=mesh,
        in_specs=placed,
        out_specs=(
            P("ctx", "tp"),
            P("ctx", "tp"),
            P("ctx", "tp"),
            P("ctx", "tp"),
            P("ctx", "tp"),
            P(None, None, "tp"),
        ),
        check_vma=False,
    )
```

profile of v0, /device:TPU:0, one launch (start us, length us, event | category | flops | bytes accessed | tf_op | source)
XLA Modules:
  0.0 69.5 jit_solution(11434463966246927462)
XLA Ops:
  0.6 2.6 %pack.1 = bf16[8,640,128]{2,1,0:T(8,128)(2,1)} custom-call(bf16[128,1024]{1,0:T(8,128)(2,1)} %refs_0_.1, bf16[128,1024]{1,0:T(8,128)(2,1)} %refs_1_.1, bf16[128,1024]{1,0:T(8,128)(2,1)} %refs_2_.1, bf16[128,1024]{1,0:T(8,128)(2,1)} %refs_3_.1, bf16[128,1024]{1,0:T(8,128)(2,1)} %refs_4_.1), custom_call_target="tpu_custom_call" | custom-call | tf_op jit(solution)/shard_map/pack/pallas_call | solution.py:480
  3.2 0.0 copy-start.4
  3.2 0.0 copy-start
  3.2 5.3 %all-to-all-start = ((bf16[8,640,128]{2,1,0:T(8,128)(2,1)}), bf16[8,640,128]{2,1,0:T(8,128)(2,1)S(1)}, u32[]{:S(2)}, u32[]{:S(2)}) async-start(bf16[8,640,128]{2,1,0:T(8,128)(2,1)} %pack.1), calls=%async_computation | async-start | bytes 2621440 | tf_op jit(solution)/shard_map/all_to_all | solution.py:487
  8.5 0.0 copy-done.4
  8.6 18.2 %all-to-all-done.got_ref = bf16[8,640,128]{2,1,0:T(8,128)(2,1)S(1)} async-done(((bf16[8,640,128]{2,1,0:T(8,128)(2,1)}), bf16[8,640,128]{2,1,0:T(8,128)(2,1)S(1)}, u32[]{:S(2)}, u32[]{:S(2)}) %all-to-all-start) | async-done | bytes 1310752 | tf_op jit(solution)/shard_map/all_to_all | solution.py:487
  26.7 0.0 copy-done
  26.7 0.0 copy-start.1
  26.7 1.3 %copy-done.1 = bf16[9,256,256]{2,1,0:T(8,128)(2,1)S(1)} copy-done((bf16[9,256,256]{2,1,0:T(8,128)(2,1)S(1)}, bf16[9,256,256]{2,1,0:T(8,128)(2,1)}, u32[]{:S(2)}) %copy-start.1) | copy-done | bytes 1179672
  28.0 0.0 copy-start.2
  28.0 1.3 %copy-done.2 = bf16[9,256,256]{2,1,0:T(8,128)(2,1)S(1)} copy-done((bf16[9,256,256]{2,1,0:T(8,128)(2,1)S(1)}, bf16[9,256,256]{2,1,0:T(8,128)(2,1)}, u32[]{:S(2)}) %copy-start.2) | copy-done | bytes 1179672
  29.3 0.0 copy-start.3
  29.3 1.3 %copy-done.3 = bf16[9,256,256]{2,1,0:T(8,128)(2,1)S(1)} copy-done((bf16[9,256,256]{2,1,0:T(8,128)(2,1)S(1)}, bf16[9,256,256]{2,1,0:T(8,128)(2,1)}, u32[]{:S(2)}) %copy-start.3) | copy-done | bytes 1179672
  30.6 9.9 %layer.1 = bf16[8,800,128]{2,1,0:T(8,128)(2,1)S(1)} custom-call(f32[9,128]{1,0:T(8,128)S(1)} %dynamic-slice_convert_fusion.taps_ref, bf16[8,640,128]{2,1,0:T(8,128)(2,1)S(1)} %all-to-all-done.got_ref, bf16[9,256,256]{2,1,0:T(8,128)(2,1)S(1)} %copy-done.3, bf16[9,256,256]{2,1,0:T(8,128)(2,1)S(1)} %copy-done.2, bf16[9,256,256]{2,1,0:T(8,128)(2,1)S(1)} %copy-done.1, ...), custom_call_target="tpu_custom_call" | custom-call | tf_op jit(solution)/shard_map/layer/pallas_call | solution.py:494
  40.4 24.8 %all_to_all.10.got_ref = bf16[8,800,128]{2,1,0:T(8,128)(2,1)} all-to-all(bf16[8,800,128]{2,1,0:T(8,128)(2,1)S(1)} %layer.1), channel_id=1, replica_groups=mesh['ctx'=8,'tp'=4] {'ctx'}, dimensions={0} | all-to-all | bytes 3276800 | tf_op jit(solution)/shard_map/all_to_all | solution.py:508
  65.3 2.7 %unpack.1 = (bf16[128,1024]{1,0:T(8,128)(2,1)}, bf16[128,1024]{1,0:T(8,128)(2,1)}, bf16[128,1024]{1,0:T(8,128)(2,1)}, bf16[128,1024]{1,0:T(8,128)(2,1)}, f32[128,1024]{1,0:T(8,128)}, /*index=5*/f32[16,1024]{1,0:T(8,128)}) custom-call(bf16[8,800,128]{2,1,0:T(8,128)(2,1)} %all_to_all.10.got_ref), custom_call_target="tpu_custom_call" | custom-call | tf_op jit(solution)/shard_map/unpack/pallas_call | solution.py:509
  68.0 1.5 %reshape.19 = f32[3,3,1024]{2,1,0:T(4,128)} reshape(f32[9,1024]{1,0:T(8,128)} %bitcast.1) | data formatting | bytes 73728 | tf_op jit(solution)/shard_map/reshape | solution.py:517
  (2 shorter events, 0.0 us)
Async XLA Ops:
  3.2 5.3 %copy-start.4 = (bf16[3,3,1024]{2,1,0:T(4,128)(2,1)S(1)}, bf16[3,3,1024]{2,1,0:T(4,128)(2,1)}, u32[]{:S(2)}) copy-start(bf16[3,3,1024]{2,1,0:T(4,128)(2,1)} %param.14) | copy-start | bytes 55300
  3.2 23.5 %copy-start = (bf16[9,256,256]{2,1,0:T(8,128)(2,1)S(1)}, bf16[9,256,256]{2,1,0:T(8,128)(2,1)}, u32[]{:S(2)}) copy-start(bf16[9,256,256]{2,1,0:T(8,128)(2,1)} %constant.23.clone.il_ref) | copy-start | bytes 3538948
  3.2 23.5 %all-to-all-start = ((bf16[8,640,128]{2,1,0:T(8,128)(2,1)}), bf16[8,640,128]{2,1,0:T(8,128)(2,1)S(1)}, u32[]{:S(2)}, u32[]{:S(2)}) async-start(bf16[8,640,128]{2,1,0:T(8,128)(2,1)} %pack.1), calls=%async_computation | async-start | bytes 2621440 | tf_op jit(solution)/shard_map/all_to_all | solution.py:487
  26.7 1.3 %copy-start.1 = (bf16[9,256,256]{2,1,0:T(8,128)(2,1)S(1)}, bf16[9,256,256]{2,1,0:T(8,128)(2,1)}, u32[]{:S(2)}) copy-start(bf16[9,256,256]{2,1,0:T(8,128)(2,1)} %constant.22.clone.ih_ref) | copy-start | bytes 3538948
  28.0 1.3 %copy-start.2 = (bf16[9,256,256]{2,1,0:T(8,128)(2,1)S(1)}, bf16[9,256,256]{2,1,0:T(8,128)(2,1)}, u32[]{:S(2)}) copy-start(bf16[9,256,256]{2,1,0:T(8,128)(2,1)} %constant.21.clone.fl_ref) | copy-start | bytes 3538948
  29.3 1.3 %copy-start.3 = (bf16[9,256,256]{2,1,0:T(8,128)(2,1)S(1)}, bf16[9,256,256]{2,1,0:T(8,128)(2,1)}, u32[]{:S(2)}) copy-start(bf16[9,256,256]{2,1,0:T(8,128)(2,1)} %constant.20.clone.fh_ref) | copy-start | bytes 3538948
where the time goes:
time: 69.9 us; the launch traced here: 69.5 us
  blocking collectives  24.8 us (35%)
  waiting for transfers between devices  18.2 us (26%)
  Pallas kernels  15.2 us (22%)
  local copies, waits for them, and re-layouts  5.32 us (8%)
  starting transfers between devices  5.3 us (8%)
    all_to_all x1, blocking collectives, local_fast(): back = lax.all_to_all(done, 'ctx', 0, 0)  24.8 us
    all_to_all x1, waiting for transfers between devices, local_fast(): got = lax.all_to_all(packed, 'ctx', 0, 0)  18.2 us
    pallas_call x1, Pallas kernels, local_fast(): pl.pallas_call(layer_kernel, out_shape=shape((blocks, height, LANES), bf1...  9.89 us
    all_to_all x1, starting transfers between devices, local_fast(): got = lax.all_to_all(packed, 'ctx', 0, 0)  5.3 us
    unnamed x10, local copies, waits for them, and re-layouts  3.82 us
    pallas_call x1, Pallas kernels, local_fast(): pl.pallas_call(unpack_kernel, out_shape=[shape((rows, channels), bf16)] *...  2.73 us
    pallas_call x1, Pallas kernels, local_fast(): pl.pallas_call(pack_kernel, out_shape=shape((blocks, 5 * rows, LANES), bf...  2.58 us
    reshape x1, local copies, waits for them, and re-layouts, local_fast(): return (*result[:5], result[5][:9].reshape(3, 3, channels))  1.48 us
  transfers between devices with their start and end apart: 1, of which 1 were waited for; matrix products, arithmetic and copies ran while one was open for 0% of the time, Pallas kernels for 0%

commit v1 on v0

--- a/solution.py
+++ b/solution.py
@@ -200,11 +200,15 @@
 
 
 RADIX = 8
-FIELD_NAMES = ("query", "key", "value", "filter", "out_grad")
+FIELDS = 5
 CLASSES = (0, 8, 4, 2, 6, 1, 5, 9, 13)
 LANES = 128
 PAD = 8
 CHUNK = 16
+CURVE = 15.0
+REACH = 120.0
+SLOPE = 2.0 * REACH / math.log2(1.0 + CURVE)
+TINY = 1e-30
 
 
 def split_pair(values):
@@ -291,20 +295,40 @@
     ]
 
 
+def log_code(values, inverse_scale):
+    share = 1.0 + CURVE * (jnp.abs(values) * inverse_scale)
+    code = jnp.exp2(jnp.log2(share) * SLOPE - REACH)
+    return jnp.where(values < 0.0, -code, code).astype(jnp.bfloat16)
+
+
+def log_decode(code, scale):
+    code = code.astype(jnp.float32)
+    share = jnp.exp2((jnp.log2(jnp.abs(code)) + REACH) * (1.0 / SLOPE)) - 1.0
+    values = share * (scale * (1.0 / CURVE))
+    return jnp.where(code < 0.0, -values, values)
+
+
 def layer_kernel(
-    taps_ref, got_ref, fh_ref, fl_ref, ih_ref, il_ref, out_ref,
-    qp, kp, vp, qs, ks, vs, xh, xl, zs, g0, g1, g2, sums,
+    taps_ref, got_ref, fh_any, fl_any, ih_any, il_any, out_ref,
+    qp, kp, vp, qs, ks, vs, xh, xl, zs, conv, mgrad, fgrad, peak, sums, head,
+    fh_ref, fl_ref, ih_ref, il_ref, table_sem,
 ):
     blocks, height, _ = got_ref.shape
-    rows = height // len(FIELD_NAMES)
+    rows = height // FIELDS
     total = blocks * rows
     chunks = rows // CHUNK
     f32 = jnp.float32
+    copies = [
+        pltpu.make_async_copy(src, dst, table_sem.at[n])
+        for n, (src, dst) in enumerate(
+            ((fh_any, fh_ref), (fl_any, fl_ref), (ih_any, ih_ref), (il_any, il_ref))
+        )
+    ]
+    for copy in copies:
+        copy.start()
     zero = jnp.zeros((PAD, LANES), f32)
     for ref in (qp, kp, vp):
         ref[pl.ds(0, PAD), :] = zero
-    for ref in (g0, g1, g2):
-        ref[pl.ds(total, PAD), :] = zero
     gain = [[taps_ref[3 * i + j : 3 * i + j + 1, :] for j in range(3)] for i in range(3)]
 
     def widen(step, carry):
@@ -354,7 +378,6 @@
         for a in range(blocks):
             at = a * rows + b0
             query_filt = short(qp, 0, PAD + at)
-            qs[pl.ds(at, CHUNK), :] = query_filt
             conv_grad.append(
                 query_filt * got_ref[a, pl.ds(4 * rows + b0, CHUNK), :].astype(f32)
             )
@@ -362,6 +385,8 @@
         return carry
 
     lax.fori_loop(0, chunks, enter, 0)
+    for copy in copies:
+        copy.wait()
 
     def three(high_table, low_table, high, low):
         return (
@@ -383,66 +408,77 @@
         return carry
 
     lax.fori_loop(0, len(CLASSES), turn, 0)
-    grad_scale = 1.0 / math.sqrt(total)
+    peak[...] = jnp.zeros_like(peak)
+    sums[...] = jnp.zeros_like(sums)
 
     def leave(step, carry):
         b0 = pl.multiple_of(step * CHUNK, CHUNK)
 
-        def take(column):
+        def take(column, ref):
             lanes = pl.ds(column * LANES, LANES)
-            return inverse_classes(
+            found = inverse_classes(
                 [
                     (zs[f, pl.ds(b0, CHUNK), lanes], zs[f, pl.ds(rows + b0, CHUNK), lanes])
                     for f in range(len(CLASSES))
                 ]
             )
-
-        for a, conv in enumerate(take(0)):
-            at = a * rows + b0
-            out_ref[a, pl.ds(b0, CHUNK), :] = (qs[pl.ds(at, CHUNK), :] * conv).astype(jnp.bfloat16)
-            g0[pl.ds(at, CHUNK), :] = conv * got_ref[a, pl.ds(4 * rows + b0, CHUNK), :].astype(f32)
-        for a, mixed_grad in enumerate(take(1)):
-            at = a * rows + b0
-            g1[pl.ds(at, CHUNK), :] = mixed_grad * vs[pl.ds(at, CHUNK), :]
-            g2[pl.ds(at, CHUNK), :] = mixed_grad * ks[pl.ds(at, CHUNK), :]
-        for a, value in enumerate(take(2)):
-            high, low = split_pair(value * grad_scale)
-            out_ref[a, pl.ds(4 * rows + b0, CHUNK), :] = high
-            out_ref[a, pl.ds(5 * rows + b0, CHUNK), :] = low
-        return carry
-
-    lax.fori_loop(0, chunks, leave, 0)
-    sums[...] = jnp.zeros_like(sums)
-
-    def close(step, carry):
-        b0 = pl.multiple_of(step * CHUNK, CHUNK)
-        for i, (grad, source) in enumerate(((g0, qp), (g1, kp), (g2, vp))):
+            for a, value in enumerate(found):
+                ref[pl.ds(a * rows + b0, CHUNK), :] = value
+                size = jnp.abs(value)
+                peak[column, a] = jnp.maximum(peak[column, a], jnp.maximum(size[:8], size[8:]))
+            return found
+
+        def add(i, source, grads):
             found = [jnp.zeros((CHUNK, LANES), f32)] * 3
-            for a in range(blocks):
-                at = a * rows + b0
-                now = grad[pl.ds(at, CHUNK), :]
-                value = (
-                    gain[i][0] * now
-                    + gain[i][1] * grad[pl.ds(at + 1, CHUNK), :]
-                    + gain[i][2] * grad[pl.ds(at + 2, CHUNK), :]
-                )
-                out_ref[a, pl.ds((1 + i) * rows + b0, CHUNK), :] = value.astype(jnp.bfloat16)
+            for a, now in enumerate(grads):
                 for j in range(3):
-                    found[j] = found[j] + now * source[pl.ds(PAD + at - j, CHUNK), :]
+                    found[j] = found[j] + now * source[pl.ds(PAD + a * rows + b0 - j, CHUNK), :]
             for j in range(3):
                 sums[3 * i + j] += found[j][:8] + found[j][8:]
+
+        found = take(0, conv)
+        add(0, qp, [
+            value * got_ref[a, pl.ds(4 * rows + b0, CHUNK), :].astype(f32)
+            for a, value in enumerate(found)
+        ])
+        found = take(1, mgrad)
+        add(1, kp, [
+            value * vs[pl.ds(a * rows + b0, CHUNK), :] for a, value in enumerate(found)
+        ])
+        add(2, vp, [
+            value * ks[pl.ds(a * rows + b0, CHUNK), :] for a, value in enumerate(found)
+        ])
+        take(2, fgrad)
         return carry
 
-    lax.fori_loop(0, chunks, close, 0)
-    place = lax.broadcasted_iota(jnp.int32, (CHUNK, LANES), 0)
-    taps = jnp.zeros((CHUNK, LANES), f32)
+    lax.fori_loop(0, chunks, leave, 0)
+    grad_scale = 1.0 / math.sqrt(total)
+    head[pl.ds(0, 48), :] = jnp.zeros((48, LANES), f32)
     for n in range(9):
-        line = jnp.sum(sums[n], axis=0, keepdims=True) * grad_scale
-        taps = jnp.where(place == n, line, taps)
-    high, low = split_pair(taps)
+        at = 32 + n if n < 8 else 22
+        head[pl.ds(at, 1), :] = jnp.sum(sums[n], axis=0, keepdims=True) * grad_scale
+    head[pl.ds(40, 8), :] = split_pair(head[pl.ds(32, 8), :])[1].astype(f32)
     for a in range(blocks):
-        out_ref[a, pl.ds(6 * rows, CHUNK), :] = high
-        out_ref[a, pl.ds(6 * rows + CHUNK, CHUNK), :] = low
+        first = a * rows
+        for i, ref in enumerate((qp, kp, vp)):
+            head[pl.ds(2 * i, 2), :] = ref[pl.ds(PAD + first - 2, 2), :]
+        for column, ref in enumerate((conv, mgrad, fgrad)):
+            top = jnp.max(peak[column, a], axis=0, keepdims=True)
+            scale = jnp.maximum(top * (1.0 + 2.0**-7), TINY).astype(jnp.bfloat16).astype(f32)
+            head[pl.ds(6 + column, 1), :] = scale
+            out_ref[a, pl.ds(column * rows, rows), :] = log_code(
+                ref[pl.ds(first, rows), :], 1.0 / scale
+            )
+        if a + 1 < blocks:
+            after = first + rows
+            grad_in = got_ref[a + 1, pl.ds(4 * rows, CHUNK), :].astype(f32)[:2]
+            head[pl.ds(16, 2), :] = conv[pl.ds(after, 2), :] * grad_in
+            head[pl.ds(18, 2), :] = mgrad[pl.ds(after, 2), :] * vs[pl.ds(after, 2), :]
+            head[pl.ds(20, 2), :] = mgrad[pl.ds(after, 2), :] * ks[pl.ds(after, 2), :]
+        else:
+            head[pl.ds(16, 6), :] = jnp.zeros((6, LANES), f32)
+        head[pl.ds(24, 8), :] = split_pair(head[pl.ds(16, 8), :])[1].astype(f32)
+        out_ref[a, pl.ds(3 * rows, 48), :] = head[...].astype(jnp.bfloat16)
 
 
 def whole_vmem(count):
@@ -457,18 +493,50 @@
             out_ref[a, pl.ds(field * rows, rows), :] = ref[:, a * LANES : (a + 1) * LANES]
 
 
-def unpack_kernel(got_ref, output, query_grad, key_grad, value_grad, filter_grad, taps_grad):
+def finish_kernel(
+    got_ref, query_ref, key_ref, value_ref, cot_ref, taps_ref,
+    output, query_grad, key_grad, value_grad, filter_grad, taps_grad,
+    wide, grads,
+):
     rows = output.shape[0]
+    f32, bf16 = jnp.float32, jnp.bfloat16
     for a in range(got_ref.shape[0]):
         lanes = slice(a * LANES, (a + 1) * LANES)
-        for field, ref in enumerate((output, query_grad, key_grad, value_grad)):
-            ref[:, lanes] = got_ref[a, pl.ds(field * rows, rows), :]
-        high, low = [got_ref[a, pl.ds(n * rows, rows), :].astype(jnp.float32) for n in (4, 5)]
-        filter_grad[:, lanes] = high + low
-        high, low = [
-            got_ref[a, pl.ds(6 * rows + n * CHUNK, CHUNK), :].astype(jnp.float32) for n in (0, 1)
+        head = got_ref[a, pl.ds(3 * rows, 48), :].astype(f32)
+        conv, mixed_grad, filt = [
+            log_decode(got_ref[a, pl.ds(n * rows, rows), :], head[6 + n : 7 + n]) for n in range(3)
         ]
-        taps_grad[:, lanes] = high + low
+        filter_grad[:, lanes] = filt * (1.0 / math.sqrt(got_ref.shape[0] * rows))
+        taps = head[32:40] + head[40:48]
+        for n in range(8):
+            taps_grad[n // 3, n % 3 : n % 3 + 1, lanes] = taps[n : n + 1]
+        pairs = head[16:24] + head[24:32]
+        taps_grad[2, 2:3, lanes] = pairs[6:7]
+        filtered = []
+        gain = []
+        for i, ref in enumerate((query_ref, key_ref, value_ref)):
+            gain.append([taps_ref[i, j : j + 1, lanes].astype(f32) for j in range(3)])
+            wide[i, pl.ds(PAD - 2, 2), :] = head[2 * i : 2 * i + 2]
+            wide[i, pl.ds(PAD, rows), :] = ref[:, lanes].astype(f32)
+            filtered.append(
+                gain[i][0] * wide[i, pl.ds(PAD, rows), :]
+                + gain[i][1] * wide[i, pl.ds(PAD - 1, rows), :]
+                + gain[i][2] * wide[i, pl.ds(PAD - 2, rows), :]
+            )
+        output[:, lanes] = (filtered[0] * conv).astype(bf16)
+        inner = (
+            conv * cot_ref[:, lanes].astype(f32),
+            mixed_grad * filtered[2],
+            mixed_grad * filtered[1],
+        )
+        for i, ref in enumerate((query_grad, key_grad, value_grad)):
+            grads[i, pl.ds(0, rows), :] = inner[i]
+            grads[i, pl.ds(rows, 2), :] = pairs[2 * i : 2 * i + 2]
+            ref[:, lanes] = (
+                gain[i][0] * inner[i]
+                + gain[i][1] * grads[i, pl.ds(1, rows), :]
+                + gain[i][2] * grads[i, pl.ds(2, rows), :]
+            ).astype(bf16)
 
 
 def local_fast(query_in, key_in, value_in, long_filter, short_taps, out_grad):
@@ -479,7 +547,7 @@
     shape = jax.ShapeDtypeStruct
     packed = pl.pallas_call(
         pack_kernel,
-        out_shape=shape((blocks, 5 * rows, LANES), bf16),
+        out_shape=shape((blocks, FIELDS * rows, LANES), bf16),
         in_specs=whole_vmem(5),
         out_specs=whole_vmem(1)[0],
         name="pack",
@@ -490,31 +558,41 @@
     ).astype(f32)
     tables = class_tables(rows)
     count = len(CLASSES)
-    height = 6 * rows + 2 * CHUNK
     done = pl.pallas_call(
         layer_kernel,
-        out_shape=shape((blocks, height, LANES), bf16),
-        in_specs=whole_vmem(6),
+        out_shape=shape((blocks, 3 * rows + 48, LANES), bf16),
+        in_specs=whole_vmem(2) + [pl.BlockSpec(memory_space=pl.ANY)] * 4,
         out_specs=whole_vmem(1)[0],
         scratch_shapes=[pltpu.VMEM((total + PAD, LANES), f32)] * 3
         + [pltpu.VMEM((total, LANES), f32)] * 3
         + [pltpu.VMEM((count, 2 * rows, 3 * LANES), bf16)] * 2
         + [pltpu.VMEM((count, 2 * rows, 3 * LANES), f32)]
-        + [pltpu.VMEM((total + PAD, LANES), f32)] * 3
-        + [pltpu.VMEM((9, 8, LANES), f32)],
-        compiler_params=pltpu.CompilerParams(vmem_limit_bytes=40 * 1024 * 1024),
+        + [pltpu.VMEM((total, LANES), f32)] * 3
+        + [
+            pltpu.VMEM((3, blocks, 8, LANES), f32),
+            pltpu.VMEM((9, 8, LANES), f32),
+            pltpu.VMEM((48, LANES), f32),
+        ]
+        + [pltpu.VMEM((count, 2 * rows, 2 * rows), bf16)] * 4
+        + [pltpu.SemaphoreType.DMA((4,))],
+        compiler_params=pltpu.CompilerParams(vmem_limit_bytes=48 * 1024 * 1024),
         name="layer",
     )(gain, got, *tables)
     back = lax.all_to_all(done, "ctx", 0, 0)
-    result = pl.pallas_call(
-        unpack_kernel,
-        out_shape=[shape((rows, channels), bf16)] * 4
-        + [shape((rows, channels), f32), shape((CHUNK, channels), f32)],
-        in_specs=whole_vmem(1),
-        out_specs=whole_vmem(6),
-        name="unpack",
-    )(back)
-    return (*result[:5], result[5][:9].reshape(3, 3, channels))
+    return tuple(
+        pl.pallas_call(
+            finish_kernel,
+            out_shape=[shape((rows, channels), bf16)] * 4
+            + [shape((rows, channels), f32), shape((3, 3, channels), f32)],
+            in_specs=whole_vmem(6),
+            out_specs=whole_vmem(6),
+            scratch_shapes=[
+                pltpu.VMEM((3, PAD + rows, LANES), f32),
+                pltpu.VMEM((3, rows + PAD, LANES), f32),
+            ],
+            name="finish",
+        )(back, query_in, key_in, value_in, out_grad, short_taps)
+    )
 
 
 def local(query_in, key_in, value_in, long_filter, short_taps, out_grad):

time: 69.9 us -> 61.8 us (0.88)
  blocking collectives: 24.8 us -> 16.7 us
  Pallas kernels: 15.2 us -> 19.1 us
  local copies, waits for them, and re-layouts: 5.32 us -> 2.66 us
  waiting for transfers between devices: 18.2 us -> 16.3 us
    all_to_all x1, blocking collectives: 24.8 us -> 16.7 us  [local_fast(): back = lax.all_to_all(done, 'ctx', 0, 0)]
    pallas_call x3, Pallas kernels: 15.2 us -> 19.1 us  [the longest x1 12.4 us: local_fast(): pl.pallas_call(layer_kernel, out_shape=shape((blocks, 3 * rows + 48, LANE...]
    unnamed x10 -> x8, local copies, waits for them, and re-layouts: 3.82 us -> 1.28 us
    all_to_all x1, waiting for transfers between devices: 18.2 us -> 16.3 us  [local_fast(): got = lax.all_to_all(packed, 'ctx', 0, 0)]
    reshape x1 -> x0, local copies, waits for them, and re-layouts: 1.48 us -> none  [local_fast(): return (*result[:5], result[5][:9].reshape(3, 3, channels))]
    reshape x1, local copies, waits for them, and re-layouts: 0.03 us -> 1.38 us  [local_fast(): short_taps.reshape(9, channels)]
  transfers between devices with their start and end apart: 1 -> 1, of which waited for: 1 -> 1; matrix products, arithmetic and copies ran while one was open for 0% -> 3% of each run, Pallas kernels for 0% -> 0%
where the time goes in v1:
time: 61.8 us; the launch traced here: 61.4 us
  Pallas kernels  19.1 us (31%)
  blocking collectives  16.7 us (27%)
  waiting for transfers between devices  16.3 us (26%)
  starting transfers between devices  5.3 us (9%)
  local copies, waits for them, and re-layouts  2.66 us (4%)
  other arithmetic  0.69 us (1%)
  between operations  0.66 us (1%)
    all_to_all x1, blocking collectives, local_fast(): back = lax.all_to_all(done, 'ctx', 0, 0)  16.7 us
    all_to_all x1, waiting for transfers between devices, local_fast(): got = lax.all_to_all(packed, 'ctx', 0, 0)  16.3 us
    pallas_call x1, Pallas kernels, local_fast(): pl.pallas_call(layer_kernel, out_shape=shape((blocks, 3 * rows + 48, LANE...  12.4 us
    all_to_all x1, starting transfers between devices, local_fast(): got = lax.all_to_all(packed, 'ctx', 0, 0)  5.3 us
    pallas_call x1, Pallas kernels, local_fast(): pl.pallas_call(finish_kernel, out_shape=[shape((rows, channels), bf16)] *...  4.03 us
    pallas_call x1, Pallas kernels, local_fast(): pl.pallas_call(pack_kernel, out_shape=shape((blocks, FIELDS * rows, LANES...  2.67 us
    reshape x1, local copies, waits for them, and re-layouts, local_fast(): short_taps.reshape(9, channels)  1.38 us
    unnamed x8, local copies, waits for them, and re-layouts  1.28 us
  transfers between devices with their start and end apart: 1, of which 1 were waited for; matrix products, arithmetic and copies ran while one was open for 3% of the time, Pallas kernels for 0%

profile of v1, /device:TPU:0, one launch (start us, length us, event | category | flops | bytes accessed | tf_op | source)
XLA Modules:
  0.0 61.4 jit_solution(16161231264417719624)
XLA Ops:
  0.6 0.0 copy-start.2
  0.6 2.7 %pack.1 = bf16[8,640,128]{2,1,0:T(8,128)(2,1)} custom-call(bf16[128,1024]{1,0:T(8,128)(2,1)} %query_ref.1, bf16[128,1024]{1,0:T(8,128)(2,1)} %key_ref.1, bf16[128,1024]{1,0:T(8,128)(2,1)} %value_ref.1, bf16[128,1024]{1,0:T(8,128)(2,1)} %refs_3_.1, bf16[128,1024]{1,0:T(8,128)(2,1)} %cot_ref.1), custom_call_target="tpu_custom_call" | custom-call | tf_op jit(solution)/shard_map/pack/pallas_call | solution.py:548
  3.3 0.0 copy-start
  3.3 0.0 copy-start.1
  3.3 5.3 %all-to-all-start = ((bf16[8,640,128]{2,1,0:T(8,128)(2,1)}), bf16[8,640,128]{2,1,0:T(8,128)(2,1)}, u32[]{:S(2)}, u32[]{:S(2)}) async-start(bf16[8,640,128]{2,1,0:T(8,128)(2,1)} %pack.1), calls=%async_computation | async-start | bytes 2621440 | tf_op jit(solution)/shard_map/all_to_all | solution.py:555
  8.6 1.4 %reshape.15 = bf16[9,1024]{1,0:T(8,128)(2,1)} reshape(bf16[3,3,1024]{2,1,0:T(4,128)(2,1)} %taps_ref.1) | data formatting | bytes 36864 | tf_op jit(solution)/shard_map/reshape | solution.py:557
  10.0 0.7 %dynamic-slice_convert_fusion.taps_ref = f32[9,128]{1,0:T(8,128)S(1)} fusion(bf16[9,1024]{1,0:T(8,128)(2,1)} %reshape.15, s32[]{:T(128)S(6)} %select_n.3), kind=kLoop, calls=%fused_computation | loop fusion | flops 1152 | bytes 6916 | tf_op jit(solution)/shard_map/convert_element_type | solution.py:558
  10.7 16.3 %all-to-all-done.got_ref = bf16[8,640,128]{2,1,0:T(8,128)(2,1)} async-done(((bf16[8,640,128]{2,1,0:T(8,128)(2,1)}), bf16[8,640,128]{2,1,0:T(8,128)(2,1)}, u32[]{:S(2)}, u32[]{:S(2)}) %all-to-all-start) | async-done | bytes 1310752 | tf_op jit(solution)/shard_map/all_to_all | solution.py:555
  26.9 0.0 copy-done.2
  26.9 0.0 copy-done
  26.9 0.0 copy-done.1
  27.0 0.0 copy-start.3
  27.0 1.3 %copy-done.3 = bf16[9,256,256]{2,1,0:T(8,128)(2,1)S(1)} copy-done((bf16[9,256,256]{2,1,0:T(8,128)(2,1)S(1)}, bf16[9,256,256]{2,1,0:T(8,128)(2,1)}, u32[]{:S(2)}) %copy-start.3) | copy-done | bytes 1179672
  28.2 12.4 %layer.1 = bf16[8,432,128]{2,1,0:T(8,128)(2,1)S(1)} custom-call(f32[9,128]{1,0:T(8,128)S(1)} %dynamic-slice_convert_fusion.taps_ref, bf16[8,640,128]{2,1,0:T(8,128)(2,1)} %all-to-all-done.got_ref, bf16[9,256,256]{2,1,0:T(8,128)(2,1)S(1)} %copy-done.3, bf16[9,256,256]{2,1,0:T(8,128)(2,1)S(1)} %copy-done.2, bf16[9,256,256]{2,1,0:T(8,128)(2,1)S(1)} %copy-done.1, ...), custom_call_target="tpu_custom_call" | custom-call | tf_op jit(solution)/shard_map/layer/pallas_call | solution.py:561
  40.7 16.7 %all_to_all.10.got_ref = bf16[8,432,128]{2,1,0:T(8,128)(2,1)} all-to-all(bf16[8,432,128]{2,1,0:T(8,128)(2,1)S(1)} %layer.1), channel_id=1, replica_groups=mesh['ctx'=8,'tp'=4] {'ctx'}, dimensions={0} | all-to-all | bytes 1769472 | tf_op jit(solution)/shard_map/all_to_all | solution.py:581
  57.4 4.0 %finish.1 = (bf16[128,1024]{1,0:T(8,128)(2,1)}, bf16[128,1024]{1,0:T(8,128)(2,1)}, bf16[128,1024]{1,0:T(8,128)(2,1)}, bf16[128,1024]{1,0:T(8,128)(2,1)}, f32[128,1024]{1,0:T(8,128)}, /*index=5*/f32[3,3,1024]{2,1,0:T(4,128)}) custom-call(bf16[8,432,128]{2,1,0:T(8,128)(2,1)} %all_to_all.10.got_ref, bf16[128,1024]{1,0:T(8,128)(2,1)} %query_ref.1, ...), custom_call_target="tpu_custom_call" | custom-call | tf_op jit(solution)/shard_map/finish/pallas_call | solution.py:583
Async XLA Ops:
  0.6 26.3 %copy-start.2 = (bf16[9,256,256]{2,1,0:T(8,128)(2,1)S(1)}, bf16[9,256,256]{2,1,0:T(8,128)(2,1)}, u32[]{:S(2)}) copy-start(bf16[9,256,256]{2,1,0:T(8,128)(2,1)} %constant.21.clone.fl_any) | copy-start | bytes 3538948
  3.3 23.6 %copy-start = (bf16[9,256,256]{2,1,0:T(8,128)(2,1)S(1)}, bf16[9,256,256]{2,1,0:T(8,128)(2,1)}, u32[]{:S(2)}) copy-start(bf16[9,256,256]{2,1,0:T(8,128)(2,1)} %constant.23.clone.il_any) | copy-start | bytes 3538948
  3.3 23.6 %copy-start.1 = (bf16[9,256,256]{2,1,0:T(8,128)(2,1)S(1)}, bf16[9,256,256]{2,1,0:T(8,128)(2,1)}, u32[]{:S(2)}) copy-start(bf16[9,256,256]{2,1,0:T(8,128)(2,1)} %constant.22.clone.ih_any) | copy-start | bytes 3538948
  3.3 23.6 %all-to-all-start = ((bf16[8,640,128]{2,1,0:T(8,128)(2,1)}), bf16[8,640,128]{2,1,0:T(8,128)(2,1)}, u32[]{:S(2)}, u32[]{:S(2)}) async-start(bf16[8,640,128]{2,1,0:T(8,128)(2,1)} %pack.1), calls=%async_computation | async-start | bytes 2621440 | tf_op jit(solution)/shard_map/all_to_all | solution.py:555
  27.0 1.3 %copy-start.3 = (bf16[9,256,256]{2,1,0:T(8,128)(2,1)S(1)}, bf16[9,256,256]{2,1,0:T(8,128)(2,1)}, u32[]{:S(2)}) copy-start(bf16[9,256,256]{2,1,0:T(8,128)(2,1)} %constant.20.clone.fh_any) | copy-start | bytes 3538948

commit v2 on v1

--- a/solution.py
+++ b/solution.py
@@ -201,10 +201,11 @@
 
 RADIX = 8
 FIELDS = 5
-CLASSES = (0, 8, 4, 2, 6, 1, 5, 9, 13)
+CLASSES = (4, 2, 6, 1, 5, 9, 13)
 LANES = 128
 PAD = 8
 CHUNK = 16
+PLACES = (0, 6, 2, 5, 3, 7, 4, 1)
 CURVE = 15.0
 REACH = 120.0
 SLOPE = 2.0 * REACH / math.log2(1.0 + CURVE)
@@ -221,20 +222,31 @@
 def class_tables(rows):
     length = 2 * RADIX * rows
     back = np.arange(rows)
-    forward, inverse = [], []
-    for residue in CLASSES:
-        product = np.outer(2 * RADIX * back + residue, back) % length
-        angle = -2.0 * np.pi * product / length
-        cosine, sine = np.cos(angle), np.sin(angle)
-        forward.append(np.block([[cosine, -sine], [sine, cosine]]))
-        weight = (1.0 if residue in (0, RADIX) else 2.0) / length
-        inverse.append(weight * np.block([[cosine.T, sine.T], [-sine.T, cosine.T]]))
+
+    def waves(residue, count):
+        angle = 2.0 * np.pi * (np.outer(2 * RADIX * np.arange(count) + residue, back) % length) / length
+        return np.cos(angle), np.sin(angle)
+
+    half = rows // 2
+    cos0, sin0 = waves(0, half)
+    cos8, sin8 = waves(RADIX, half)
+    none = np.zeros((half, rows))
+    middle = (1.0 - 2.0 * (back % 2))[None, :]
+    imag0 = np.concatenate([middle, -sin0[1:]])
+    first = np.block([[cos0, none], [none, cos8], [imag0, none], [none, -sin8]])
+    weight = np.full((2 * rows, 1), 2.0)
+    weight[0] = weight[rows] = 1.0
+    cosine, sine = waves(0, rows)
+    other = np.block([[cosine, sine], [-sine, cosine]])
     tables = []
-    for table in (np.stack(forward), np.stack(inverse)):
+    for table in (np.stack([first, other]), np.stack([(weight * first).T, 2.0 * other.T]) / length):
         high = table.astype(ml_dtypes.bfloat16)
         low = (table - high.astype(np.float64)).astype(ml_dtypes.bfloat16)
-        tables += [high, low]
-    return tables
+        tables.append(np.stack([high, low]))
+    turns = np.zeros((rows, LANES), np.float32)
+    for n, residue in enumerate(CLASSES):
+        turns[:, 2 * n], turns[:, 2 * n + 1] = [wave[0] for wave in waves(residue, 1)]
+    return (*tables, turns)
 
 
 ROOT = math.sqrt(0.5)
@@ -248,8 +260,7 @@
     even, odd = u[0] + u[2], u[1] + u[3]
     dif, tot = ROOT * (d[1] - d[3]), ROOT * (d[1] + d[3])
     found = [
-        (even + odd, None),
-        (even - odd, None),
+        (even + odd, even - odd),
         (u[0] - u[2], u[3] - u[1]),
         (d[0] + dif, -d[2] - tot),
         (d[0] - dif, d[2] - tot),
@@ -270,12 +281,12 @@
 
 
 def inverse_classes(z):
-    (z0, _), (z8, _), (r4, i4), (r2, i2), (r6, i6) = z[:5]
+    (z0, z8), (r4, i4), (r2, i2), (r6, i6) = z[:4]
     up, down = z0 + z8, z0 - z8
     even = [up + r4, down - i4, up - r4, down + i4]
     gap, tot = ROOT * (r2 - r6), ROOT * (i2 + i6)
     turn = [r2 + r6, gap - tot, i6 - i2, -gap - tot]
-    (r1, i1), (r5, i5), (r9, i9), (rd, id_) = z[5:]
+    (r1, i1), (r5, i5), (r9, i9), (rd, id_) = z[4:]
     s = (r1 + r9, i1 + i9)
     d = (r1 - r9, i1 - i9)
     t = (r5 + rd, i5 + id_)
@@ -308,106 +319,128 @@
     return jnp.where(code < 0.0, -values, values)
 
 
-def layer_kernel(
-    taps_ref, got_ref, fh_any, fl_any, ih_any, il_any, out_ref,
-    qp, kp, vp, qs, ks, vs, xh, xl, zs, conv, mgrad, fgrad, peak, sums, head,
-    fh_ref, fl_ref, ih_ref, il_ref, table_sem,
-):
-    blocks, height, _ = got_ref.shape
-    rows = height // FIELDS
-    total = blocks * rows
-    chunks = rows // CHUNK
+def table_dot(table_ref, f, both):
+    half = both.shape[1] // 2
+    which = min(f, 1)
+    found = jnp.dot(table_ref[0, which], both, preferred_element_type=jnp.float32)
+    rest = jnp.dot(table_ref[1, which], both[:, :half], preferred_element_type=jnp.float32)
+    return found[:, :half] + (found[:, half:] + rest)
+
+
+def times_spec(first, second, conj_second, packed):
+    (ar, ai), (br, bi) = first, second
+    inner = ai * bi
+    cross = ai * br - ar * bi if conj_second else ai * br + ar * bi
+    if packed:
+        line = lax.broadcasted_iota(jnp.int32, inner.shape, 0) == 0
+        cross = jnp.where(line, inner, cross)
+        inner = jnp.where(line, 0.0, inner)
+    return (ar * br + inner if conj_second else ar * br - inner), cross
+
+
+def spec_parts(spec, rows, column):
+    lanes = slice(column * LANES, (column + 1) * LANES)
+    return spec[:rows, lanes], spec[rows:, lanes]
+
+
+def side_by_side(products):
+    pairs = [split_pair(jnp.concatenate(pair, axis=0)) for pair in products]
+    return jnp.concatenate([high for high, _ in pairs] + [low for _, low in pairs], axis=1)
+
+
+def put_classes(ref, column, columns, rows, b0, values, turn):
+    for f, pair in enumerate(forward_classes(values)):
+        if f > 0:
+            cosine, sine = [turn[2 * f - 2 + n, pl.ds(b0, CHUNK), :] for n in range(2)]
+            pair = (pair[0] * cosine + pair[1] * sine, pair[1] * cosine - pair[0] * sine)
+        for part, value in enumerate(pair):
+            high, low = split_pair(value)
+            at = pl.ds(part * rows + b0, CHUNK)
+            ref[f, at, pl.ds(column * LANES, LANES)] = high
+            ref[f, at, pl.ds((columns + column) * LANES, LANES)] = low
+
+
+def take_classes(ref, column, rows, b0, turn):
+    lanes = pl.ds(column * LANES, LANES)
+    found = []
+    for f in range(ref.shape[0]):
+        pair = ref[f, pl.ds(b0, CHUNK), lanes], ref[f, pl.ds(rows + b0, CHUNK), lanes]
+        if f > 0:
+            cosine, sine = [turn[2 * f - 2 + n, pl.ds(b0, CHUNK), :] for n in range(2)]
+            pair = (pair[0] * cosine - pair[1] * sine, pair[1] * cosine + pair[0] * sine)
+        found.append(pair)
+    return inverse_classes(found)
+
+
+def short_filter(gain, ref, at):
+    return (
+        gain[0] * ref[pl.ds(at, CHUNK), :]
+        + gain[1] * ref[pl.ds(at - 1, CHUNK), :]
+        + gain[2] * ref[pl.ds(at - 2, CHUNK), :]
+    )
+
+
+def widen(me_ref, got, targets, rows):
+    def body(step, carry):
+        b0 = pl.multiple_of(step * CHUNK, CHUNK)
+        for k, ref in zip(PLACES, got):
+            at = pl.multiple_of((me_ref[0] ^ k) * rows + b0, CHUNK)
+            for field, (target, pad) in enumerate(targets):
+                target[pl.ds(pad + at, CHUNK), :] = ref[pl.ds(field * rows + b0, CHUNK), :].astype(
+                    jnp.float32
+                )
+        return carry
+
+    lax.fori_loop(0, rows // CHUNK, body, 0)
+
+
+def gains(taps_ref):
+    return [[taps_ref[3 * i + j : 3 * i + j + 1, :] for j in range(3)] for i in range(3)]
+
+
+def layer_kernel(me_ref, gain_ref, turn, forward_ref, inverse_ref, *refs):
+    got, outs = refs[:RADIX], refs[RADIX : 2 * RADIX]
+    qp, kp, vp, hs, cot, ks, vs, xs, zs, conv, mgrad, fgrad, peak, sums, head = refs[2 * RADIX :]
+    rows = got[0].shape[0] // FIELDS
+    total = RADIX * rows
     f32 = jnp.float32
-    copies = [
-        pltpu.make_async_copy(src, dst, table_sem.at[n])
-        for n, (src, dst) in enumerate(
-            ((fh_any, fh_ref), (fl_any, fl_ref), (ih_any, ih_ref), (il_any, il_ref))
-        )
-    ]
-    for copy in copies:
-        copy.start()
-    zero = jnp.zeros((PAD, LANES), f32)
+    gain = gains(gain_ref)
     for ref in (qp, kp, vp):
-        ref[pl.ds(0, PAD), :] = zero
-    gain = [[taps_ref[3 * i + j : 3 * i + j + 1, :] for j in range(3)] for i in range(3)]
-
-    def widen(step, carry):
-        b0 = pl.multiple_of(step * CHUNK, CHUNK)
-        for a in range(blocks):
-            for field, ref in enumerate((qp, kp, vp)):
-                ref[pl.ds(PAD + a * rows + b0, CHUNK), :] = got_ref[
-                    a, pl.ds(field * rows + b0, CHUNK), :
-                ].astype(f32)
-        return carry
-
-    lax.fori_loop(0, chunks, widen, 0)
-    for f in (0, 1):
-        xh[f, pl.ds(rows, rows), :] = jnp.zeros((rows, 3 * LANES), jnp.bfloat16)
-        xl[f, pl.ds(rows, rows), :] = jnp.zeros((rows, 3 * LANES), jnp.bfloat16)
-
-    def short(ref, i, at):
-        return (
-            gain[i][0] * ref[pl.ds(at, CHUNK), :]
-            + gain[i][1] * ref[pl.ds(at - 1, CHUNK), :]
-            + gain[i][2] * ref[pl.ds(at - 2, CHUNK), :]
-        )
+        ref[pl.ds(0, PAD), :] = jnp.zeros((PAD, LANES), f32)
+    for ref in (cot, ks, vs, conv, mgrad):
+        ref[pl.ds(total, PAD), :] = jnp.zeros((PAD, LANES), f32)
+    widen(me_ref, got, ((qp, PAD), (kp, PAD), (vp, PAD), (hs, 0), (cot, 0)), rows)
 
     def enter(step, carry):
         b0 = pl.multiple_of(step * CHUNK, CHUNK)
-
-        def put(column, values):
-            for f, (real, imag) in enumerate(forward_classes(values)):
-                for part, value in ((0, real), (1, imag)):
-                    if value is not None:
-                        high, low = split_pair(value)
-                        place = (f, pl.ds(part * rows + b0, CHUNK), pl.ds(column * LANES, LANES))
-                        xh[place] = high
-                        xl[place] = low
-
         mixed = []
-        for a in range(blocks):
+        for a in range(RADIX):
             at = a * rows + b0
-            key_filt = short(kp, 1, PAD + at)
-            value_filt = short(vp, 2, PAD + at)
+            key_filt = short_filter(gain[1], kp, PAD + at)
+            value_filt = short_filter(gain[2], vp, PAD + at)
             ks[pl.ds(at, CHUNK), :] = key_filt
             vs[pl.ds(at, CHUNK), :] = value_filt
             mixed.append(key_filt * value_filt)
-        put(0, mixed)
-        put(1, [got_ref[a, pl.ds(3 * rows + b0, CHUNK), :].astype(f32) for a in range(blocks)])
+        put_classes(xs, 0, 3, rows, b0, mixed, turn)
+        filt = [hs[pl.ds(a * rows + b0, CHUNK), :] for a in range(RADIX)]
+        put_classes(xs, 1, 3, rows, b0, filt, turn)
         conv_grad = []
-        for a in range(blocks):
+        for a in range(RADIX):
             at = a * rows + b0
-            query_filt = short(qp, 0, PAD + at)
-            conv_grad.append(
-                query_filt * got_ref[a, pl.ds(4 * rows + b0, CHUNK), :].astype(f32)
-            )
-        put(2, conv_grad)
+            conv_grad.append(short_filter(gain[0], qp, PAD + at) * cot[pl.ds(at, CHUNK), :])
+        put_classes(xs, 2, 3, rows, b0, conv_grad, turn)
         return carry
 
-    lax.fori_loop(0, chunks, enter, 0)
-    for copy in copies:
-        copy.wait()
-
-    def three(high_table, low_table, high, low):
-        return (
-            jnp.dot(high_table, high, preferred_element_type=f32)
-            + jnp.dot(high_table, low, preferred_element_type=f32)
-            + jnp.dot(low_table, high, preferred_element_type=f32)
-        )
-
-    def turn(f, carry):
-        spec = three(fh_ref[f], fl_ref[f], xh[f], xl[f])
-        (mr, hr, gr), (mi, hi, gi) = [
-            [spec[p * rows : (p + 1) * rows, c * LANES : (c + 1) * LANES] for c in range(3)]
-            for p in range(2)
+    lax.fori_loop(0, rows // CHUNK, enter, 0)
+    for f in range(xs.shape[0]):
+        spec = table_dot(forward_ref, f, xs[f])
+        mixed, filt, grad = [spec_parts(spec, rows, c) for c in range(3)]
+        products = [
+            times_spec(mixed, filt, False, f == 0),
+            times_spec(grad, filt, True, f == 0),
+            times_spec(grad, mixed, True, f == 0),
         ]
-        real = jnp.concatenate([mr * hr - mi * hi, gr * hr + gi * hi, gr * mr + gi * mi], axis=1)
-        imag = jnp.concatenate([mr * hi + mi * hr, gi * hr - gr * hi, gi * mr - gr * mi], axis=1)
-        high, low = split_pair(jnp.concatenate([real, imag], axis=0))
-        zs[f] = three(ih_ref[f], il_ref[f], high, low)
-        return carry
-
-    lax.fori_loop(0, len(CLASSES), turn, 0)
+        zs[f] = table_dot(inverse_ref, f, side_by_side(products))
     peak[...] = jnp.zeros_like(peak)
     sums[...] = jnp.zeros_like(sums)
 
@@ -415,98 +448,107 @@
         b0 = pl.multiple_of(step * CHUNK, CHUNK)
 
         def take(column, ref):
-            lanes = pl.ds(column * LANES, LANES)
-            found = inverse_classes(
-                [
-                    (zs[f, pl.ds(b0, CHUNK), lanes], zs[f, pl.ds(rows + b0, CHUNK), lanes])
-                    for f in range(len(CLASSES))
-                ]
-            )
+            found = take_classes(zs, column, rows, b0, turn)
             for a, value in enumerate(found):
                 ref[pl.ds(a * rows + b0, CHUNK), :] = value
                 size = jnp.abs(value)
                 peak[column, a] = jnp.maximum(peak[column, a], jnp.maximum(size[:8], size[8:]))
             return found
 
-        def add(i, source, grads):
+        def add(i, source, values, other):
             found = [jnp.zeros((CHUNK, LANES), f32)] * 3
-            for a, now in enumerate(grads):
+            for a, value in enumerate(values):
+                at = a * rows + b0
+                now = value * other[pl.ds(at, CHUNK), :]
                 for j in range(3):
-                    found[j] = found[j] + now * source[pl.ds(PAD + a * rows + b0 - j, CHUNK), :]
+                    found[j] = found[j] + now * source[pl.ds(PAD + at - j, CHUNK), :]
             for j in range(3):
                 sums[3 * i + j] += found[j][:8] + found[j][8:]
 
-        found = take(0, conv)
-        add(0, qp, [
-            value * got_ref[a, pl.ds(4 * rows + b0, CHUNK), :].astype(f32)
-            for a, value in enumerate(found)
-        ])
+        add(0, qp, take(0, conv), cot)
         found = take(1, mgrad)
-        add(1, kp, [
-            value * vs[pl.ds(a * rows + b0, CHUNK), :] for a, value in enumerate(found)
-        ])
-        add(2, vp, [
-            value * ks[pl.ds(a * rows + b0, CHUNK), :] for a, value in enumerate(found)
-        ])
+        add(1, kp, found, vs)
+        add(2, vp, found, ks)
         take(2, fgrad)
         return carry
 
-    lax.fori_loop(0, chunks, leave, 0)
+    lax.fori_loop(0, rows // CHUNK, leave, 0)
     grad_scale = 1.0 / math.sqrt(total)
-    head[pl.ds(0, 48), :] = jnp.zeros((48, LANES), f32)
+    head[...] = jnp.zeros_like(head)
     for n in range(9):
         at = 32 + n if n < 8 else 22
         head[pl.ds(at, 1), :] = jnp.sum(sums[n], axis=0, keepdims=True) * grad_scale
     head[pl.ds(40, 8), :] = split_pair(head[pl.ds(32, 8), :])[1].astype(f32)
-    for a in range(blocks):
-        first = a * rows
+    for k, out_ref in zip(PLACES, outs):
+        a = me_ref[0] ^ k
+        first = pl.multiple_of(a * rows, rows)
+        after = first + rows
         for i, ref in enumerate((qp, kp, vp)):
-            head[pl.ds(2 * i, 2), :] = ref[pl.ds(PAD + first - 2, 2), :]
+            head[pl.ds(2 * i, 2), :] = ref[pl.ds(first + PAD - 2, 2), :]
         for column, ref in enumerate((conv, mgrad, fgrad)):
             top = jnp.max(peak[column, a], axis=0, keepdims=True)
             scale = jnp.maximum(top * (1.0 + 2.0**-7), TINY).astype(jnp.bfloat16).astype(f32)
             head[pl.ds(6 + column, 1), :] = scale
-            out_ref[a, pl.ds(column * rows, rows), :] = log_code(
+            out_ref[pl.ds(column * rows, rows), :] = log_code(
                 ref[pl.ds(first, rows), :], 1.0 / scale
             )
-        if a + 1 < blocks:
-            after = first + rows
-            grad_in = got_ref[a + 1, pl.ds(4 * rows, CHUNK), :].astype(f32)[:2]
-            head[pl.ds(16, 2), :] = conv[pl.ds(after, 2), :] * grad_in
-            head[pl.ds(18, 2), :] = mgrad[pl.ds(after, 2), :] * vs[pl.ds(after, 2), :]
-            head[pl.ds(20, 2), :] = mgrad[pl.ds(after, 2), :] * ks[pl.ds(after, 2), :]
-        else:
-            head[pl.ds(16, 6), :] = jnp.zeros((6, LANES), f32)
+        for i, (ref, other) in enumerate(((conv, cot), (mgrad, vs), (mgrad, ks))):
+            head[pl.ds(16 + 2 * i, 2), :] = ref[pl.ds(after, 2), :] * other[pl.ds(after, 2), :]
         head[pl.ds(24, 8), :] = split_pair(head[pl.ds(16, 8), :])[1].astype(f32)
-        out_ref[a, pl.ds(3 * rows, 48), :] = head[...].astype(jnp.bfloat16)
+        out_ref[pl.ds(3 * rows, 48), :] = head[...].astype(jnp.bfloat16)
+
+
+def prepare_kernel(
+    me_ref, turns_ref, forward_any, inverse_any, taps_any, _, turn, forward_ref, inverse_ref, gain_ref, wide_ref,
+):
+    lane = pl.ds(pl.multiple_of(me_ref[0] * LANES, LANES), LANES)
+    forward_ref[...] = forward_any[...]
+    inverse_ref[...] = inverse_any[...]
+    for n in range(turn.shape[0]):
+        turn[n] = jnp.broadcast_to(turns_ref[:, n : n + 1], turn.shape[1:])
+    for i in range(3):
+        for j in range(3):
+            at = 3 * i + j
+            wide_ref[at : at + 1, :] = taps_any[i, j : j + 1, :].astype(jnp.float32)
+            gain_ref[at : at + 1, :] = taps_any[i, j : j + 1, lane].astype(jnp.float32)
 
 
 def whole_vmem(count):
     return [pl.BlockSpec(memory_space=pltpu.VMEM)] * count
 
 
-def pack_kernel(*refs):
-    *sources, out_ref = refs
+def whole_any(count):
+    return [pl.BlockSpec(memory_space=pl.ANY)] * count
+
+
+IN_SMEM = pl.BlockSpec(memory_space=pltpu.SMEM)
+
+
+def pack_kernel(me_ref, *refs):
+    sources, outs = refs[:FIELDS], refs[FIELDS:]
     rows = sources[0].shape[0]
-    for a in range(out_ref.shape[0]):
-        for field, ref in enumerate(sources):
-            out_ref[a, pl.ds(field * rows, rows), :] = ref[:, a * LANES : (a + 1) * LANES]
-
-
-def finish_kernel(
-    got_ref, query_ref, key_ref, value_ref, cot_ref, taps_ref,
-    output, query_grad, key_grad, value_grad, filter_grad, taps_grad,
-    wide, grads,
-):
+    for k, out_ref in zip(PLACES, outs):
+        lane = pl.multiple_of((me_ref[0] ^ k) * LANES, LANES)
+        for field, source in enumerate(sources):
+            out_ref[pl.ds(field * rows, rows), :] = source[:, pl.ds(lane, LANES)]
+
+
+def finish_kernel(me_ref, *refs):
+    got, (query_ref, key_ref, value_ref, cot_ref, taps_ref), outs = (
+        refs[:RADIX],
+        refs[RADIX : RADIX + 5],
+        refs[RADIX + 5 :],
+    )
+    output, query_grad, key_grad, value_grad, filter_grad, taps_grad, wide, grads = outs
     rows = output.shape[0]
     f32, bf16 = jnp.float32, jnp.bfloat16
-    for a in range(got_ref.shape[0]):
-        lanes = slice(a * LANES, (a + 1) * LANES)
-        head = got_ref[a, pl.ds(3 * rows, 48), :].astype(f32)
+    for k, got_ref in zip(PLACES, got):
+        lanes = pl.ds(pl.multiple_of((me_ref[0] ^ k) * LANES, LANES), LANES)
+        head = got_ref[pl.ds(3 * rows, 48), :].astype(f32)
         conv, mixed_grad, filt = [
-            log_decode(got_ref[a, pl.ds(n * rows, rows), :], head[6 + n : 7 + n]) for n in range(3)
+            log_decode(got_ref[pl.ds(n * rows, rows), :], head[6 + n : 7 + n]) for n in range(3)
         ]
-        filter_grad[:, lanes] = filt * (1.0 / math.sqrt(got_ref.shape[0] * rows))
+        filter_grad[:, lanes] = filt * (1.0 / math.sqrt(RADIX * rows))
         taps = head[32:40] + head[40:48]
         for n in range(8):
             taps_grad[n // 3, n % 3 : n % 3 + 1, lanes] = taps[n : n + 1]
@@ -515,7 +557,7 @@
         filtered = []
         gain = []
         for i, ref in enumerate((query_ref, key_ref, value_ref)):
-            gain.append([taps_ref[i, j : j + 1, lanes].astype(f32) for j in range(3)])
+            gain.append([taps_ref[3 * i + j : 3 * i + j + 1, lanes] for j in range(3)])
             wide[i, pl.ds(PAD - 2, 2), :] = head[2 * i : 2 * i + 2]
             wide[i, pl.ds(PAD, rows), :] = ref[:, lanes].astype(f32)
             filtered.append(
@@ -539,59 +581,81 @@
             ).astype(bf16)
 
 
+def swap_blocks(blocks):
+    devices = range(RADIX)
+    return [
+        lax.ppermute(block, "ctx", [(i, i ^ k) for i in devices]) if k else block
+        for k, block in zip(PLACES, blocks)
+    ]
+
+
+def held(arrays, space):
+    return [pltpu.with_memory_space_constraint(jnp.asarray(one), space) for one in arrays]
+
+
 def local_fast(query_in, key_in, value_in, long_filter, short_taps, out_grad):
     rows, channels = query_in.shape
-    blocks = lax.axis_size("ctx")
-    total = blocks * rows
+    total = RADIX * rows
     f32, bf16 = jnp.float32, jnp.bfloat16
     shape = jax.ShapeDtypeStruct
+    me = lax.axis_index("ctx").astype(jnp.int32).reshape(1)
     packed = pl.pallas_call(
         pack_kernel,
-        out_shape=shape((blocks, FIELDS * rows, LANES), bf16),
-        in_specs=whole_vmem(5),
-        out_specs=whole_vmem(1)[0],
+        out_shape=[pltpu.VMEM((FIELDS * rows, LANES), bf16)] * RADIX,
+        in_specs=[IN_SMEM] + whole_vmem(FIELDS),
+        out_specs=whole_vmem(RADIX),
         name="pack",
-    )(query_in, key_in, value_in, long_filter, out_grad)
-    got = lax.all_to_all(packed, "ctx", 0, 0)
-    gain = lax.dynamic_slice_in_dim(
-        short_taps.reshape(9, channels), lax.axis_index("ctx") * LANES, LANES, 1
-    ).astype(f32)
-    tables = class_tables(rows)
-    count = len(CLASSES)
+    )(me, query_in, key_in, value_in, long_filter, out_grad)
+    got = swap_blocks(packed)
+    forward, inverse, turns = class_tables(rows)
+    count = 1 + len(CLASSES)
+    ready = pl.pallas_call(
+        prepare_kernel,
+        out_shape=[
+            pltpu.VMEM((2 * len(CLASSES), rows, LANES), f32),
+            pltpu.VMEM(forward.shape, bf16),
+            pltpu.VMEM(inverse.shape, bf16),
+            pltpu.VMEM((16, LANES), f32),
+            pltpu.VMEM((16, channels), f32),
+        ],
+        in_specs=[IN_SMEM] + whole_vmem(5),
+        out_specs=whole_vmem(5),
+        name="prepare",
+    )(me, *held((turns, forward, inverse), pltpu.HBM), short_taps, *held(got[1:2], pltpu.VMEM))
+    ready = held(ready, pltpu.VMEM)
     done = pl.pallas_call(
         layer_kernel,
-        out_shape=shape((blocks, 3 * rows + 48, LANES), bf16),
-        in_specs=whole_vmem(2) + [pl.BlockSpec(memory_space=pl.ANY)] * 4,
-        out_specs=whole_vmem(1)[0],
-        scratch_shapes=[pltpu.VMEM((total + PAD, LANES), f32)] * 3
-        + [pltpu.VMEM((total, LANES), f32)] * 3
-        + [pltpu.VMEM((count, 2 * rows, 3 * LANES), bf16)] * 2
-        + [pltpu.VMEM((count, 2 * rows, 3 * LANES), f32)]
-        + [pltpu.VMEM((total, LANES), f32)] * 3
+        out_shape=[pltpu.VMEM((3 * rows + 48, LANES), bf16)] * RADIX,
+        in_specs=[IN_SMEM] + whole_vmem(4 + RADIX),
+        out_specs=whole_vmem(RADIX),
+        scratch_shapes=[pltpu.VMEM((total + PAD, LANES), f32)] * 7
         + [
-            pltpu.VMEM((3, blocks, 8, LANES), f32),
+            pltpu.VMEM((count, 2 * rows, 6 * LANES), bf16),
+            pltpu.VMEM((count, 2 * rows, 3 * LANES), f32),
+        ]
+        + [pltpu.VMEM((total + PAD, LANES), f32)] * 3
+        + [
+            pltpu.VMEM((3, RADIX, 8, LANES), f32),
             pltpu.VMEM((9, 8, LANES), f32),
             pltpu.VMEM((48, LANES), f32),
-        ]
-        + [pltpu.VMEM((count, 2 * rows, 2 * rows), bf16)] * 4
-        + [pltpu.SemaphoreType.DMA((4,))],
-        compiler_params=pltpu.CompilerParams(vmem_limit_bytes=48 * 1024 * 1024),
+        ],
+        compiler_params=pltpu.CompilerParams(vmem_limit_bytes=32 * 1024 * 1024),
         name="layer",
-    )(gain, got, *tables)
-    back = lax.all_to_all(done, "ctx", 0, 0)
+    )(me, ready[3], *ready[:3], *held(got, pltpu.VMEM))
+    back = swap_blocks(done)
     return tuple(
         pl.pallas_call(
             finish_kernel,
             out_shape=[shape((rows, channels), bf16)] * 4
             + [shape((rows, channels), f32), shape((3, 3, channels), f32)],
-            in_specs=whole_vmem(6),
+            in_specs=[IN_SMEM] + whole_vmem(RADIX + 5),
             out_specs=whole_vmem(6),
             scratch_shapes=[
                 pltpu.VMEM((3, PAD + rows, LANES), f32),
                 pltpu.VMEM((3, rows + PAD, LANES), f32),
             ],
             name="finish",
-        )(back, query_in, key_in, value_in, out_grad, short_taps)
+        )(me, *held(back, pltpu.VMEM), query_in, key_in, value_in, out_grad, ready[4])
     )
 
 

time: 61.8 us -> 47.4 us (0.77)
  blocking collectives: 16.7 us -> 0 us
  starting transfers between devices: 5.3 us -> 16.6 us
  Pallas kernels: 19.1 us -> 16.2 us
  local copies, waits for them, and re-layouts: 2.66 us -> 0 us
  waiting for transfers between devices: 16.3 us -> 13.7 us
  other arithmetic: 0.69 us -> 0 us
    all_to_all x1 -> x0, blocking collectives: 16.7 us -> none  [local_fast(): back = lax.all_to_all(done, 'ctx', 0, 0)]
    ppermute x0 -> x14, starting transfers between devices: none -> 16.6 us  [swap_blocks(): lax.ppermute(block, 'ctx', [(i, i ^ k) for i in devices])]
    all_to_all x1 -> x0, waiting for transfers between devices: 16.3 us -> none  [local_fast(): got = lax.all_to_all(packed, 'ctx', 0, 0)]
    ppermute x0 -> x14, waiting for transfers between devices: none -> 13.7 us  [swap_blocks(): lax.ppermute(block, 'ctx', [(i, i ^ k) for i in devices])]
    all_to_all x1 -> x0, starting transfers between devices: 5.3 us -> none  [local_fast(): got = lax.all_to_all(packed, 'ctx', 0, 0)]
    pallas_call x2 -> x3, Pallas kernels: 15.1 us -> 12.4 us  [the longest x1 8.44 us: local_fast(): pl.pallas_call(layer_kernel, out_shape=[pltpu.VMEM((3 * rows + 48, LANES)...]
    reshape x1 -> x0, local copies, waits for them, and re-layouts: 1.38 us -> none  [local_fast(): short_taps.reshape(9, channels)]
    unnamed x8 -> x0, local copies, waits for them, and re-layouts: 1.28 us -> none
  transfers between devices with their start and end apart: 1 -> 14, of which waited for: 1 -> 9; matrix products, arithmetic and copies ran while one was open for 3% -> 0% of each run, Pallas kernels for 0% -> 3%
where the time goes in v2:
time: 47.4 us; the launch traced here: 47.2 us
  starting transfers between devices  16.6 us (35%)
  Pallas kernels  16.2 us (34%)
  waiting for transfers between devices  13.7 us (29%)
  between operations  0.67 us (1%)
    ppermute x14, starting transfers between devices, swap_blocks(): lax.ppermute(block, 'ctx', [(i, i ^ k) for i in devices])  16.6 us
    ppermute x14, waiting for transfers between devices, swap_blocks(): lax.ppermute(block, 'ctx', [(i, i ^ k) for i in devices])  13.7 us
    pallas_call x1, Pallas kernels, local_fast(): pl.pallas_call(layer_kernel, out_shape=[pltpu.VMEM((3 * rows + 48, LANES)...  8.44 us
    pallas_call x1, Pallas kernels, local_fast(): pl.pallas_call(finish_kernel, out_shape=[shape((rows, channels), bf16)] *...  3.77 us
    pallas_call x1, Pallas kernels, local_fast(): pl.pallas_call(pack_kernel, out_shape=[pltpu.VMEM((FIELDS * rows, LANES),...  2.38 us
    pallas_call x1, Pallas kernels, local_fast(): pl.pallas_call(prepare_kernel, out_shape=[pltpu.VMEM((2 * len(CLASSES), r...  1.61 us
  transfers between devices with their start and end apart: 14, of which 9 were waited for; matrix products, arithmetic and copies ran while one was open for 0% of the time, Pallas kernels for 3%

profile of v2, /device:TPU:0, one launch (start us, length us, event | category | flops | bytes accessed | tf_op | source)
XLA Modules:
  0.0 47.2 jit_solution(17835964012785859092)
XLA Ops:
  0.6 2.4 %pack.1 = (bf16[640,128]{1,0:T(8,128)(2,1)S(1)}, bf16[640,128]{1,0:T(8,128)(2,1)S(1)}, bf16[640,128]{1,0:T(8,128)(2,1)S(1)}, bf16[640,128]{1,0:T(8,128)(2,1)}, b...) custom-call(s32[1]{0:T(128)} %bitcast.me_ref, ...), custom_call_target="tpu_custom_call" | custom-call | tf_op jit(solution)/shard_map/pack/pallas_call | solution.py:602
  3.0 3.9 %collective-permute-start = (bf16[640,128]{1,0:T(8,128)(2,1)S(1)}, bf16[640,128]{1,0:T(8,128)(2,1)S(1)}, u32[]{:S(2)}, u32[]{:S(2)}) collective-permute-start(bf16[640,128]{1,0:T(8,128)(2,1)S(1)} %get-tuple-element.27), channel_id=1, source_target_pairs={{0,24},{4,28},{8,16},{12,20},{16,8},{20,12},{24,0},{28,4},{1,25},{... | collective-permute-start | bytes 491528 | tf_op jit(solution)/shard_map/ppermute | solution.py:587
  6.9 0.5 %collective-permute-start.1 = (bf16[640,128]{1,0:T(8,128)(2,1)S(1)}, bf16[640,128]{1,0:T(8,128)(2,1)S(1)}, u32[]{:S(2)}, u32[]{:S(2)}) collective-permute-start(bf16[640,128]{1,0:T(8,128)(2,1)S(1)} %get-tuple-element.33), channel_id=1, source_target_pairs={{0,8},{4,12},{8,0},{12,4},{16,24},{20,28},{24,16},{28,20},{1,9},{5... | collective-permute-start | bytes 491528 | tf_op jit(solution)/shard_map/ppermute | solution.py:587
  7.5 1.7 %collective-permute-start.3 = (bf16[640,128]{1,0:T(8,128)(2,1)}, bf16[640,128]{1,0:T(8,128)(2,1)S(1)}, u32[]{:S(2)}, u32[]{:S(2)}) collective-permute-start(bf16[640,128]{1,0:T(8,128)(2,1)} %get-tuple-element.35), channel_id=1, source_target_pairs={{0,12},{4,8},{8,4},{12,0},{16,28},{20,24},{24,20},{28,16},{1,13},{... | collective-permute-start | bytes 491528 | tf_op jit(solution)/shard_map/ppermute | solution.py:587
  9.2 1.0 %collective-permute-start.4 = (bf16[640,128]{1,0:T(8,128)(2,1)}, bf16[640,128]{1,0:T(8,128)(2,1)S(1)}, u32[]{:S(2)}, u32[]{:S(2)}) collective-permute-start(bf16[640,128]{1,0:T(8,128)(2,1)} %get-tuple-element.36), channel_id=1, source_target_pairs={{0,28},{4,24},{8,20},{12,16},{16,12},{20,8},{24,4},{28,0},{1,29},{... | collective-permute-start | bytes 491528 | tf_op jit(solution)/shard_map/ppermute | solution.py:587
  10.1 1.8 %collective-permute-done._.refs_1_ = bf16[640,128]{1,0:T(8,128)(2,1)S(1)} collective-permute-done((bf16[640,128]{1,0:T(8,128)(2,1)S(1)}, bf16[640,128]{1,0:T(8,128)(2,1)S(1)}, u32[]{:S(2)}, u32[]{:S(2)}) %collective-permute-start) | collective-permute-done | bytes 163872 | tf_op jit(solution)/shard_map/ppermute | solution.py:587
  11.9 2.0 %collective-permute-start.5 = (bf16[640,128]{1,0:T(8,128)(2,1)}, bf16[640,128]{1,0:T(8,128)(2,1)S(1)}, u32[]{:S(2)}, u32[]{:S(2)}) collective-permute-start(bf16[640,128]{1,0:T(8,128)(2,1)} %get-tuple-element.37), channel_id=1, source_target_pairs={{0,16},{4,20},{8,24},{12,28},{16,0},{20,4},{24,8},{28,12},{1,17},{... | collective-permute-start | bytes 491528 | tf_op jit(solution)/shard_map/ppermute | solution.py:587
  14.0 2.0 %collective-permute-done.1.refs_2_ = bf16[640,128]{1,0:T(8,128)(2,1)S(1)} collective-permute-done((bf16[640,128]{1,0:T(8,128)(2,1)S(1)}, bf16[640,128]{1,0:T(8,128)(2,1)S(1)}, u32[]{:S(2)}, u32[]{:S(2)}) %collective-permute-start.1) | collective-permute-done | bytes 163872 | tf_op jit(solution)/shard_map/ppermute | solution.py:587
  16.0 1.6 %prepare.1 = (f32[14,128,128]{2,1,0:T(8,128)S(1)}, bf16[2,2,256,256]{3,2,1,0:T(8,128)(2,1)S(1)}, bf16[2,2,256,256]{3,2,1,0:T(8,128)(2,1)S(1)}, f32[16,128]{1,0:T(8,128)S(1)}, f32[16,1024]{1,0:T(8,128)S(1)}) custom-call(s32[1]{0:T(128)} %bitcast.me_ref, f32[128,128]{1,0:T(8,128)} %constant.12.clone.turns_ref, ...), custom_call_target="tpu_custom_call" | custom-call | tf_op jit(solution)/shard_map/prepare/pallas_call | solution.py:612
  17.6 1.0 %collective-permute-done.3.refs_4_ = bf16[640,128]{1,0:T(8,128)(2,1)S(1)} collective-permute-done((bf16[640,128]{1,0:T(8,128)(2,1)}, bf16[640,128]{1,0:T(8,128)(2,1)S(1)}, u32[]{:S(2)}, u32[]{:S(2)}) %collective-permute-start.3) | collective-permute-done | bytes 163872 | tf_op jit(solution)/shard_map/ppermute | solution.py:587
  18.6 2.4 %collective-permute-done.4.refs_5_ = bf16[640,128]{1,0:T(8,128)(2,1)S(1)} collective-permute-done((bf16[640,128]{1,0:T(8,128)(2,1)}, bf16[640,128]{1,0:T(8,128)(2,1)S(1)}, u32[]{:S(2)}, u32[]{:S(2)}) %collective-permute-start.4) | collective-permute-done | bytes 163872 | tf_op jit(solution)/shard_map/ppermute | solution.py:587
  21.0 8.4 %layer.1 = (bf16[432,128]{1,0:T(8,128)(2,1)S(1)}, bf16[432,128]{1,0:T(8,128)(2,1)S(1)}, bf16[432,128]{1,0:T(8,128)(2,1)S(1)}, bf16[432,128]{1,0:T(8,128)(2,1)S(1...) custom-call(s32[1]{0:T(128)} %bitcast.me_ref, ...), custom_call_target="tpu_custom_call" | custom-call | tf_op jit(solution)/shard_map/layer/pallas_call | solution.py:626
  29.5 2.2 %collective-permute-start.7 = (bf16[432,128]{1,0:T(8,128)(2,1)S(1)}, bf16[432,128]{1,0:T(8,128)(2,1)S(1)}, u32[]{:S(2)}, u32[]{:S(2)}) collective-permute-start(bf16[432,128]{1,0:T(8,128)(2,1)S(1)} %get-tuple-element.40), channel_id=1, source_target_pairs={{0,24},{4,28},{8,16},{12,20},{16,8},{20,12},{24,0},{28,4},{1,25},{... | collective-permute-start | bytes 331784 | tf_op jit(solution)/shard_map/ppermute | solution.py:587
  31.7 0.5 %collective-permute-start.8 = (bf16[432,128]{1,0:T(8,128)(2,1)S(1)}, bf16[432,128]{1,0:T(8,128)(2,1)S(1)}, u32[]{:S(2)}, u32[]{:S(2)}) collective-permute-start(bf16[432,128]{1,0:T(8,128)(2,1)S(1)} %get-tuple-element.41), channel_id=1, source_target_pairs={{0,8},{4,12},{8,0},{12,4},{16,24},{20,28},{24,16},{28,20},{1,9},{5... | collective-permute-start | bytes 331784 | tf_op jit(solution)/shard_map/ppermute | solution.py:587
  32.2 0.4 collective-permute-start.9
  32.6 1.3 %collective-permute-start.10 = (bf16[432,128]{1,0:T(8,128)(2,1)S(1)}, bf16[432,128]{1,0:T(8,128)(2,1)S(1)}, u32[]{:S(2)}, u32[]{:S(2)}) collective-permute-start(bf16[432,128]{1,0:T(8,128)(2,1)S(1)} %get-tuple-element.43), channel_id=1, source_target_pairs={{0,12},{4,8},{8,4},{12,0},{16,28},{20,24},{24,20},{28,16},{1,13},{... | collective-permute-start | bytes 331784 | tf_op jit(solution)/shard_map/ppermute | solution.py:587
  33.9 1.5 %collective-permute-start.11 = (bf16[432,128]{1,0:T(8,128)(2,1)S(1)}, bf16[432,128]{1,0:T(8,128)(2,1)S(1)}, u32[]{:S(2)}, u32[]{:S(2)}) collective-permute-start(bf16[432,128]{1,0:T(8,128)(2,1)S(1)} %get-tuple-element.44), channel_id=1, source_target_pairs={{0,28},{4,24},{8,20},{12,16},{16,12},{20,8},{24,4},{28,0},{1,29},{... | collective-permute-start | bytes 331784 | tf_op jit(solution)/shard_map/ppermute | solution.py:587
  35.5 0.8 %collective-permute-done.7.refs_1_ = bf16[432,128]{1,0:T(8,128)(2,1)S(1)} collective-permute-done((bf16[432,128]{1,0:T(8,128)(2,1)S(1)}, bf16[432,128]{1,0:T(8,128)(2,1)S(1)}, u32[]{:S(2)}, u32[]{:S(2)}) %collective-permute-start.7) | collective-permute-done | bytes 110624 | tf_op jit(solution)/shard_map/ppermute | solution.py:587
  36.3 1.4 %collective-permute-start.12 = (bf16[432,128]{1,0:T(8,128)(2,1)S(1)}, bf16[432,128]{1,0:T(8,128)(2,1)S(1)}, u32[]{:S(2)}, u32[]{:S(2)}) collective-permute-start(bf16[432,128]{1,0:T(8,128)(2,1)S(1)} %get-tuple-element.45), channel_id=1, source_target_pairs={{0,16},{4,20},{8,24},{12,28},{16,0},{20,4},{24,8},{28,12},{1,17},{... | collective-permute-start | bytes 331784 | tf_op jit(solution)/shard_map/ppermute | solution.py:587
  37.7 0.8 %collective-permute-done.8.refs_2_ = bf16[432,128]{1,0:T(8,128)(2,1)S(1)} collective-permute-done((bf16[432,128]{1,0:T(8,128)(2,1)S(1)}, bf16[432,128]{1,0:T(8,128)(2,1)S(1)}, u32[]{:S(2)}, u32[]{:S(2)}) %collective-permute-start.8) | collective-permute-done | bytes 110624 | tf_op jit(solution)/shard_map/ppermute | solution.py:587
  38.6 2.3 %collective-permute-done.10.refs_4_ = bf16[432,128]{1,0:T(8,128)(2,1)S(1)} collective-permute-done((bf16[432,128]{1,0:T(8,128)(2,1)S(1)}, bf16[432,128]{1,0:T(8,128)(2,1)S(1)}, u32[]{:S(2)}, u32[]{:S(2)}) %collective-permute-start.10) | collective-permute-done | bytes 110624 | tf_op jit(solution)/shard_map/ppermute | solution.py:587
  40.8 1.8 %collective-permute-done.11.refs_5_ = bf16[432,128]{1,0:T(8,128)(2,1)S(1)} collective-permute-done((bf16[432,128]{1,0:T(8,128)(2,1)S(1)}, bf16[432,128]{1,0:T(8,128)(2,1)S(1)}, u32[]{:S(2)}, u32[]{:S(2)}) %collective-permute-start.11) | collective-permute-done | bytes 110624 | tf_op jit(solution)/shard_map/ppermute | solution.py:587
  42.6 0.8 %collective-permute-done.12.refs_6_ = bf16[432,128]{1,0:T(8,128)(2,1)S(1)} collective-permute-done((bf16[432,128]{1,0:T(8,128)(2,1)S(1)}, bf16[432,128]{1,0:T(8,128)(2,1)S(1)}, u32[]{:S(2)}, u32[]{:S(2)}) %collective-permute-start.12) | collective-permute-done | bytes 110624 | tf_op jit(solution)/shard_map/ppermute | solution.py:587
  43.4 3.8 %finish.1 = (bf16[128,1024]{1,0:T(8,128)(2,1)}, bf16[128,1024]{1,0:T(8,128)(2,1)}, bf16[128,1024]{1,0:T(8,128)(2,1)}, bf16[128,1024]{1,0:T(8,128)(2,1)}, f32[128,1024]{1,0:T(8,128)}, /*index=5*/f32[3,3,1024]{2,1,0:T(4,128)}) custom-call(s32[1]{0:T(128)} %bitcast.me_ref, bf16[432,128]{1,0:T(8,128)(2,1)S(1)} %get-tuple-element.39.refs_0_, ...), custom_call_target="tpu_custom_call" | custom-call | tf_op jit(solution)/shard_map/finish/pallas_call | solution.py:647
  (8 shorter events, 0.1 us)
Async XLA Ops:
  3.0 8.9 %collective-permute-start = (bf16[640,128]{1,0:T(8,128)(2,1)S(1)}, bf16[640,128]{1,0:T(8,128)(2,1)S(1)}, u32[]{:S(2)}, u32[]{:S(2)}) collective-permute-start(bf16[640,128]{1,0:T(8,128)(2,1)S(1)} %get-tuple-element.27), channel_id=1, source_target_pairs={{0,24},{4,28},{8,16},{12,20},{16,8},{20,12},{24,0},{28,4},{1,25},{... | collective-permute-start | bytes 491528 | tf_op jit(solution)/shard_map/ppermute | solution.py:587
  6.9 9.1 %collective-permute-start.1 = (bf16[640,128]{1,0:T(8,128)(2,1)S(1)}, bf16[640,128]{1,0:T(8,128)(2,1)S(1)}, u32[]{:S(2)}, u32[]{:S(2)}) collective-permute-start(bf16[640,128]{1,0:T(8,128)(2,1)S(1)} %get-tuple-element.33), channel_id=1, source_target_pairs={{0,8},{4,12},{8,0},{12,4},{16,24},{20,28},{24,16},{28,20},{1,9},{5... | collective-permute-start | bytes 491528 | tf_op jit(solution)/shard_map/ppermute | solution.py:587
  7.5 10.2 %collective-permute-start.2 = (bf16[640,128]{1,0:T(8,128)(2,1)}, bf16[640,128]{1,0:T(8,128)(2,1)S(1)}, u32[]{:S(2)}, u32[]{:S(2)}) collective-permute-start(bf16[640,128]{1,0:T(8,128)(2,1)} %get-tuple-element.34), channel_id=1, source_target_pairs={{0,20},{4,16},{8,28},{12,24},{16,4},{20,0},{24,12},{28,8},{1,21},{... | collective-permute-start | bytes 491528 | tf_op jit(solution)/shard_map/ppermute | solution.py:587
  7.5 11.2 %collective-permute-start.3 = (bf16[640,128]{1,0:T(8,128)(2,1)}, bf16[640,128]{1,0:T(8,128)(2,1)S(1)}, u32[]{:S(2)}, u32[]{:S(2)}) collective-permute-start(bf16[640,128]{1,0:T(8,128)(2,1)} %get-tuple-element.35), channel_id=1, source_target_pairs={{0,12},{4,8},{8,4},{12,0},{16,28},{20,24},{24,20},{28,16},{1,13},{... | collective-permute-start | bytes 491528 | tf_op jit(solution)/shard_map/ppermute | solution.py:587
  9.2 11.8 %collective-permute-start.4 = (bf16[640,128]{1,0:T(8,128)(2,1)}, bf16[640,128]{1,0:T(8,128)(2,1)S(1)}, u32[]{:S(2)}, u32[]{:S(2)}) collective-permute-start(bf16[640,128]{1,0:T(8,128)(2,1)} %get-tuple-element.36), channel_id=1, source_target_pairs={{0,28},{4,24},{8,20},{12,16},{16,12},{20,8},{24,4},{28,0},{1,29},{... | collective-permute-start | bytes 491528 | tf_op jit(solution)/shard_map/ppermute | solution.py:587
  11.9 9.1 %collective-permute-start.5 = (bf16[640,128]{1,0:T(8,128)(2,1)}, bf16[640,128]{1,0:T(8,128)(2,1)S(1)}, u32[]{:S(2)}, u32[]{:S(2)}) collective-permute-start(bf16[640,128]{1,0:T(8,128)(2,1)} %get-tuple-element.37), channel_id=1, source_target_pairs={{0,16},{4,20},{8,24},{12,28},{16,0},{20,4},{24,8},{28,12},{1,17},{... | collective-permute-start | bytes 491528 | tf_op jit(solution)/shard_map/ppermute | solution.py:587
  16.0 5.0 %collective-permute-start.6 = (bf16[640,128]{1,0:T(8,128)(2,1)S(1)}, bf16[640,128]{1,0:T(8,128)(2,1)S(1)}, u32[]{:S(2)}, u32[]{:S(2)}) collective-permute-start(bf16[640,128]{1,0:T(8,128)(2,1)S(1)} %get-tuple-element.38), channel_id=1, source_target_pairs={{0,4},{4,0},{8,12},{12,8},{16,20},{20,16},{24,28},{28,24},{1,5},{5... | collective-permute-start | bytes 491528 | tf_op jit(solution)/shard_map/ppermute | solution.py:587
  29.5 6.8 %collective-permute-start.7 = (bf16[432,128]{1,0:T(8,128)(2,1)S(1)}, bf16[432,128]{1,0:T(8,128)(2,1)S(1)}, u32[]{:S(2)}, u32[]{:S(2)}) collective-permute-start(bf16[432,128]{1,0:T(8,128)(2,1)S(1)} %get-tuple-element.40), channel_id=1, source_target_pairs={{0,24},{4,28},{8,16},{12,20},{16,8},{20,12},{24,0},{28,4},{1,25},{... | collective-permute-start | bytes 331784 | tf_op jit(solution)/shard_map/ppermute | solution.py:587
  31.7 6.8 %collective-permute-start.8 = (bf16[432,128]{1,0:T(8,128)(2,1)S(1)}, bf16[432,128]{1,0:T(8,128)(2,1)S(1)}, u32[]{:S(2)}, u32[]{:S(2)}) collective-permute-start(bf16[432,128]{1,0:T(8,128)(2,1)S(1)} %get-tuple-element.41), channel_id=1, source_target_pairs={{0,8},{4,12},{8,0},{12,4},{16,24},{20,28},{24,16},{28,20},{1,9},{5... | collective-permute-start | bytes 331784 | tf_op jit(solution)/shard_map/ppermute | solution.py:587
  32.2 6.4 %collective-permute-start.9 = (bf16[432,128]{1,0:T(8,128)(2,1)S(1)}, bf16[432,128]{1,0:T(8,128)(2,1)S(1)}, u32[]{:S(2)}, u32[]{:S(2)}) collective-permute-start(bf16[432,128]{1,0:T(8,128)(2,1)S(1)} %get-tuple-element.42), channel_id=1, source_target_pairs={{0,20},{4,16},{8,28},{12,24},{16,4},{20,0},{24,12},{28,8},{1,21},{... | collective-permute-start | bytes 331784 | tf_op jit(solution)/shard_map/ppermute | solution.py:587
  32.6 8.2 %collective-permute-start.10 = (bf16[432,128]{1,0:T(8,128)(2,1)S(1)}, bf16[432,128]{1,0:T(8,128)(2,1)S(1)}, u32[]{:S(2)}, u32[]{:S(2)}) collective-permute-start(bf16[432,128]{1,0:T(8,128)(2,1)S(1)} %get-tuple-element.43), channel_id=1, source_target_pairs={{0,12},{4,8},{8,4},{12,0},{16,28},{20,24},{24,20},{28,16},{1,13},{... | collective-permute-start | bytes 331784 | tf_op jit(solution)/shard_map/ppermute | solution.py:587
  33.9 8.7 %collective-permute-start.11 = (bf16[432,128]{1,0:T(8,128)(2,1)S(1)}, bf16[432,128]{1,0:T(8,128)(2,1)S(1)}, u32[]{:S(2)}, u32[]{:S(2)}) collective-permute-start(bf16[432,128]{1,0:T(8,128)(2,1)S(1)} %get-tuple-element.44), channel_id=1, source_target_pairs={{0,28},{4,24},{8,20},{12,16},{16,12},{20,8},{24,4},{28,0},{1,29},{... | collective-permute-start | bytes 331784 | tf_op jit(solution)/shard_map/ppermute | solution.py:587
  36.3 7.1 %collective-permute-start.12 = (bf16[432,128]{1,0:T(8,128)(2,1)S(1)}, bf16[432,128]{1,0:T(8,128)(2,1)S(1)}, u32[]{:S(2)}, u32[]{:S(2)}) collective-permute-start(bf16[432,128]{1,0:T(8,128)(2,1)S(1)} %get-tuple-element.45), channel_id=1, source_target_pairs={{0,16},{4,20},{8,24},{12,28},{16,0},{20,4},{24,8},{28,12},{1,17},{... | collective-permute-start | bytes 331784 | tf_op jit(solution)/shard_map/ppermute | solution.py:587
  38.5 4.9 %collective-permute-start.13 = (bf16[432,128]{1,0:T(8,128)(2,1)S(1)}, bf16[432,128]{1,0:T(8,128)(2,1)S(1)}, u32[]{:S(2)}, u32[]{:S(2)}) collective-permute-start(bf16[432,128]{1,0:T(8,128)(2,1)S(1)} %get-tuple-element.46), channel_id=1, source_target_pairs={{0,4},{4,0},{8,12},{12,8},{16,20},{20,16},{24,28},{28,24},{1,5},{5... | collective-permute-start | bytes 331784 | tf_op jit(solution)/shard_map/ppermute | solution.py:587

commit v3 on v2

--- a/solution.py
+++ b/solution.py
@@ -206,6 +206,7 @@
 PAD = 8
 CHUNK = 16
 PLACES = (0, 6, 2, 5, 3, 7, 4, 1)
+EARLY = 4
 CURVE = 15.0
 REACH = 120.0
 SLOPE = 2.0 * REACH / math.log2(1.0 + CURVE)
@@ -433,14 +434,17 @@
 
     lax.fori_loop(0, rows // CHUNK, enter, 0)
     for f in range(xs.shape[0]):
-        spec = table_dot(forward_ref, f, xs[f])
-        mixed, filt, grad = [spec_parts(spec, rows, c) for c in range(3)]
+        zs[f] = table_dot(forward_ref, f, xs[f])
+    for f in range(xs.shape[0]):
+        mixed, filt, grad = [spec_parts(zs[f], rows, c) for c in range(3)]
         products = [
             times_spec(mixed, filt, False, f == 0),
             times_spec(grad, filt, True, f == 0),
             times_spec(grad, mixed, True, f == 0),
         ]
-        zs[f] = table_dot(inverse_ref, f, side_by_side(products))
+        xs[f] = side_by_side(products)
+    for f in range(xs.shape[0]):
+        zs[f] = table_dot(inverse_ref, f, xs[f])
     peak[...] = jnp.zeros_like(peak)
     sums[...] = jnp.zeros_like(sums)
 
@@ -499,7 +503,8 @@
 
 
 def prepare_kernel(
-    me_ref, turns_ref, forward_any, inverse_any, taps_any, _, turn, forward_ref, inverse_ref, gain_ref, wide_ref,
+    me_ref, turns_ref, forward_any, inverse_any, taps_any, _, query_ref, key_ref, value_ref, cot_ref,
+    turn, forward_ref, inverse_ref, gain_ref, wide_ref, early_ref, wide,
 ):
     lane = pl.ds(pl.multiple_of(me_ref[0] * LANES, LANES), LANES)
     forward_ref[...] = forward_any[...]
@@ -511,6 +516,16 @@
             at = 3 * i + j
             wide_ref[at : at + 1, :] = taps_any[i, j : j + 1, :].astype(jnp.float32)
             gain_ref[at : at + 1, :] = taps_any[i, j : j + 1, lane].astype(jnp.float32)
+    rows = cot_ref.shape[0]
+    for i, ref in enumerate((query_ref, key_ref, value_ref)):
+        wide[pl.ds(0, PAD), :] = jnp.zeros((PAD, wide.shape[1]), jnp.float32)
+        wide[pl.ds(PAD, rows), :] = ref[...].astype(jnp.float32)
+        early_ref[i] = (
+            wide_ref[3 * i : 3 * i + 1, :] * wide[pl.ds(PAD, rows), :]
+            + wide_ref[3 * i + 1 : 3 * i + 2, :] * wide[pl.ds(PAD - 1, rows), :]
+            + wide_ref[3 * i + 2 : 3 * i + 3, :] * wide[pl.ds(PAD - 2, rows), :]
+        )
+    early_ref[3] = cot_ref[...].astype(jnp.float32)
 
 
 def whole_vmem(count):
@@ -524,61 +539,94 @@
 IN_SMEM = pl.BlockSpec(memory_space=pltpu.SMEM)
 
 
-def pack_kernel(me_ref, *refs):
-    sources, outs = refs[:FIELDS], refs[FIELDS:]
+def pack_kernel(places, me_ref, *refs):
+    sources, outs, land, sem = refs[:FIELDS], refs[FIELDS:-2], refs[-2], refs[-1]
     rows = sources[0].shape[0]
-    for k, out_ref in zip(PLACES, outs):
-        lane = pl.multiple_of((me_ref[0] ^ k) * LANES, LANES)
-        for field, source in enumerate(sources):
-            out_ref[pl.ds(field * rows, rows), :] = source[:, pl.ds(lane, LANES)]
-
-
-def finish_kernel(me_ref, *refs):
-    got, (query_ref, key_ref, value_ref, cot_ref, taps_ref), outs = (
-        refs[:RADIX],
-        refs[RADIX : RADIX + 5],
-        refs[RADIX + 5 :],
-    )
-    output, query_grad, key_grad, value_grad, filter_grad, taps_grad, wide, grads = outs
-    rows = output.shape[0]
+    copies = [
+        pltpu.make_async_copy(source, land.at[field], sem.at[field])
+        for field, source in enumerate(sources)
+    ]
+    for copy in copies:
+        copy.start()
+    for field, copy in enumerate(copies):
+        copy.wait()
+        for k, out_ref in zip(places, outs):
+            lane = pl.multiple_of((me_ref[0] ^ k) * LANES, LANES)
+            out_ref[pl.ds(field * rows, rows), :] = land[field, :, pl.ds(lane, LANES)]
+
+
+def finish_blocks(me_ref, places, got, wide_ref, early_ref, outs, grads, stage, stage_filter, sem):
+    rows = early_ref.shape[1]
     f32, bf16 = jnp.float32, jnp.bfloat16
-    for k, got_ref in zip(PLACES, got):
+    copies = []
+    for n, (k, got_ref) in enumerate(zip(places, got)):
         lanes = pl.ds(pl.multiple_of((me_ref[0] ^ k) * LANES, LANES), LANES)
         head = got_ref[pl.ds(3 * rows, 48), :].astype(f32)
         conv, mixed_grad, filt = [
-            log_decode(got_ref[pl.ds(n * rows, rows), :], head[6 + n : 7 + n]) for n in range(3)
+            log_decode(got_ref[pl.ds(c * rows, rows), :], head[6 + c : 7 + c]) for c in range(3)
         ]
-        filter_grad[:, lanes] = filt * (1.0 / math.sqrt(RADIX * rows))
-        taps = head[32:40] + head[40:48]
-        for n in range(8):
-            taps_grad[n // 3, n % 3 : n % 3 + 1, lanes] = taps[n : n + 1]
+        stage_filter[n] = filt * (1.0 / math.sqrt(RADIX * rows))
         pairs = head[16:24] + head[24:32]
-        taps_grad[2, 2:3, lanes] = pairs[6:7]
+        line = lax.broadcasted_iota(jnp.int32, (PAD, LANES), 0)
         filtered = []
         gain = []
-        for i, ref in enumerate((query_ref, key_ref, value_ref)):
-            gain.append([taps_ref[3 * i + j : 3 * i + j + 1, lanes] for j in range(3)])
-            wide[i, pl.ds(PAD - 2, 2), :] = head[2 * i : 2 * i + 2]
-            wide[i, pl.ds(PAD, rows), :] = ref[:, lanes].astype(f32)
-            filtered.append(
-                gain[i][0] * wide[i, pl.ds(PAD, rows), :]
-                + gain[i][1] * wide[i, pl.ds(PAD - 1, rows), :]
-                + gain[i][2] * wide[i, pl.ds(PAD - 2, rows), :]
+        for i in range(3):
+            gain.append([wide_ref[3 * i + j : 3 * i + j + 1, lanes] for j in range(3)])
+            before, last = head[2 * i : 2 * i + 1], head[2 * i + 1 : 2 * i + 2]
+            top = early_ref[i, 0:PAD, lanes] + jnp.where(
+                line == 0,
+                gain[i][1] * last + gain[i][2] * before,
+                jnp.where(line == 1, gain[i][2] * last, 0.0),
             )
-        output[:, lanes] = (filtered[0] * conv).astype(bf16)
+            filtered.append(jnp.concatenate([top, early_ref[i, PAD:, lanes]], axis=0))
+        stage[n, 0] = (filtered[0] * conv).astype(bf16)
         inner = (
-            conv * cot_ref[:, lanes].astype(f32),
+            conv * early_ref[3, :, lanes],
             mixed_grad * filtered[2],
             mixed_grad * filtered[1],
         )
-        for i, ref in enumerate((query_grad, key_grad, value_grad)):
+        for i in range(3):
             grads[i, pl.ds(0, rows), :] = inner[i]
             grads[i, pl.ds(rows, 2), :] = pairs[2 * i : 2 * i + 2]
-            ref[:, lanes] = (
+            stage[n, 1 + i] = (
                 gain[i][0] * inner[i]
                 + gain[i][1] * grads[i, pl.ds(1, rows), :]
                 + gain[i][2] * grads[i, pl.ds(2, rows), :]
             ).astype(bf16)
+        for c, out in enumerate(outs):
+            source = stage.at[n, c] if c < 4 else stage_filter.at[n]
+            copies.append(pltpu.make_async_copy(source, out.at[:, lanes], sem.at[len(copies)]))
+            copies[-1].start()
+    return copies
+
+
+def finish_kernel(me_ref, *refs):
+    got, (wide_ref, early_ref), outs, scratch = refs[:EARLY], refs[EARLY : EARLY + 2], refs[EARLY + 2 : EARLY + 7], refs[EARLY + 7 :]
+    for copy in finish_blocks(me_ref, PLACES[:EARLY], got, wide_ref, early_ref, outs, *scratch):
+        copy.wait()
+
+
+def finish_last_kernel(me_ref, *refs):
+    got, (wide_ref, early_ref), outs, taps_grad, scratch = (
+        refs[:RADIX],
+        refs[RADIX : RADIX + 2],
+        refs[RADIX + 7 : RADIX + 12],
+        refs[RADIX + 12],
+        refs[RADIX + 13 :],
+    )
+    rows = early_ref.shape[1]
+    copies = finish_blocks(
+        me_ref, PLACES[EARLY:], got[EARLY:], wide_ref, early_ref, outs, *scratch
+    )
+    for k, got_ref in zip(PLACES, got):
+        lanes = pl.ds(pl.multiple_of((me_ref[0] ^ k) * LANES, LANES), LANES)
+        head = got_ref[pl.ds(3 * rows, 48), :].astype(jnp.float32)
+        taps = head[32:40] + head[40:48]
+        for n in range(8):
+            taps_grad[n // 3, n % 3 : n % 3 + 1, lanes] = taps[n : n + 1]
+        taps_grad[2, 2:3, lanes] = head[22:23] + head[30:31]
+    for copy in copies:
+        copy.wait()
 
 
 def swap_blocks(blocks):
@@ -598,14 +646,26 @@
     total = RADIX * rows
     f32, bf16 = jnp.float32, jnp.bfloat16
     shape = jax.ShapeDtypeStruct
+    inputs = held((query_in, key_in, value_in, out_grad), pltpu.HBM)
+    small = pltpu.CompilerParams(vmem_limit_bytes=12 * 1024 * 1024)
     me = lax.axis_index("ctx").astype(jnp.int32).reshape(1)
-    packed = pl.pallas_call(
-        pack_kernel,
-        out_shape=[pltpu.VMEM((FIELDS * rows, LANES), bf16)] * RADIX,
-        in_specs=[IN_SMEM] + whole_vmem(FIELDS),
-        out_specs=whole_vmem(RADIX),
-        name="pack",
-    )(me, query_in, key_in, value_in, long_filter, out_grad)
+    sources = held((query_in, key_in, value_in, long_filter, out_grad), pltpu.HBM)
+
+    def pack(places):
+        return pl.pallas_call(
+            partial(pack_kernel, places),
+            out_shape=[pltpu.VMEM((FIELDS * rows, LANES), bf16)] * len(places),
+            in_specs=[IN_SMEM] + whole_any(FIELDS),
+            out_specs=whole_vmem(len(places)),
+            scratch_shapes=[
+                pltpu.VMEM((FIELDS, rows, channels), bf16),
+                pltpu.SemaphoreType.DMA((FIELDS,)),
+            ],
+            compiler_params=small,
+            name="pack",
+        )(me, *sources)
+
+    packed = pack(PLACES)
     got = swap_blocks(packed)
     forward, inverse, turns = class_tables(rows)
     count = 1 + len(CLASSES)
@@ -617,11 +677,14 @@
             pltpu.VMEM(inverse.shape, bf16),
             pltpu.VMEM((16, LANES), f32),
             pltpu.VMEM((16, channels), f32),
+            pltpu.VMEM((4, rows, channels), f32),
         ],
-        in_specs=[IN_SMEM] + whole_vmem(5),
-        out_specs=whole_vmem(5),
+        in_specs=[IN_SMEM] + whole_vmem(9),
+        out_specs=whole_vmem(6),
+        scratch_shapes=[pltpu.VMEM((PAD + rows, channels), f32)],
+        compiler_params=small,
         name="prepare",
-    )(me, *held((turns, forward, inverse), pltpu.HBM), short_taps, *held(got[1:2], pltpu.VMEM))
+    )(me, *held((turns, forward, inverse), pltpu.HBM), short_taps, *held(got[1:2], pltpu.VMEM), *inputs)
     ready = held(ready, pltpu.VMEM)
     done = pl.pallas_call(
         layer_kernel,
@@ -639,23 +702,40 @@
             pltpu.VMEM((9, 8, LANES), f32),
             pltpu.VMEM((48, LANES), f32),
         ],
-        compiler_params=pltpu.CompilerParams(vmem_limit_bytes=32 * 1024 * 1024),
+        compiler_params=pltpu.CompilerParams(vmem_limit_bytes=20 * 1024 * 1024),
         name="layer",
     )(me, ready[3], *ready[:3], *held(got, pltpu.VMEM))
-    back = swap_blocks(done)
+    back = held(swap_blocks(done), pltpu.VMEM)
+    results = [shape((rows, channels), bf16)] * 4 + [shape((rows, channels), f32)]
+
+    def finish_scratch(count):
+        return [
+            pltpu.VMEM((3, rows + PAD, LANES), f32),
+            pltpu.VMEM((count, 4, rows, LANES), bf16),
+            pltpu.VMEM((count, rows, LANES), f32),
+            pltpu.SemaphoreType.DMA((5 * count,)),
+        ]
+
+    begun = pl.pallas_call(
+        finish_kernel,
+        out_shape=results,
+        in_specs=[IN_SMEM] + whole_vmem(EARLY + 2),
+        out_specs=whole_any(5),
+        scratch_shapes=finish_scratch(EARLY),
+        compiler_params=small,
+        name="finish",
+    )(me, *back[:EARLY], *ready[4:])
     return tuple(
         pl.pallas_call(
-            finish_kernel,
-            out_shape=[shape((rows, channels), bf16)] * 4
-            + [shape((rows, channels), f32), shape((3, 3, channels), f32)],
-            in_specs=[IN_SMEM] + whole_vmem(RADIX + 5),
-            out_specs=whole_vmem(6),
-            scratch_shapes=[
-                pltpu.VMEM((3, PAD + rows, LANES), f32),
-                pltpu.VMEM((3, rows + PAD, LANES), f32),
-            ],
-            name="finish",
-        )(me, *held(back, pltpu.VMEM), query_in, key_in, value_in, out_grad, ready[4])
+            finish_last_kernel,
+            out_shape=results + [shape((3, 3, channels), f32)],
+            in_specs=[IN_SMEM] + whole_vmem(RADIX + 2) + whole_any(5),
+            out_specs=whole_any(5) + whole_vmem(1),
+            scratch_shapes=finish_scratch(RADIX - EARLY),
+            input_output_aliases={RADIX + 3 + n: n for n in range(5)},
+            compiler_params=small,
+            name="finish_last",
+        )(me, *back, *ready[4:], *begun)
     )
 
 

time: 47.4 us -> 43.7 us (0.922)
  waiting for transfers between devices: 13.7 us -> 10 us
  Pallas kernels: 16.2 us -> 15.2 us
  local copies, waits for them, and re-layouts: 0 us -> 0.74 us
    ppermute x14, waiting for transfers between devices: 13.7 us -> 10 us  [swap_blocks(): lax.ppermute(block, 'ctx', [(i, i ^ k) for i in devices])]
    pallas_call x2 -> x3, Pallas kernels: 6.15 us -> 4.94 us  [the longest x1 2.09 us: local_fast(): pl.pallas_call(finish_last_kernel, out_shape=results + [shape((3, 3, chan...]
    pallas_call x1, Pallas kernels: 1.61 us -> 2.76 us  [local_fast(): pl.pallas_call(prepare_kernel, out_shape=[pltpu.VMEM((2 * len(CLASSES), r...]
    pallas_call x1, Pallas kernels: 8.44 us -> 7.49 us  [local_fast(): pl.pallas_call(layer_kernel, out_shape=[pltpu.VMEM((3 * rows + 48, LANES)...]
    unnamed x0 -> x2, local copies, waits for them, and re-layouts: none -> 0.74 us
  transfers between devices with their start and end apart: 14 -> 14, of which waited for: 9 -> 8; matrix products, arithmetic and copies ran while one was open for 0% -> 0% of each run, Pallas kernels for 3% -> 10%
where the time goes in v3:
time: 43.7 us; the launch traced here: 43.5 us
  starting transfers between devices  16.9 us (39%)
  Pallas kernels  15.2 us (35%)
  waiting for transfers between devices  10 us (23%)
  local copies, waits for them, and re-layouts  0.74 us (2%)
  between operations  0.69 us (2%)
    ppermute x14, starting transfers between devices, swap_blocks(): lax.ppermute(block, 'ctx', [(i, i ^ k) for i in devices])  16.9 us
    ppermute x14, waiting for transfers between devices, swap_blocks(): lax.ppermute(block, 'ctx', [(i, i ^ k) for i in devices])  10 us
    pallas_call x1, Pallas kernels, local_fast(): pl.pallas_call(layer_kernel, out_shape=[pltpu.VMEM((3 * rows + 48, LANES)...  7.49 us
    pallas_call x1, Pallas kernels, local_fast(): pl.pallas_call(prepare_kernel, out_shape=[pltpu.VMEM((2 * len(CLASSES), r...  2.76 us
    pallas_call x1, Pallas kernels, local_fast(): pl.pallas_call(finish_last_kernel, out_shape=results + [shape((3, 3, chan...  2.09 us
    pallas_call x1, Pallas kernels, local_fast(): pl.pallas_call(finish_kernel, out_shape=results, in_specs=[IN_SMEM] + who...  1.47 us
    pallas_call x1, Pallas kernels, pack(): pl.pallas_call(partial(pack_kernel, places), out_shape=[pltpu.VMEM((FIELD...  1.38 us
  transfers between devices with their start and end apart: 14, of which 8 were waited for; matrix products, arithmetic and copies ran while one was open for 0% of the time, Pallas kernels for 10%

profile of v3, /device:TPU:0, one launch (start us, length us, event | category | flops | bytes accessed | tf_op | source)
XLA Modules:
  0.0 43.5 jit_solution(10089074548339509520)
XLA Ops:
  0.6 1.4 %pack.1 = (bf16[640,128]{1,0:T(8,128)(2,1)S(1)}, bf16[640,128]{1,0:T(8,128)(2,1)S(1)}, bf16[640,128]{1,0:T(8,128)(2,1)S(1)}, bf16[640,128]{1,0:T(8,128)(2,1)S(1)...) custom-call(s32[1]{0:T(128)} %bitcast.me_ref, ...), custom_call_target="tpu_custom_call" | custom-call | tf_op jit(solution)/shard_map/pack/pallas_call | solution.py:655
  2.0 4.0 %collective-permute-start = (bf16[640,128]{1,0:T(8,128)(2,1)S(1)}, bf16[640,128]{1,0:T(8,128)(2,1)S(1)}, u32[]{:S(2)}, u32[]{:S(2)}) collective-permute-start(bf16[640,128]{1,0:T(8,128)(2,1)S(1)} %get-tuple-element.33), channel_id=1, source_target_pairs={{0,24},{4,28},{8,16},{12,20},{16,8},{20,12},{24,0},{28,4},{1,25},{... | collective-permute-start | bytes 491528 | tf_op jit(solution)/shard_map/ppermute | solution.py:635
  6.0 0.5 %collective-permute-start.1 = (bf16[640,128]{1,0:T(8,128)(2,1)S(1)}, bf16[640,128]{1,0:T(8,128)(2,1)S(1)}, u32[]{:S(2)}, u32[]{:S(2)}) collective-permute-start(bf16[640,128]{1,0:T(8,128)(2,1)S(1)} %get-tuple-element.39), channel_id=1, source_target_pairs={{0,8},{4,12},{8,0},{12,4},{16,24},{20,28},{24,16},{28,20},{1,9},{5... | collective-permute-start | bytes 491528 | tf_op jit(solution)/shard_map/ppermute | solution.py:635
  6.5 1.7 %collective-permute-start.3 = (bf16[640,128]{1,0:T(8,128)(2,1)S(1)}, bf16[640,128]{1,0:T(8,128)(2,1)S(1)}, u32[]{:S(2)}, u32[]{:S(2)}) collective-permute-start(bf16[640,128]{1,0:T(8,128)(2,1)S(1)} %get-tuple-element.41), channel_id=1, source_target_pairs={{0,12},{4,8},{8,4},{12,0},{16,28},{20,24},{24,20},{28,16},{1,13},{... | collective-permute-start | bytes 491528 | tf_op jit(solution)/shard_map/ppermute | solution.py:635
  8.2 1.0 %collective-permute-start.4 = (bf16[640,128]{1,0:T(8,128)(2,1)S(1)}, bf16[640,128]{1,0:T(8,128)(2,1)S(1)}, u32[]{:S(2)}, u32[]{:S(2)}) collective-permute-start(bf16[640,128]{1,0:T(8,128)(2,1)S(1)} %get-tuple-element.42), channel_id=1, source_target_pairs={{0,28},{4,24},{8,20},{12,16},{16,12},{20,8},{24,4},{28,0},{1,29},{... | collective-permute-start | bytes 491528 | tf_op jit(solution)/shard_map/ppermute | solution.py:635
  9.2 1.8 %collective-permute-done._.refs_1_ = bf16[640,128]{1,0:T(8,128)(2,1)S(1)} collective-permute-done((bf16[640,128]{1,0:T(8,128)(2,1)S(1)}, bf16[640,128]{1,0:T(8,128)(2,1)S(1)}, u32[]{:S(2)}, u32[]{:S(2)}) %collective-permute-start) | collective-permute-done | bytes 163872 | tf_op jit(solution)/shard_map/ppermute | solution.py:635
  11.0 2.0 %collective-permute-start.5 = (bf16[640,128]{1,0:T(8,128)(2,1)S(1)}, bf16[640,128]{1,0:T(8,128)(2,1)S(1)}, u32[]{:S(2)}, u32[]{:S(2)}) collective-permute-start(bf16[640,128]{1,0:T(8,128)(2,1)S(1)} %get-tuple-element.43), channel_id=1, source_target_pairs={{0,16},{4,20},{8,24},{12,28},{16,0},{20,4},{24,8},{28,12},{1,17},{... | collective-permute-start | bytes 491528 | tf_op jit(solution)/shard_map/ppermute | solution.py:635
  13.0 2.0 %collective-permute-done.1.refs_2_ = bf16[640,128]{1,0:T(8,128)(2,1)S(1)} collective-permute-done((bf16[640,128]{1,0:T(8,128)(2,1)S(1)}, bf16[640,128]{1,0:T(8,128)(2,1)S(1)}, u32[]{:S(2)}, u32[]{:S(2)}) %collective-permute-start.1) | collective-permute-done | bytes 163872 | tf_op jit(solution)/shard_map/ppermute | solution.py:635
  15.1 0.7 %copy-done = bf16[3,3,1024]{2,1,0:T(4,128)(2,1)S(1)} copy-done((bf16[3,3,1024]{2,1,0:T(4,128)(2,1)S(1)}, bf16[3,3,1024]{2,1,0:T(4,128)(2,1)}, u32[]{:S(2)}) %copy-start) | copy-done | bytes 18456
  15.8 2.8 %prepare.1 = (f32[14,128,128]{2,1,0:T(8,128)S(1)}, bf16[2,2,256,256]{3,2,1,0:T(8,128)(2,1)S(1)}, bf16[2,2,256,256]{3,2,1,0:T(8,128)(2,1)S(1)}, f32[16,128]{1,0:T...) custom-call(s32[1]{0:T(128)} %bitcast.me_ref, f32[128,128]{1,0:T(8,128)} %constant.12.clone.turns_ref, ...), custom_call_target="tpu_custom_call" | custom-call | tf_op jit(solution)/shard_map/prepare/pallas_call | solution.py:672
  18.6 1.4 %collective-permute-done.4.refs_5_ = bf16[640,128]{1,0:T(8,128)(2,1)S(1)} collective-permute-done((bf16[640,128]{1,0:T(8,128)(2,1)S(1)}, bf16[640,128]{1,0:T(8,128)(2,1)S(1)}, u32[]{:S(2)}, u32[]{:S(2)}) %collective-permute-start.4) | collective-permute-done | bytes 163872 | tf_op jit(solution)/shard_map/ppermute | solution.py:635
  20.0 7.5 %layer.1 = (bf16[432,128]{1,0:T(8,128)(2,1)S(1)}, bf16[432,128]{1,0:T(8,128)(2,1)S(1)}, bf16[432,128]{1,0:T(8,128)(2,1)S(1)}, bf16[432,128]{1,0:T(8,128)(2,1)S(1...) custom-call(s32[1]{0:T(128)} %bitcast.me_ref, ...), custom_call_target="tpu_custom_call" | custom-call | tf_op jit(solution)/shard_map/layer/pallas_call | solution.py:689
  27.5 2.3 %collective-permute-start.7 = (bf16[432,128]{1,0:T(8,128)(2,1)S(1)}, bf16[432,128]{1,0:T(8,128)(2,1)S(1)}, u32[]{:S(2)}, u32[]{:S(2)}) collective-permute-start(bf16[432,128]{1,0:T(8,128)(2,1)S(1)} %get-tuple-element.46), channel_id=1, source_target_pairs={{0,24},{4,28},{8,16},{12,20},{16,8},{20,12},{24,0},{28,4},{1,25},{... | collective-permute-start | bytes 331784 | tf_op jit(solution)/shard_map/ppermute | solution.py:635
  29.8 0.5 %collective-permute-start.8 = (bf16[432,128]{1,0:T(8,128)(2,1)S(1)}, bf16[432,128]{1,0:T(8,128)(2,1)S(1)}, u32[]{:S(2)}, u32[]{:S(2)}) collective-permute-start(bf16[432,128]{1,0:T(8,128)(2,1)S(1)} %get-tuple-element.47), channel_id=1, source_target_pairs={{0,8},{4,12},{8,0},{12,4},{16,24},{20,28},{24,16},{28,20},{1,9},{5... | collective-permute-start | bytes 331784 | tf_op jit(solution)/shard_map/ppermute | solution.py:635
  30.7 1.3 %collective-permute-start.10 = (bf16[432,128]{1,0:T(8,128)(2,1)S(1)}, bf16[432,128]{1,0:T(8,128)(2,1)S(1)}, u32[]{:S(2)}, u32[]{:S(2)}) collective-permute-start(bf16[432,128]{1,0:T(8,128)(2,1)S(1)} %get-tuple-element.49), channel_id=1, source_target_pairs={{0,12},{4,8},{8,4},{12,0},{16,28},{20,24},{24,20},{28,16},{1,13},{... | collective-permute-start | bytes 331784 | tf_op jit(solution)/shard_map/ppermute | solution.py:635
  32.0 1.5 %collective-permute-start.11 = (bf16[432,128]{1,0:T(8,128)(2,1)S(1)}, bf16[432,128]{1,0:T(8,128)(2,1)S(1)}, u32[]{:S(2)}, u32[]{:S(2)}) collective-permute-start(bf16[432,128]{1,0:T(8,128)(2,1)S(1)} %get-tuple-element.50), channel_id=1, source_target_pairs={{0,28},{4,24},{8,20},{12,16},{16,12},{20,8},{24,4},{28,0},{1,29},{... | collective-permute-start | bytes 331784 | tf_op jit(solution)/shard_map/ppermute | solution.py:635
  33.6 0.7 %collective-permute-done.7.refs_1_ = bf16[432,128]{1,0:T(8,128)(2,1)S(1)} collective-permute-done((bf16[432,128]{1,0:T(8,128)(2,1)S(1)}, bf16[432,128]{1,0:T(8,128)(2,1)S(1)}, u32[]{:S(2)}, u32[]{:S(2)}) %collective-permute-start.7) | collective-permute-done | bytes 110624 | tf_op jit(solution)/shard_map/ppermute | solution.py:635
  34.3 1.5 %collective-permute-start.12 = (bf16[432,128]{1,0:T(8,128)(2,1)S(1)}, bf16[432,128]{1,0:T(8,128)(2,1)S(1)}, u32[]{:S(2)}, u32[]{:S(2)}) collective-permute-start(bf16[432,128]{1,0:T(8,128)(2,1)S(1)} %get-tuple-element.51), channel_id=1, source_target_pairs={{0,16},{4,20},{8,24},{12,28},{16,0},{20,4},{24,8},{28,12},{1,17},{... | collective-permute-start | bytes 331784 | tf_op jit(solution)/shard_map/ppermute | solution.py:635
  35.8 0.8 %collective-permute-done.8.refs_2_ = bf16[432,128]{1,0:T(8,128)(2,1)S(1)} collective-permute-done((bf16[432,128]{1,0:T(8,128)(2,1)S(1)}, bf16[432,128]{1,0:T(8,128)(2,1)S(1)}, u32[]{:S(2)}, u32[]{:S(2)}) %collective-permute-start.8) | collective-permute-done | bytes 110624 | tf_op jit(solution)/shard_map/ppermute | solution.py:635
  36.7 1.5 %finish.1 = (bf16[128,1024]{1,0:T(8,128)(2,1)}, bf16[128,1024]{1,0:T(8,128)(2,1)}, bf16[128,1024]{1,0:T(8,128)(2,1)}, bf16[128,1024]{1,0:T(8,128)(2,1)}, f32[128,1024]{1,0:T(8,128)}) custom-call(s32[1]{0:T(128)} %bitcast.me_ref, bf16[432,128]{1,0:T(8,128)(2,1)S(1)} %get-tuple-element.45.refs_0_, bf16[432,128]{1,0:T(8,128)(2,1)S(1)} %collective-permute-done.7.refs_1_, ...), custom_call_target="tpu_custom_call" | custom-call | tf_op jit(solution)/shard_map/finish/pallas_call | solution.py:719
  38.2 0.8 %collective-permute-done.10.refs_4_ = bf16[432,128]{1,0:T(8,128)(2,1)S(1)} collective-permute-done((bf16[432,128]{1,0:T(8,128)(2,1)S(1)}, bf16[432,128]{1,0:T(8,128)(2,1)S(1)}, u32[]{:S(2)}, u32[]{:S(2)}) %collective-permute-start.10) | collective-permute-done | bytes 110624 | tf_op jit(solution)/shard_map/ppermute | solution.py:635
  39.0 1.9 %collective-permute-done.11.refs_5_ = bf16[432,128]{1,0:T(8,128)(2,1)S(1)} collective-permute-done((bf16[432,128]{1,0:T(8,128)(2,1)S(1)}, bf16[432,128]{1,0:T(8,128)(2,1)S(1)}, u32[]{:S(2)}, u32[]{:S(2)}) %collective-permute-start.11) | collective-permute-done | bytes 110624 | tf_op jit(solution)/shard_map/ppermute | solution.py:635
  40.8 0.6 %collective-permute-done.12.refs_6_ = bf16[432,128]{1,0:T(8,128)(2,1)S(1)} collective-permute-done((bf16[432,128]{1,0:T(8,128)(2,1)S(1)}, bf16[432,128]{1,0:T(8,128)(2,1)S(1)}, u32[]{:S(2)}, u32[]{:S(2)}) %collective-permute-start.12) | collective-permute-done | bytes 110624 | tf_op jit(solution)/shard_map/ppermute | solution.py:635
  41.4 2.1 %finish_last.1 = (bf16[128,1024]{1,0:T(8,128)(2,1)}, bf16[128,1024]{1,0:T(8,128)(2,1)}, bf16[128,1024]{1,0:T(8,128)(2,1)}, bf16[128,1024]{1,0:T(8,128)(2,1)}, f3...) custom-call(s32[1]{0:T(128)} %bitcast.me_ref, ...), custom_call_target="tpu_custom_call", output_to_operand_aliasing={{0}: (11, {}), {1}: (12, {}), {2}: (13, {}), {3}: (14, {}),... | custom-call | tf_op jit(solution)/shard_map/finish_last/pallas_call | solution.py:729
  (11 shorter events, 0.5 us)
Async XLA Ops:
  2.0 9.0 %collective-permute-start = (bf16[640,128]{1,0:T(8,128)(2,1)S(1)}, bf16[640,128]{1,0:T(8,128)(2,1)S(1)}, u32[]{:S(2)}, u32[]{:S(2)}) collective-permute-start(bf16[640,128]{1,0:T(8,128)(2,1)S(1)} %get-tuple-element.33), channel_id=1, source_target_pairs={{0,24},{4,28},{8,16},{12,20},{16,8},{20,12},{24,0},{28,4},{1,25},{... | collective-permute-start | bytes 491528 | tf_op jit(solution)/shard_map/ppermute | solution.py:635
  6.0 9.1 %collective-permute-start.1 = (bf16[640,128]{1,0:T(8,128)(2,1)S(1)}, bf16[640,128]{1,0:T(8,128)(2,1)S(1)}, u32[]{:S(2)}, u32[]{:S(2)}) collective-permute-start(bf16[640,128]{1,0:T(8,128)(2,1)S(1)} %get-tuple-element.39), channel_id=1, source_target_pairs={{0,8},{4,12},{8,0},{12,4},{16,24},{20,28},{24,16},{28,20},{1,9},{5... | collective-permute-start | bytes 491528 | tf_op jit(solution)/shard_map/ppermute | solution.py:635
  6.5 12.1 %collective-permute-start.2 = (bf16[640,128]{1,0:T(8,128)(2,1)S(1)}, bf16[640,128]{1,0:T(8,128)(2,1)S(1)}, u32[]{:S(2)}, u32[]{:S(2)}) collective-permute-start(bf16[640,128]{1,0:T(8,128)(2,1)S(1)} %get-tuple-element.40), channel_id=1, source_target_pairs={{0,20},{4,16},{8,28},{12,24},{16,4},{20,0},{24,12},{28,8},{1,21},{... | collective-permute-start | bytes 491528 | tf_op jit(solution)/shard_map/ppermute | solution.py:635
  6.5 12.1 %collective-permute-start.3 = (bf16[640,128]{1,0:T(8,128)(2,1)S(1)}, bf16[640,128]{1,0:T(8,128)(2,1)S(1)}, u32[]{:S(2)}, u32[]{:S(2)}) collective-permute-start(bf16[640,128]{1,0:T(8,128)(2,1)S(1)} %get-tuple-element.41), channel_id=1, source_target_pairs={{0,12},{4,8},{8,4},{12,0},{16,28},{20,24},{24,20},{28,16},{1,13},{... | collective-permute-start | bytes 491528 | tf_op jit(solution)/shard_map/ppermute | solution.py:635
  8.2 11.7 %collective-permute-start.4 = (bf16[640,128]{1,0:T(8,128)(2,1)S(1)}, bf16[640,128]{1,0:T(8,128)(2,1)S(1)}, u32[]{:S(2)}, u32[]{:S(2)}) collective-permute-start(bf16[640,128]{1,0:T(8,128)(2,1)S(1)} %get-tuple-element.42), channel_id=1, source_target_pairs={{0,28},{4,24},{8,20},{12,16},{16,12},{20,8},{24,4},{28,0},{1,29},{... | collective-permute-start | bytes 491528 | tf_op jit(solution)/shard_map/ppermute | solution.py:635
  11.0 9.0 %collective-permute-start.5 = (bf16[640,128]{1,0:T(8,128)(2,1)S(1)}, bf16[640,128]{1,0:T(8,128)(2,1)S(1)}, u32[]{:S(2)}, u32[]{:S(2)}) collective-permute-start(bf16[640,128]{1,0:T(8,128)(2,1)S(1)} %get-tuple-element.43), channel_id=1, source_target_pairs={{0,16},{4,20},{8,24},{12,28},{16,0},{20,4},{24,8},{28,12},{1,17},{... | collective-permute-start | bytes 491528 | tf_op jit(solution)/shard_map/ppermute | solution.py:635
  15.1 4.9 %collective-permute-start.6 = (bf16[640,128]{1,0:T(8,128)(2,1)S(1)}, bf16[640,128]{1,0:T(8,128)(2,1)S(1)}, u32[]{:S(2)}, u32[]{:S(2)}) collective-permute-start(bf16[640,128]{1,0:T(8,128)(2,1)S(1)} %get-tuple-element.44), channel_id=1, source_target_pairs={{0,4},{4,0},{8,12},{12,8},{16,20},{20,16},{24,28},{28,24},{1,5},{5... | collective-permute-start | bytes 491528 | tf_op jit(solution)/shard_map/ppermute | solution.py:635
  15.1 0.7 %copy-start = (bf16[3,3,1024]{2,1,0:T(4,128)(2,1)S(1)}, bf16[3,3,1024]{2,1,0:T(4,128)(2,1)}, u32[]{:S(2)}) copy-start(bf16[3,3,1024]{2,1,0:T(4,128)(2,1)} %taps_any.1) | copy-start | bytes 55300
  27.5 6.8 %collective-permute-start.7 = (bf16[432,128]{1,0:T(8,128)(2,1)S(1)}, bf16[432,128]{1,0:T(8,128)(2,1)S(1)}, u32[]{:S(2)}, u32[]{:S(2)}) collective-permute-start(bf16[432,128]{1,0:T(8,128)(2,1)S(1)} %get-tuple-element.46), channel_id=1, source_target_pairs={{0,24},{4,28},{8,16},{12,20},{16,8},{20,12},{24,0},{28,4},{1,25},{... | collective-permute-start | bytes 331784 | tf_op jit(solution)/shard_map/ppermute | solution.py:635
  29.8 6.8 %collective-permute-start.8 = (bf16[432,128]{1,0:T(8,128)(2,1)S(1)}, bf16[432,128]{1,0:T(8,128)(2,1)S(1)}, u32[]{:S(2)}, u32[]{:S(2)}) collective-permute-start(bf16[432,128]{1,0:T(8,128)(2,1)S(1)} %get-tuple-element.47), channel_id=1, source_target_pairs={{0,8},{4,12},{8,0},{12,4},{16,24},{20,28},{24,16},{28,20},{1,9},{5... | collective-permute-start | bytes 331784 | tf_op jit(solution)/shard_map/ppermute | solution.py:635
  30.3 6.4 %collective-permute-start.9 = (bf16[432,128]{1,0:T(8,128)(2,1)S(1)}, bf16[432,128]{1,0:T(8,128)(2,1)S(1)}, u32[]{:S(2)}, u32[]{:S(2)}) collective-permute-start(bf16[432,128]{1,0:T(8,128)(2,1)S(1)} %get-tuple-element.48), channel_id=1, source_target_pairs={{0,20},{4,16},{8,28},{12,24},{16,4},{20,0},{24,12},{28,8},{1,21},{... | collective-permute-start | bytes 331784 | tf_op jit(solution)/shard_map/ppermute | solution.py:635
  30.7 8.3 %collective-permute-start.10 = (bf16[432,128]{1,0:T(8,128)(2,1)S(1)}, bf16[432,128]{1,0:T(8,128)(2,1)S(1)}, u32[]{:S(2)}, u32[]{:S(2)}) collective-permute-start(bf16[432,128]{1,0:T(8,128)(2,1)S(1)} %get-tuple-element.49), channel_id=1, source_target_pairs={{0,12},{4,8},{8,4},{12,0},{16,28},{20,24},{24,20},{28,16},{1,13},{... | collective-permute-start | bytes 331784 | tf_op jit(solution)/shard_map/ppermute | solution.py:635
  32.0 8.8 %collective-permute-start.11 = (bf16[432,128]{1,0:T(8,128)(2,1)S(1)}, bf16[432,128]{1,0:T(8,128)(2,1)S(1)}, u32[]{:S(2)}, u32[]{:S(2)}) collective-permute-start(bf16[432,128]{1,0:T(8,128)(2,1)S(1)} %get-tuple-element.50), channel_id=1, source_target_pairs={{0,28},{4,24},{8,20},{12,16},{16,12},{20,8},{24,4},{28,0},{1,29},{... | collective-permute-start | bytes 331784 | tf_op jit(solution)/shard_map/ppermute | solution.py:635
  34.3 7.1 %collective-permute-start.12 = (bf16[432,128]{1,0:T(8,128)(2,1)S(1)}, bf16[432,128]{1,0:T(8,128)(2,1)S(1)}, u32[]{:S(2)}, u32[]{:S(2)}) collective-permute-start(bf16[432,128]{1,0:T(8,128)(2,1)S(1)} %get-tuple-element.51), channel_id=1, source_target_pairs={{0,16},{4,20},{8,24},{12,28},{16,0},{20,4},{24,8},{28,12},{1,17},{... | collective-permute-start | bytes 331784 | tf_op jit(solution)/shard_map/ppermute | solution.py:635
  36.6 4.8 %collective-permute-start.13 = (bf16[432,128]{1,0:T(8,128)(2,1)S(1)}, bf16[432,128]{1,0:T(8,128)(2,1)S(1)}, u32[]{:S(2)}, u32[]{:S(2)}) collective-permute-start(bf16[432,128]{1,0:T(8,128)(2,1)S(1)} %get-tuple-element.52), channel_id=1, source_target_pairs={{0,4},{4,0},{8,12},{12,8},{16,20},{20,16},{24,28},{28,24},{1,5},{5... | collective-permute-start | bytes 331784 | tf_op jit(solution)/shard_map/ppermute | solution.py:635

commit v4 on v3

--- a/solution.py
+++ b/solution.py
@@ -205,8 +205,9 @@
 LANES = 128
 PAD = 8
 CHUNK = 16
-PLACES = (0, 6, 2, 5, 3, 7, 4, 1)
-EARLY = 4
+SENT = (0, 6, 2, 5, 3, 4, 7, 1)
+BACK = (0, 6, 2, 5, 3, 4, 7, 1)
+FINISHED = (0, 4, 6, 8)
 CURVE = 15.0
 REACH = 120.0
 SLOPE = 2.0 * REACH / math.log2(1.0 + CURVE)
@@ -384,7 +385,7 @@
 def widen(me_ref, got, targets, rows):
     def body(step, carry):
         b0 = pl.multiple_of(step * CHUNK, CHUNK)
-        for k, ref in zip(PLACES, got):
+        for k, ref in zip(SENT, got):
             at = pl.multiple_of((me_ref[0] ^ k) * rows + b0, CHUNK)
             for field, (target, pad) in enumerate(targets):
                 target[pl.ds(pad + at, CHUNK), :] = ref[pl.ds(field * rows + b0, CHUNK), :].astype(
@@ -392,7 +393,7 @@
                 )
         return carry
 
-    lax.fori_loop(0, rows // CHUNK, body, 0)
+    lax.fori_loop(0, rows // CHUNK, body, 0, unroll=8)
 
 
 def gains(taps_ref):
@@ -401,7 +402,7 @@
 
 def layer_kernel(me_ref, gain_ref, turn, forward_ref, inverse_ref, *refs):
     got, outs = refs[:RADIX], refs[RADIX : 2 * RADIX]
-    qp, kp, vp, hs, cot, ks, vs, xs, zs, conv, mgrad, fgrad, peak, sums, head = refs[2 * RADIX :]
+    qp, kp, vp, hs, cot, ks, vs, xs, xs_grad, spec, spec_grad, ys_conv, ys, zs_conv, zs, conv, mgrad, fgrad, peak, sums, head = refs[2 * RADIX :]
     rows = got[0].shape[0] // FIELDS
     total = RADIX * rows
     f32 = jnp.float32
@@ -412,8 +413,9 @@
         ref[pl.ds(total, PAD), :] = jnp.zeros((PAD, LANES), f32)
     widen(me_ref, got, ((qp, PAD), (kp, PAD), (vp, PAD), (hs, 0), (cot, 0)), rows)
 
-    def enter(step, carry):
-        b0 = pl.multiple_of(step * CHUNK, CHUNK)
+    chunks = range(0, rows, CHUNK)
+    classes = range(xs.shape[0])
+    for b0 in chunks:
         mixed = []
         for a in range(RADIX):
             at = a * rows + b0
@@ -422,68 +424,61 @@
             ks[pl.ds(at, CHUNK), :] = key_filt
             vs[pl.ds(at, CHUNK), :] = value_filt
             mixed.append(key_filt * value_filt)
-        put_classes(xs, 0, 3, rows, b0, mixed, turn)
+        put_classes(xs, 0, 2, rows, b0, mixed, turn)
         filt = [hs[pl.ds(a * rows + b0, CHUNK), :] for a in range(RADIX)]
-        put_classes(xs, 1, 3, rows, b0, filt, turn)
+        put_classes(xs, 1, 2, rows, b0, filt, turn)
+    for f, b0 in zip(classes, chunks):
+        spec[f] = table_dot(forward_ref, f, xs[f])
         conv_grad = []
         for a in range(RADIX):
             at = a * rows + b0
             conv_grad.append(short_filter(gain[0], qp, PAD + at) * cot[pl.ds(at, CHUNK), :])
-        put_classes(xs, 2, 3, rows, b0, conv_grad, turn)
-        return carry
-
-    lax.fori_loop(0, rows // CHUNK, enter, 0)
-    for f in range(xs.shape[0]):
-        zs[f] = table_dot(forward_ref, f, xs[f])
-    for f in range(xs.shape[0]):
-        mixed, filt, grad = [spec_parts(zs[f], rows, c) for c in range(3)]
-        products = [
-            times_spec(mixed, filt, False, f == 0),
-            times_spec(grad, filt, True, f == 0),
-            times_spec(grad, mixed, True, f == 0),
-        ]
-        xs[f] = side_by_side(products)
-    for f in range(xs.shape[0]):
-        zs[f] = table_dot(inverse_ref, f, xs[f])
+        put_classes(xs_grad, 0, 1, rows, b0, conv_grad, turn)
+    for f in classes:
+        spec_grad[f] = table_dot(forward_ref, f, xs_grad[f])
+        mixed, filt = [spec_parts(spec[f], rows, c) for c in range(2)]
+        ys_conv[f] = side_by_side([times_spec(mixed, filt, False, f == 0)])
+    for f in classes:
+        zs_conv[f] = table_dot(inverse_ref, f, ys_conv[f])
+        mixed, filt = [spec_parts(spec[f], rows, c) for c in range(2)]
+        grad = spec_parts(spec_grad[f], rows, 0)
+        ys[f] = side_by_side([times_spec(grad, one, True, f == 0) for one in (filt, mixed)])
     peak[...] = jnp.zeros_like(peak)
     sums[...] = jnp.zeros_like(sums)
 
-    def leave(step, carry):
-        b0 = pl.multiple_of(step * CHUNK, CHUNK)
-
-        def take(column, ref):
-            found = take_classes(zs, column, rows, b0, turn)
-            for a, value in enumerate(found):
-                ref[pl.ds(a * rows + b0, CHUNK), :] = value
-                size = jnp.abs(value)
-                peak[column, a] = jnp.maximum(peak[column, a], jnp.maximum(size[:8], size[8:]))
-            return found
-
-        def add(i, source, values, other):
-            found = [jnp.zeros((CHUNK, LANES), f32)] * 3
-            for a, value in enumerate(values):
-                at = a * rows + b0
-                now = value * other[pl.ds(at, CHUNK), :]
-                for j in range(3):
-                    found[j] = found[j] + now * source[pl.ds(PAD + at - j, CHUNK), :]
+    def take(column, b0, ref, source, place):
+        found = take_classes(source, place, rows, b0, turn)
+        for a, value in enumerate(found):
+            ref[pl.ds(a * rows + b0, CHUNK), :] = value
+            size = jnp.abs(value)
+            peak[column, a] = jnp.maximum(peak[column, a], jnp.maximum(size[:8], size[8:]))
+        return found
+
+    def add(i, b0, source, values, other):
+        found = [jnp.zeros((CHUNK, LANES), f32)] * 3
+        for a, value in enumerate(values):
+            at = a * rows + b0
+            now = value * other[pl.ds(at, CHUNK), :]
             for j in range(3):
-                sums[3 * i + j] += found[j][:8] + found[j][8:]
-
-        add(0, qp, take(0, conv), cot)
-        found = take(1, mgrad)
-        add(1, kp, found, vs)
-        add(2, vp, found, ks)
-        take(2, fgrad)
-        return carry
-
-    lax.fori_loop(0, rows // CHUNK, leave, 0)
+                found[j] = found[j] + now * source[pl.ds(PAD + at - j, CHUNK), :]
+        for j in range(3):
+            sums[3 * i + j] += found[j][:8] + found[j][8:]
+
+    for f, b0 in zip(classes, chunks):
+        zs[f] = table_dot(inverse_ref, f, ys[f])
+        add(0, b0, qp, take(0, b0, conv, zs_conv, 0), cot)
+    for b0 in chunks:
+        found = take(1, b0, mgrad, zs, 0)
+        add(1, b0, kp, found, vs)
+        add(2, b0, vp, found, ks)
+        take(2, b0, fgrad, zs, 1)
     grad_scale = 1.0 / math.sqrt(total)
     head[...] = jnp.zeros_like(head)
     for n in range(9):
         at = 32 + n if n < 8 else 22
         head[pl.ds(at, 1), :] = jnp.sum(sums[n], axis=0, keepdims=True) * grad_scale
     head[pl.ds(40, 8), :] = split_pair(head[pl.ds(32, 8), :])[1].astype(f32)
-    for k, out_ref in zip(PLACES, outs):
+    for k, out_ref in zip(BACK, outs):
         a = me_ref[0] ^ k
         first = pl.multiple_of(a * rows, rows)
         after = first + rows
@@ -555,7 +550,7 @@
             out_ref[pl.ds(field * rows, rows), :] = land[field, :, pl.ds(lane, LANES)]
 
 
-def finish_blocks(me_ref, places, got, wide_ref, early_ref, outs, grads, stage, stage_filter, sem):
+def finish_blocks(me_ref, places, got, wide_ref, early_ref, outs, grads, stage, stage_filter, stage_taps, sem):
     rows = early_ref.shape[1]
     f32, bf16 = jnp.float32, jnp.bfloat16
     copies = []
@@ -567,6 +562,9 @@
         ]
         stage_filter[n] = filt * (1.0 / math.sqrt(RADIX * rows))
         pairs = head[16:24] + head[24:32]
+        taps = head[32:40] + head[40:48]
+        for c in range(9):
+            stage_taps[n, c // 3, c % 3 : c % 3 + 1, :] = taps[c : c + 1] if c < 8 else pairs[6:7]
         line = lax.broadcasted_iota(jnp.int32, (PAD, LANES), 0)
         filtered = []
         gain = []
@@ -594,46 +592,25 @@
                 + gain[i][2] * grads[i, pl.ds(2, rows), :]
             ).astype(bf16)
         for c, out in enumerate(outs):
-            source = stage.at[n, c] if c < 4 else stage_filter.at[n]
-            copies.append(pltpu.make_async_copy(source, out.at[:, lanes], sem.at[len(copies)]))
+            source = stage.at[n, c] if c < 4 else (stage_filter, stage_taps)[c - 4].at[n]
+            target = out.at[:, lanes] if c < 5 else out.at[:, :, lanes]
+            copies.append(pltpu.make_async_copy(source, target, sem.at[len(copies)]))
             copies[-1].start()
     return copies
 
 
-def finish_kernel(me_ref, *refs):
-    got, (wide_ref, early_ref), outs, scratch = refs[:EARLY], refs[EARLY : EARLY + 2], refs[EARLY + 2 : EARLY + 7], refs[EARLY + 7 :]
-    for copy in finish_blocks(me_ref, PLACES[:EARLY], got, wide_ref, early_ref, outs, *scratch):
+def finish_kernel(places, begun, me_ref, *refs):
+    count = len(places)
+    got, (wide_ref, early_ref), refs = refs[:count], refs[count : count + 2], refs[count + 2 + begun :]
+    for copy in finish_blocks(me_ref, places, got, wide_ref, early_ref, refs[:6], *refs[6:]):
         copy.wait()
 
 
-def finish_last_kernel(me_ref, *refs):
-    got, (wide_ref, early_ref), outs, taps_grad, scratch = (
-        refs[:RADIX],
-        refs[RADIX : RADIX + 2],
-        refs[RADIX + 7 : RADIX + 12],
-        refs[RADIX + 12],
-        refs[RADIX + 13 :],
-    )
-    rows = early_ref.shape[1]
-    copies = finish_blocks(
-        me_ref, PLACES[EARLY:], got[EARLY:], wide_ref, early_ref, outs, *scratch
-    )
-    for k, got_ref in zip(PLACES, got):
-        lanes = pl.ds(pl.multiple_of((me_ref[0] ^ k) * LANES, LANES), LANES)
-        head = got_ref[pl.ds(3 * rows, 48), :].astype(jnp.float32)
-        taps = head[32:40] + head[40:48]
-        for n in range(8):
-            taps_grad[n // 3, n % 3 : n % 3 + 1, lanes] = taps[n : n + 1]
-        taps_grad[2, 2:3, lanes] = head[22:23] + head[30:31]
-    for copy in copies:
-        copy.wait()
-
-
-def swap_blocks(blocks):
+def swap_blocks(places, blocks):
     devices = range(RADIX)
     return [
         lax.ppermute(block, "ctx", [(i, i ^ k) for i in devices]) if k else block
-        for k, block in zip(PLACES, blocks)
+        for k, block in zip(places, blocks)
     ]
 
 
@@ -665,8 +642,8 @@
             name="pack",
         )(me, *sources)
 
-    packed = pack(PLACES)
-    got = swap_blocks(packed)
+    packed = pack(SENT)
+    got = swap_blocks(SENT, packed)
     forward, inverse, turns = class_tables(rows)
     count = 1 + len(CLASSES)
     ready = pl.pallas_call(
@@ -693,8 +670,10 @@
         out_specs=whole_vmem(RADIX),
         scratch_shapes=[pltpu.VMEM((total + PAD, LANES), f32)] * 7
         + [
-            pltpu.VMEM((count, 2 * rows, 6 * LANES), bf16),
-            pltpu.VMEM((count, 2 * rows, 3 * LANES), f32),
+            pltpu.VMEM((count, 2 * rows, columns * LANES), kind)
+            for columns, kind in (
+                (4, bf16), (2, bf16), (2, f32), (1, f32), (2, bf16), (4, bf16), (1, f32), (2, f32)
+            )
         ]
         + [pltpu.VMEM((total + PAD, LANES), f32)] * 3
         + [
@@ -705,38 +684,32 @@
         compiler_params=pltpu.CompilerParams(vmem_limit_bytes=20 * 1024 * 1024),
         name="layer",
     )(me, ready[3], *ready[:3], *held(got, pltpu.VMEM))
-    back = held(swap_blocks(done), pltpu.VMEM)
-    results = [shape((rows, channels), bf16)] * 4 + [shape((rows, channels), f32)]
-
-    def finish_scratch(count):
-        return [
-            pltpu.VMEM((3, rows + PAD, LANES), f32),
-            pltpu.VMEM((count, 4, rows, LANES), bf16),
-            pltpu.VMEM((count, rows, LANES), f32),
-            pltpu.SemaphoreType.DMA((5 * count,)),
-        ]
-
-    begun = pl.pallas_call(
-        finish_kernel,
-        out_shape=results,
-        in_specs=[IN_SMEM] + whole_vmem(EARLY + 2),
-        out_specs=whole_any(5),
-        scratch_shapes=finish_scratch(EARLY),
-        compiler_params=small,
-        name="finish",
-    )(me, *back[:EARLY], *ready[4:])
-    return tuple(
-        pl.pallas_call(
-            finish_last_kernel,
-            out_shape=results + [shape((3, 3, channels), f32)],
-            in_specs=[IN_SMEM] + whole_vmem(RADIX + 2) + whole_any(5),
-            out_specs=whole_any(5) + whole_vmem(1),
-            scratch_shapes=finish_scratch(RADIX - EARLY),
-            input_output_aliases={RADIX + 3 + n: n for n in range(5)},
+    back = held(swap_blocks(BACK, done), pltpu.VMEM)
+    results = [shape((rows, channels), bf16)] * 4 + [
+        shape((rows, channels), f32),
+        shape((3, 3, channels), f32),
+    ]
+
+    begun = []
+    for first, last in zip(FINISHED, FINISHED[1:]):
+        count = last - first
+        begun = pl.pallas_call(
+            partial(finish_kernel, BACK[first:last], len(begun)),
+            out_shape=results,
+            in_specs=[IN_SMEM] + whole_vmem(count + 2) + whole_any(len(begun)),
+            out_specs=whole_any(6),
+            scratch_shapes=[
+                pltpu.VMEM((3, rows + PAD, LANES), f32),
+                pltpu.VMEM((count, 4, rows, LANES), bf16),
+                pltpu.VMEM((count, rows, LANES), f32),
+                pltpu.VMEM((count, 3, 3, LANES), f32),
+                pltpu.SemaphoreType.DMA((6 * count,)),
+            ],
+            input_output_aliases={count + 3 + n: n for n in range(len(begun))},
             compiler_params=small,
-            name="finish_last",
-        )(me, *back, *ready[4:], *begun)
-    )
+            name="finish",
+        )(me, *back[first:last], *ready[4:], *begun)
+    return tuple(begun)
 
 
 def local(query_in, key_in, value_in, long_filter, short_taps, out_grad):

time: 43.7 us -> 40.8 us (0.934)
  waiting for transfers between devices: 10 us -> 8.58 us
  Pallas kernels: 15.2 us -> 14 us
    ppermute x14, waiting for transfers between devices: 10 us -> 8.58 us  [swap_blocks(): lax.ppermute(block, 'ctx', [(i, i ^ k) for i in devices])]
    pallas_call x1, Pallas kernels: 7.49 us -> 6.16 us  [local_fast(): pl.pallas_call(layer_kernel, out_shape=[pltpu.VMEM((3 * rows + 48, LANES)...]
    pallas_call x2 -> x3, Pallas kernels: 3.56 us -> 3.72 us  [local_fast(): pl.pallas_call(partial(finish_kernel, BACK[first:last], len(begun)), out_...]
  transfers between devices with their start and end apart: 14 -> 14, of which waited for: 8 -> 8; matrix products, arithmetic and copies ran while one was open for 0% -> 0% of each run, Pallas kernels for 10% -> 13%
where the time goes in v4:
time: 40.8 us; the launch traced here: 40.5 us
  starting transfers between devices  16.5 us (40%)
  Pallas kernels  14 us (34%)
  waiting for transfers between devices  8.58 us (21%)
  local copies, waits for them, and re-layouts  0.74 us (2%)
  between operations  0.71 us (2%)
    ppermute x14, starting transfers between devices, swap_blocks(): lax.ppermute(block, 'ctx', [(i, i ^ k) for i in devices])  16.5 us
    ppermute x14, waiting for transfers between devices, swap_blocks(): lax.ppermute(block, 'ctx', [(i, i ^ k) for i in devices])  8.58 us
    pallas_call x1, Pallas kernels, local_fast(): pl.pallas_call(layer_kernel, out_shape=[pltpu.VMEM((3 * rows + 48, LANES)...  6.16 us
    pallas_call x3, Pallas kernels, local_fast(): pl.pallas_call(partial(finish_kernel, BACK[first:last], len(begun)), out_...  3.72 us
    pallas_call x1, Pallas kernels, local_fast(): pl.pallas_call(prepare_kernel, out_shape=[pltpu.VMEM((2 * len(CLASSES), r...  2.76 us
    pallas_call x1, Pallas kernels, pack(): pl.pallas_call(partial(pack_kernel, places), out_shape=[pltpu.VMEM((FIELD...  1.38 us
  transfers between devices with their start and end apart: 14, of which 8 were waited for; matrix products, arithmetic and copies ran while one was open for 0% of the time, Pallas kernels for 13%

profile of v4, /device:TPU:0, one launch (start us, length us, event | category | flops | bytes accessed | tf_op | source)
XLA Modules:
  0.0 40.5 jit_solution(13826345523131341823)
XLA Ops:
  0.6 1.4 %pack.1 = (bf16[640,128]{1,0:T(8,128)(2,1)S(1)}, bf16[640,128]{1,0:T(8,128)(2,1)S(1)}, bf16[640,128]{1,0:T(8,128)(2,1)S(1)}, bf16[640,128]{1,0:T(8,128)(2,1)S(1)...) custom-call(s32[1]{0:T(128)} %bitcast.me_ref, ...), custom_call_target="tpu_custom_call" | custom-call | tf_op jit(solution)/shard_map/pack/pallas_call | solution.py:632
  2.0 4.0 %collective-permute-start = (bf16[640,128]{1,0:T(8,128)(2,1)S(1)}, bf16[640,128]{1,0:T(8,128)(2,1)S(1)}, u32[]{:S(2)}, u32[]{:S(2)}) collective-permute-start(bf16[640,128]{1,0:T(8,128)(2,1)S(1)} %get-tuple-element.40), channel_id=1, source_target_pairs={{0,24},{4,28},{8,16},{12,20},{16,8},{20,12},{24,0},{28,4},{1,25},{... | collective-permute-start | bytes 491528 | tf_op jit(solution)/shard_map/ppermute | solution.py:612
  6.0 0.5 %collective-permute-start.1 = (bf16[640,128]{1,0:T(8,128)(2,1)S(1)}, bf16[640,128]{1,0:T(8,128)(2,1)S(1)}, u32[]{:S(2)}, u32[]{:S(2)}) collective-permute-start(bf16[640,128]{1,0:T(8,128)(2,1)S(1)} %get-tuple-element.46), channel_id=1, source_target_pairs={{0,8},{4,12},{8,0},{12,4},{16,24},{20,28},{24,16},{28,20},{1,9},{5... | collective-permute-start | bytes 491528 | tf_op jit(solution)/shard_map/ppermute | solution.py:612
  6.5 1.7 %collective-permute-start.3 = (bf16[640,128]{1,0:T(8,128)(2,1)S(1)}, bf16[640,128]{1,0:T(8,128)(2,1)S(1)}, u32[]{:S(2)}, u32[]{:S(2)}) collective-permute-start(bf16[640,128]{1,0:T(8,128)(2,1)S(1)} %get-tuple-element.48), channel_id=1, source_target_pairs={{0,12},{4,8},{8,4},{12,0},{16,28},{20,24},{24,20},{28,16},{1,13},{... | collective-permute-start | bytes 491528 | tf_op jit(solution)/shard_map/ppermute | solution.py:612
  8.2 1.5 %collective-permute-start.4 = (bf16[640,128]{1,0:T(8,128)(2,1)S(1)}, bf16[640,128]{1,0:T(8,128)(2,1)S(1)}, u32[]{:S(2)}, u32[]{:S(2)}) collective-permute-start(bf16[640,128]{1,0:T(8,128)(2,1)S(1)} %get-tuple-element.49), channel_id=1, source_target_pairs={{0,16},{4,20},{8,24},{12,28},{16,0},{20,4},{24,8},{28,12},{1,17},{... | collective-permute-start | bytes 491528 | tf_op jit(solution)/shard_map/ppermute | solution.py:612
  9.8 1.3 %collective-permute-done._.refs_1_ = bf16[640,128]{1,0:T(8,128)(2,1)S(1)} collective-permute-done((bf16[640,128]{1,0:T(8,128)(2,1)S(1)}, bf16[640,128]{1,0:T(8,128)(2,1)S(1)}, u32[]{:S(2)}, u32[]{:S(2)}) %collective-permute-start) | collective-permute-done | bytes 163872 | tf_op jit(solution)/shard_map/ppermute | solution.py:612
  11.0 0.4 collective-permute-start.5
  11.4 3.7 %collective-permute-done.1.refs_2_ = bf16[640,128]{1,0:T(8,128)(2,1)S(1)} collective-permute-done((bf16[640,128]{1,0:T(8,128)(2,1)S(1)}, bf16[640,128]{1,0:T(8,128)(2,1)S(1)}, u32[]{:S(2)}, u32[]{:S(2)}) %collective-permute-start.1) | collective-permute-done | bytes 163872 | tf_op jit(solution)/shard_map/ppermute | solution.py:612
  15.1 0.7 %copy-done = bf16[3,3,1024]{2,1,0:T(4,128)(2,1)S(1)} copy-done((bf16[3,3,1024]{2,1,0:T(4,128)(2,1)S(1)}, bf16[3,3,1024]{2,1,0:T(4,128)(2,1)}, u32[]{:S(2)}) %copy-start) | copy-done | bytes 18456
  15.8 2.8 %prepare.1 = (f32[14,128,128]{2,1,0:T(8,128)S(1)}, bf16[2,2,256,256]{3,2,1,0:T(8,128)(2,1)S(1)}, bf16[2,2,256,256]{3,2,1,0:T(8,128)(2,1)S(1)}, f32[16,128]{1,0:T...) custom-call(s32[1]{0:T(128)} %bitcast.me_ref, f32[128,128]{1,0:T(8,128)} %constant.12.clone.turns_ref, ...), custom_call_target="tpu_custom_call" | custom-call | tf_op jit(solution)/shard_map/prepare/pallas_call | solution.py:649
  18.6 1.3 %collective-permute-done.5.refs_6_ = bf16[640,128]{1,0:T(8,128)(2,1)S(1)} collective-permute-done((bf16[640,128]{1,0:T(8,128)(2,1)S(1)}, bf16[640,128]{1,0:T(8,128)(2,1)S(1)}, u32[]{:S(2)}, u32[]{:S(2)}) %collective-permute-start.5) | collective-permute-done | bytes 163872 | tf_op jit(solution)/shard_map/ppermute | solution.py:612
  20.0 6.2 %layer.1 = (bf16[432,128]{1,0:T(8,128)(2,1)S(1)}, bf16[432,128]{1,0:T(8,128)(2,1)S(1)}, bf16[432,128]{1,0:T(8,128)(2,1)S(1)}, bf16[432,128]{1,0:T(8,128)(2,1)S(1...) custom-call(s32[1]{0:T(128)} %bitcast.me_ref, ...), custom_call_target="tpu_custom_call" | custom-call | tf_op jit(solution)/shard_map/layer/pallas_call | solution.py:666
  26.1 2.3 %collective-permute-start.11 = (bf16[432,128]{1,0:T(8,128)(2,1)S(1)}, bf16[432,128]{1,0:T(8,128)(2,1)S(1)}, u32[]{:S(2)}, u32[]{:S(2)}) collective-permute-start(bf16[432,128]{1,0:T(8,128)(2,1)S(1)} %get-tuple-element.59), channel_id=1, source_target_pairs={{0,24},{4,28},{8,16},{12,20},{16,8},{20,12},{24,0},{28,4},{1,25},{... | collective-permute-start | bytes 331784 | tf_op jit(solution)/shard_map/ppermute | solution.py:612
  28.4 0.5 %collective-permute-start.12 = (bf16[432,128]{1,0:T(8,128)(2,1)S(1)}, bf16[432,128]{1,0:T(8,128)(2,1)S(1)}, u32[]{:S(2)}, u32[]{:S(2)}) collective-permute-start(bf16[432,128]{1,0:T(8,128)(2,1)S(1)} %get-tuple-element.60), channel_id=1, source_target_pairs={{0,8},{4,12},{8,0},{12,4},{16,24},{20,28},{24,16},{28,20},{1,9},{5... | collective-permute-start | bytes 331784 | tf_op jit(solution)/shard_map/ppermute | solution.py:612
  29.0 0.4 collective-permute-start.13
  29.4 1.3 %collective-permute-start.9 = (bf16[432,128]{1,0:T(8,128)(2,1)S(1)}, bf16[432,128]{1,0:T(8,128)(2,1)S(1)}, u32[]{:S(2)}, u32[]{:S(2)}) collective-permute-start(bf16[432,128]{1,0:T(8,128)(2,1)S(1)} %get-tuple-element.56), channel_id=1, source_target_pairs={{0,12},{4,8},{8,4},{12,0},{16,28},{20,24},{24,20},{28,16},{1,13},{... | collective-permute-start | bytes 331784 | tf_op jit(solution)/shard_map/ppermute | solution.py:612
  30.7 1.5 %collective-permute-start.10 = (bf16[432,128]{1,0:T(8,128)(2,1)S(1)}, bf16[432,128]{1,0:T(8,128)(2,1)S(1)}, u32[]{:S(2)}, u32[]{:S(2)}) collective-permute-start(bf16[432,128]{1,0:T(8,128)(2,1)S(1)} %get-tuple-element.57), channel_id=1, source_target_pairs={{0,16},{4,20},{8,24},{12,28},{16,0},{20,4},{24,8},{28,12},{1,17},{... | collective-permute-start | bytes 331784 | tf_op jit(solution)/shard_map/ppermute | solution.py:612
  32.2 0.7 %collective-permute-done.11.refs_1_ = bf16[432,128]{1,0:T(8,128)(2,1)S(1)} collective-permute-done((bf16[432,128]{1,0:T(8,128)(2,1)S(1)}, bf16[432,128]{1,0:T(8,128)(2,1)S(1)}, u32[]{:S(2)}, u32[]{:S(2)}) %collective-permute-start.11) | collective-permute-done | bytes 110624 | tf_op jit(solution)/shard_map/ppermute | solution.py:612
  33.0 2.1 %collective-permute-start.7 = (bf16[432,128]{1,0:T(8,128)(2,1)S(1)}, bf16[432,128]{1,0:T(8,128)(2,1)S(1)}, u32[]{:S(2)}, u32[]{:S(2)}) collective-permute-start(bf16[432,128]{1,0:T(8,128)(2,1)S(1)} %get-tuple-element.52), channel_id=1, source_target_pairs={{0,28},{4,24},{8,20},{12,16},{16,12},{20,8},{24,4},{28,0},{1,29},{... | collective-permute-start | bytes 331784 | tf_op jit(solution)/shard_map/ppermute | solution.py:612
  35.5 1.5 %finish.3 = (bf16[128,1024]{1,0:T(8,128)(2,1)}, bf16[128,1024]{1,0:T(8,128)(2,1)}, bf16[128,1024]{1,0:T(8,128)(2,1)}, bf16[128,1024]{1,0:T(8,128)(2,1)}, f32[128,1024]{1,0:T(8,128)}, /*index=5*/f32[3,3,1024]{2,1,0:T(4,128)}) custom-call(s32[1]{0:T(128)} %bitcast.me_ref, bf16[432,128]{1,0:T(8,128)(2,1)S(1)} %get-tuple-element.58.refs_0_, ...), custom_call_target="tpu_custom_call" | custom-call | tf_op jit(solution)/shard_map/finish/pallas_call | solution.py:696
  37.0 0.6 %collective-permute-done.9.refs_0_ = bf16[432,128]{1,0:T(8,128)(2,1)S(1)} collective-permute-done((bf16[432,128]{1,0:T(8,128)(2,1)S(1)}, bf16[432,128]{1,0:T(8,128)(2,1)S(1)}, u32[]{:S(2)}, u32[]{:S(2)}) %collective-permute-start.9) | collective-permute-done | bytes 110624 | tf_op jit(solution)/shard_map/ppermute | solution.py:612
  37.7 1.1 %finish.4 = (bf16[128,1024]{1,0:T(8,128)(2,1)}, bf16[128,1024]{1,0:T(8,128)(2,1)}, bf16[128,1024]{1,0:T(8,128)(2,1)}, bf16[128,1024]{1,0:T(8,128)(2,1)}, f32[128,1024]{1,0:T(8,128)}, /*index=5*/f32[3,3,1024]{2,1,0:T(4,128)}) custom-call(s32[1]{0:T(128)} %bitcast.me_ref, ...), custom_call_target="tpu_custom_call", output_to_operand_aliasing={{0}: (5, {}), {1}: (6, {}), {2}: (7, {}), {3}: (8, {}), {4}... | custom-call | tf_op jit(solution)/shard_map/finish/pallas_call | solution.py:696
  38.8 0.6 %collective-permute-done.7.refs_0_ = bf16[432,128]{1,0:T(8,128)(2,1)S(1)} collective-permute-done((bf16[432,128]{1,0:T(8,128)(2,1)S(1)}, bf16[432,128]{1,0:T(8,128)(2,1)S(1)}, u32[]{:S(2)}, u32[]{:S(2)}) %collective-permute-start.7) | collective-permute-done | bytes 110624 | tf_op jit(solution)/shard_map/ppermute | solution.py:612
  39.4 1.1 %finish.5 = (bf16[128,1024]{1,0:T(8,128)(2,1)}, bf16[128,1024]{1,0:T(8,128)(2,1)}, bf16[128,1024]{1,0:T(8,128)(2,1)}, bf16[128,1024]{1,0:T(8,128)(2,1)}, f32[128,1024]{1,0:T(8,128)}, /*index=5*/f32[3,3,1024]{2,1,0:T(4,128)}) custom-call(s32[1]{0:T(128)} %bitcast.me_ref, ...), custom_call_target="tpu_custom_call", output_to_operand_aliasing={{0}: (5, {}), {1}: (6, {}), {2}: (7, {}), {3}: (8, {}), {4}... | custom-call | tf_op jit(solution)/shard_map/finish/pallas_call | solution.py:696
  (12 shorter events, 0.5 us)
Async XLA Ops:
  2.0 9.0 %collective-permute-start = (bf16[640,128]{1,0:T(8,128)(2,1)S(1)}, bf16[640,128]{1,0:T(8,128)(2,1)S(1)}, u32[]{:S(2)}, u32[]{:S(2)}) collective-permute-start(bf16[640,128]{1,0:T(8,128)(2,1)S(1)} %get-tuple-element.40), channel_id=1, source_target_pairs={{0,24},{4,28},{8,16},{12,20},{16,8},{20,12},{24,0},{28,4},{1,25},{... | collective-permute-start | bytes 491528 | tf_op jit(solution)/shard_map/ppermute | solution.py:612
  6.0 9.1 %collective-permute-start.1 = (bf16[640,128]{1,0:T(8,128)(2,1)S(1)}, bf16[640,128]{1,0:T(8,128)(2,1)S(1)}, u32[]{:S(2)}, u32[]{:S(2)}) collective-permute-start(bf16[640,128]{1,0:T(8,128)(2,1)S(1)} %get-tuple-element.46), channel_id=1, source_target_pairs={{0,8},{4,12},{8,0},{12,4},{16,24},{20,28},{24,16},{28,20},{1,9},{5... | collective-permute-start | bytes 491528 | tf_op jit(solution)/shard_map/ppermute | solution.py:612
  6.5 12.1 %collective-permute-start.2 = (bf16[640,128]{1,0:T(8,128)(2,1)S(1)}, bf16[640,128]{1,0:T(8,128)(2,1)S(1)}, u32[]{:S(2)}, u32[]{:S(2)}) collective-permute-start(bf16[640,128]{1,0:T(8,128)(2,1)S(1)} %get-tuple-element.47), channel_id=1, source_target_pairs={{0,20},{4,16},{8,28},{12,24},{16,4},{20,0},{24,12},{28,8},{1,21},{... | collective-permute-start | bytes 491528 | tf_op jit(solution)/shard_map/ppermute | solution.py:612
  6.5 12.1 %collective-permute-start.3 = (bf16[640,128]{1,0:T(8,128)(2,1)S(1)}, bf16[640,128]{1,0:T(8,128)(2,1)S(1)}, u32[]{:S(2)}, u32[]{:S(2)}) collective-permute-start(bf16[640,128]{1,0:T(8,128)(2,1)S(1)} %get-tuple-element.48), channel_id=1, source_target_pairs={{0,12},{4,8},{8,4},{12,0},{16,28},{20,24},{24,20},{28,16},{1,13},{... | collective-permute-start | bytes 491528 | tf_op jit(solution)/shard_map/ppermute | solution.py:612
  8.2 10.4 %collective-permute-start.4 = (bf16[640,128]{1,0:T(8,128)(2,1)S(1)}, bf16[640,128]{1,0:T(8,128)(2,1)S(1)}, u32[]{:S(2)}, u32[]{:S(2)}) collective-permute-start(bf16[640,128]{1,0:T(8,128)(2,1)S(1)} %get-tuple-element.49), channel_id=1, source_target_pairs={{0,16},{4,20},{8,24},{12,28},{16,0},{20,4},{24,8},{28,12},{1,17},{... | collective-permute-start | bytes 491528 | tf_op jit(solution)/shard_map/ppermute | solution.py:612
  11.0 9.0 %collective-permute-start.5 = (bf16[640,128]{1,0:T(8,128)(2,1)S(1)}, bf16[640,128]{1,0:T(8,128)(2,1)S(1)}, u32[]{:S(2)}, u32[]{:S(2)}) collective-permute-start(bf16[640,128]{1,0:T(8,128)(2,1)S(1)} %get-tuple-element.50), channel_id=1, source_target_pairs={{0,28},{4,24},{8,20},{12,16},{16,12},{20,8},{24,4},{28,0},{1,29},{... | collective-permute-start | bytes 491528 | tf_op jit(solution)/shard_map/ppermute | solution.py:612
  15.1 4.9 %collective-permute-start.6 = (bf16[640,128]{1,0:T(8,128)(2,1)S(1)}, bf16[640,128]{1,0:T(8,128)(2,1)S(1)}, u32[]{:S(2)}, u32[]{:S(2)}) collective-permute-start(bf16[640,128]{1,0:T(8,128)(2,1)S(1)} %get-tuple-element.51), channel_id=1, source_target_pairs={{0,4},{4,0},{8,12},{12,8},{16,20},{20,16},{24,28},{28,24},{1,5},{5... | collective-permute-start | bytes 491528 | tf_op jit(solution)/shard_map/ppermute | solution.py:612
  15.1 0.7 %copy-start = (bf16[3,3,1024]{2,1,0:T(4,128)(2,1)S(1)}, bf16[3,3,1024]{2,1,0:T(4,128)(2,1)}, u32[]{:S(2)}) copy-start(bf16[3,3,1024]{2,1,0:T(4,128)(2,1)} %taps_any.1) | copy-start | bytes 55300
  26.1 6.8 %collective-permute-start.11 = (bf16[432,128]{1,0:T(8,128)(2,1)S(1)}, bf16[432,128]{1,0:T(8,128)(2,1)S(1)}, u32[]{:S(2)}, u32[]{:S(2)}) collective-permute-start(bf16[432,128]{1,0:T(8,128)(2,1)S(1)} %get-tuple-element.59), channel_id=1, source_target_pairs={{0,24},{4,28},{8,16},{12,20},{16,8},{20,12},{24,0},{28,4},{1,25},{... | collective-permute-start | bytes 331784 | tf_op jit(solution)/shard_map/ppermute | solution.py:612
  28.4 6.8 %collective-permute-start.12 = (bf16[432,128]{1,0:T(8,128)(2,1)S(1)}, bf16[432,128]{1,0:T(8,128)(2,1)S(1)}, u32[]{:S(2)}, u32[]{:S(2)}) collective-permute-start(bf16[432,128]{1,0:T(8,128)(2,1)S(1)} %get-tuple-element.60), channel_id=1, source_target_pairs={{0,8},{4,12},{8,0},{12,4},{16,24},{20,28},{24,16},{28,20},{1,9},{5... | collective-permute-start | bytes 331784 | tf_op jit(solution)/shard_map/ppermute | solution.py:612
  29.0 6.5 %collective-permute-start.13 = (bf16[432,128]{1,0:T(8,128)(2,1)S(1)}, bf16[432,128]{1,0:T(8,128)(2,1)S(1)}, u32[]{:S(2)}, u32[]{:S(2)}) collective-permute-start(bf16[432,128]{1,0:T(8,128)(2,1)S(1)} %get-tuple-element.61), channel_id=1, source_target_pairs={{0,20},{4,16},{8,28},{12,24},{16,4},{20,0},{24,12},{28,8},{1,21},{... | collective-permute-start | bytes 331784 | tf_op jit(solution)/shard_map/ppermute | solution.py:612
  29.4 8.3 %collective-permute-start.9 = (bf16[432,128]{1,0:T(8,128)(2,1)S(1)}, bf16[432,128]{1,0:T(8,128)(2,1)S(1)}, u32[]{:S(2)}, u32[]{:S(2)}) collective-permute-start(bf16[432,128]{1,0:T(8,128)(2,1)S(1)} %get-tuple-element.56), channel_id=1, source_target_pairs={{0,12},{4,8},{8,4},{12,0},{16,28},{20,24},{24,20},{28,16},{1,13},{... | collective-permute-start | bytes 331784 | tf_op jit(solution)/shard_map/ppermute | solution.py:612
  30.7 7.0 %collective-permute-start.10 = (bf16[432,128]{1,0:T(8,128)(2,1)S(1)}, bf16[432,128]{1,0:T(8,128)(2,1)S(1)}, u32[]{:S(2)}, u32[]{:S(2)}) collective-permute-start(bf16[432,128]{1,0:T(8,128)(2,1)S(1)} %get-tuple-element.57), channel_id=1, source_target_pairs={{0,16},{4,20},{8,24},{12,28},{16,0},{20,4},{24,8},{28,12},{1,17},{... | collective-permute-start | bytes 331784 | tf_op jit(solution)/shard_map/ppermute | solution.py:612
  33.0 6.5 %collective-permute-start.7 = (bf16[432,128]{1,0:T(8,128)(2,1)S(1)}, bf16[432,128]{1,0:T(8,128)(2,1)S(1)}, u32[]{:S(2)}, u32[]{:S(2)}) collective-permute-start(bf16[432,128]{1,0:T(8,128)(2,1)S(1)} %get-tuple-element.52), channel_id=1, source_target_pairs={{0,28},{4,24},{8,20},{12,16},{16,12},{20,8},{24,4},{28,0},{1,29},{... | collective-permute-start | bytes 331784 | tf_op jit(solution)/shard_map/ppermute | solution.py:612
  35.3 4.2 %collective-permute-start.8 = (bf16[432,128]{1,0:T(8,128)(2,1)S(1)}, bf16[432,128]{1,0:T(8,128)(2,1)S(1)}, u32[]{:S(2)}, u32[]{:S(2)}) collective-permute-start(bf16[432,128]{1,0:T(8,128)(2,1)S(1)} %get-tuple-element.53), channel_id=1, source_target_pairs={{0,4},{4,0},{8,12},{12,8},{16,20},{20,16},{24,28},{28,24},{1,5},{5... | collective-permute-start | bytes 331784 | tf_op jit(solution)/shard_map/ppermute | solution.py:612

commit v5 on v4

--- a/solution.py
+++ b/solution.py
@@ -1,4 +1,4 @@
-from functools import lru_cache, partial
+from functools import lru_cache, partial, reduce
 import math
 
 import jax
@@ -212,6 +212,8 @@
 REACH = 120.0
 SLOPE = 2.0 * REACH / math.log2(1.0 + CURVE)
 TINY = 1e-30
+HEAD = 32
+TAPS_AT = (10, 11, 12, 13, 14, 15, 28, 29, 30)
 
 
 def split_pair(values):
@@ -235,20 +237,20 @@
     none = np.zeros((half, rows))
     middle = (1.0 - 2.0 * (back % 2))[None, :]
     imag0 = np.concatenate([middle, -sin0[1:]])
-    first = np.block([[cos0, none], [none, cos8], [imag0, none], [none, -sin8]])
+    forward = [np.block([[cos0, none], [none, cos8], [imag0, none], [none, -sin8]])]
     weight = np.full((2 * rows, 1), 2.0)
     weight[0] = weight[rows] = 1.0
-    cosine, sine = waves(0, rows)
-    other = np.block([[cosine, sine], [-sine, cosine]])
+    inverse = [(weight * forward[0]).T]
+    for residue in CLASSES:
+        cosine, sine = waves(residue, rows)
+        forward.append(np.block([[cosine, sine], [-sine, cosine]]))
+        inverse.append(2.0 * forward[-1].T)
     tables = []
-    for table in (np.stack([first, other]), np.stack([(weight * first).T, 2.0 * other.T]) / length):
+    for table in (np.stack(forward), np.stack(inverse) / length):
         high = table.astype(ml_dtypes.bfloat16)
         low = (table - high.astype(np.float64)).astype(ml_dtypes.bfloat16)
         tables.append(np.stack([high, low]))
-    turns = np.zeros((rows, LANES), np.float32)
-    for n, residue in enumerate(CLASSES):
-        turns[:, 2 * n], turns[:, 2 * n + 1] = [wave[0] for wave in waves(residue, 1)]
-    return (*tables, turns)
+    return tables
 
 
 ROOT = math.sqrt(0.5)
@@ -314,6 +316,10 @@
     return jnp.where(values < 0.0, -code, code).astype(jnp.bfloat16)
 
 
+def code_scale(peak):
+    return jnp.maximum(peak * (1.0 + 2.0**-7), TINY).astype(jnp.bfloat16).astype(jnp.float32)
+
+
 def log_decode(code, scale):
     code = code.astype(jnp.float32)
     share = jnp.exp2((jnp.log2(jnp.abs(code)) + REACH) * (1.0 / SLOPE)) - 1.0
@@ -323,9 +329,8 @@
 
 def table_dot(table_ref, f, both):
     half = both.shape[1] // 2
-    which = min(f, 1)
-    found = jnp.dot(table_ref[0, which], both, preferred_element_type=jnp.float32)
-    rest = jnp.dot(table_ref[1, which], both[:, :half], preferred_element_type=jnp.float32)
+    found = jnp.dot(table_ref[0, f], both, preferred_element_type=jnp.float32)
+    rest = jnp.dot(table_ref[1, f], both[:, :half], preferred_element_type=jnp.float32)
     return found[:, :half] + (found[:, half:] + rest)
 
 
@@ -350,11 +355,8 @@
     return jnp.concatenate([high for high, _ in pairs] + [low for _, low in pairs], axis=1)
 
 
-def put_classes(ref, column, columns, rows, b0, values, turn):
+def put_classes(ref, column, columns, rows, b0, values):
     for f, pair in enumerate(forward_classes(values)):
-        if f > 0:
-            cosine, sine = [turn[2 * f - 2 + n, pl.ds(b0, CHUNK), :] for n in range(2)]
-            pair = (pair[0] * cosine + pair[1] * sine, pair[1] * cosine - pair[0] * sine)
         for part, value in enumerate(pair):
             high, low = split_pair(value)
             at = pl.ds(part * rows + b0, CHUNK)
@@ -362,14 +364,11 @@
             ref[f, at, pl.ds((columns + column) * LANES, LANES)] = low
 
 
-def take_classes(ref, column, rows, b0, turn):
+def take_classes(ref, column, rows, b0):
     lanes = pl.ds(column * LANES, LANES)
     found = []
     for f in range(ref.shape[0]):
         pair = ref[f, pl.ds(b0, CHUNK), lanes], ref[f, pl.ds(rows + b0, CHUNK), lanes]
-        if f > 0:
-            cosine, sine = [turn[2 * f - 2 + n, pl.ds(b0, CHUNK), :] for n in range(2)]
-            pair = (pair[0] * cosine - pair[1] * sine, pair[1] * cosine + pair[0] * sine)
         found.append(pair)
     return inverse_classes(found)
 
@@ -400,7 +399,7 @@
     return [[taps_ref[3 * i + j : 3 * i + j + 1, :] for j in range(3)] for i in range(3)]
 
 
-def layer_kernel(me_ref, gain_ref, turn, forward_ref, inverse_ref, *refs):
+def layer_kernel(me_ref, gain_ref, forward_ref, inverse_ref, *refs):
     got, outs = refs[:RADIX], refs[RADIX : 2 * RADIX]
     qp, kp, vp, hs, cot, ks, vs, xs, xs_grad, spec, spec_grad, ys_conv, ys, zs_conv, zs, conv, mgrad, fgrad, peak, sums, head = refs[2 * RADIX :]
     rows = got[0].shape[0] // FIELDS
@@ -424,16 +423,16 @@
             ks[pl.ds(at, CHUNK), :] = key_filt
             vs[pl.ds(at, CHUNK), :] = value_filt
             mixed.append(key_filt * value_filt)
-        put_classes(xs, 0, 2, rows, b0, mixed, turn)
+        put_classes(xs, 0, 2, rows, b0, mixed)
         filt = [hs[pl.ds(a * rows + b0, CHUNK), :] for a in range(RADIX)]
-        put_classes(xs, 1, 2, rows, b0, filt, turn)
+        put_classes(xs, 1, 2, rows, b0, filt)
     for f, b0 in zip(classes, chunks):
         spec[f] = table_dot(forward_ref, f, xs[f])
         conv_grad = []
         for a in range(RADIX):
             at = a * rows + b0
             conv_grad.append(short_filter(gain[0], qp, PAD + at) * cot[pl.ds(at, CHUNK), :])
-        put_classes(xs_grad, 0, 1, rows, b0, conv_grad, turn)
+        put_classes(xs_grad, 0, 1, rows, b0, conv_grad)
     for f in classes:
         spec_grad[f] = table_dot(forward_ref, f, xs_grad[f])
         mixed, filt = [spec_parts(spec[f], rows, c) for c in range(2)]
@@ -447,7 +446,7 @@
     sums[...] = jnp.zeros_like(sums)
 
     def take(column, b0, ref, source, place):
-        found = take_classes(source, place, rows, b0, turn)
+        found = take_classes(source, place, rows, b0)
         for a, value in enumerate(found):
             ref[pl.ds(a * rows + b0, CHUNK), :] = value
             size = jnp.abs(value)
@@ -474,10 +473,11 @@
         take(2, b0, fgrad, zs, 1)
     grad_scale = 1.0 / math.sqrt(total)
     head[...] = jnp.zeros_like(head)
-    for n in range(9):
-        at = 32 + n if n < 8 else 22
-        head[pl.ds(at, 1), :] = jnp.sum(sums[n], axis=0, keepdims=True) * grad_scale
-    head[pl.ds(40, 8), :] = split_pair(head[pl.ds(32, 8), :])[1].astype(f32)
+    taps = [jnp.sum(sums[n], axis=0, keepdims=True) * grad_scale for n in range(9)]
+    scale = code_scale(reduce(jnp.maximum, [jnp.abs(line) for line in taps]))
+    head[pl.ds(9, 1), :] = scale
+    for at, line in zip(TAPS_AT, taps):
+        head[pl.ds(at, 1), :] = log_code(line, 1.0 / scale).astype(f32)
     for k, out_ref in zip(BACK, outs):
         a = me_ref[0] ^ k
         first = pl.multiple_of(a * rows, rows)
@@ -486,31 +486,35 @@
             head[pl.ds(2 * i, 2), :] = ref[pl.ds(first + PAD - 2, 2), :]
         for column, ref in enumerate((conv, mgrad, fgrad)):
             top = jnp.max(peak[column, a], axis=0, keepdims=True)
-            scale = jnp.maximum(top * (1.0 + 2.0**-7), TINY).astype(jnp.bfloat16).astype(f32)
+            scale = code_scale(top)
             head[pl.ds(6 + column, 1), :] = scale
             out_ref[pl.ds(column * rows, rows), :] = log_code(
                 ref[pl.ds(first, rows), :], 1.0 / scale
             )
         for i, (ref, other) in enumerate(((conv, cot), (mgrad, vs), (mgrad, ks))):
             head[pl.ds(16 + 2 * i, 2), :] = ref[pl.ds(after, 2), :] * other[pl.ds(after, 2), :]
-        head[pl.ds(24, 8), :] = split_pair(head[pl.ds(16, 8), :])[1].astype(f32)
-        out_ref[pl.ds(3 * rows, 48), :] = head[...].astype(jnp.bfloat16)
+        head[pl.ds(22, 6), :] = split_pair(head[pl.ds(16, 6), :])[1].astype(f32)
+        out_ref[pl.ds(3 * rows, HEAD), :] = head[...].astype(jnp.bfloat16)
 
 
 def prepare_kernel(
-    me_ref, turns_ref, forward_any, inverse_any, taps_any, _, query_ref, key_ref, value_ref, cot_ref,
-    turn, forward_ref, inverse_ref, gain_ref, wide_ref, early_ref, wide,
+    me_ref, forward_any, inverse_any, taps_any, _, query_ref, key_ref, value_ref, cot_ref,
+    forward_ref, inverse_ref, gain_ref, wide_ref, early_ref, wide, sem,
 ):
     lane = pl.ds(pl.multiple_of(me_ref[0] * LANES, LANES), LANES)
-    forward_ref[...] = forward_any[...]
-    inverse_ref[...] = inverse_any[...]
-    for n in range(turn.shape[0]):
-        turn[n] = jnp.broadcast_to(turns_ref[:, n : n + 1], turn.shape[1:])
+    copies = [
+        pltpu.make_async_copy(forward_any.at[n], forward_ref.at[n], sem.at[n]) for n in range(2)
+    ] + [
+        pltpu.make_async_copy(inverse_any.at[n], inverse_ref.at[n], sem.at[2 + n]) for n in range(2)
+    ]
+    for copy in copies:
+        copy.start()
+    taps = taps_any[...].astype(jnp.float32)
     for i in range(3):
         for j in range(3):
             at = 3 * i + j
-            wide_ref[at : at + 1, :] = taps_any[i, j : j + 1, :].astype(jnp.float32)
-            gain_ref[at : at + 1, :] = taps_any[i, j : j + 1, lane].astype(jnp.float32)
+            wide_ref[at : at + 1, :] = taps[i, j : j + 1, :]
+            gain_ref[at : at + 1, :] = wide_ref[at : at + 1, lane]
     rows = cot_ref.shape[0]
     for i, ref in enumerate((query_ref, key_ref, value_ref)):
         wide[pl.ds(0, PAD), :] = jnp.zeros((PAD, wide.shape[1]), jnp.float32)
@@ -521,6 +525,8 @@
             + wide_ref[3 * i + 2 : 3 * i + 3, :] * wide[pl.ds(PAD - 2, rows), :]
         )
     early_ref[3] = cot_ref[...].astype(jnp.float32)
+    for copy in copies:
+        copy.wait()
 
 
 def whole_vmem(count):
@@ -556,15 +562,14 @@
     copies = []
     for n, (k, got_ref) in enumerate(zip(places, got)):
         lanes = pl.ds(pl.multiple_of((me_ref[0] ^ k) * LANES, LANES), LANES)
-        head = got_ref[pl.ds(3 * rows, 48), :].astype(f32)
+        head = got_ref[pl.ds(3 * rows, HEAD), :].astype(f32)
         conv, mixed_grad, filt = [
             log_decode(got_ref[pl.ds(c * rows, rows), :], head[6 + c : 7 + c]) for c in range(3)
         ]
         stage_filter[n] = filt * (1.0 / math.sqrt(RADIX * rows))
-        pairs = head[16:24] + head[24:32]
-        taps = head[32:40] + head[40:48]
-        for c in range(9):
-            stage_taps[n, c // 3, c % 3 : c % 3 + 1, :] = taps[c : c + 1] if c < 8 else pairs[6:7]
+        pairs = head[16:22] + head[22:28]
+        for c, at in enumerate(TAPS_AT):
+            stage_taps[n, c // 3, c % 3 : c % 3 + 1, :] = log_decode(head[at : at + 1], head[9:10])
         line = lax.broadcasted_iota(jnp.int32, (PAD, LANES), 0)
         filtered = []
         gain = []
@@ -644,29 +649,28 @@
 
     packed = pack(SENT)
     got = swap_blocks(SENT, packed)
-    forward, inverse, turns = class_tables(rows)
+    forward, inverse = class_tables(rows)
     count = 1 + len(CLASSES)
     ready = pl.pallas_call(
         prepare_kernel,
         out_shape=[
-            pltpu.VMEM((2 * len(CLASSES), rows, LANES), f32),
             pltpu.VMEM(forward.shape, bf16),
             pltpu.VMEM(inverse.shape, bf16),
             pltpu.VMEM((16, LANES), f32),
             pltpu.VMEM((16, channels), f32),
             pltpu.VMEM((4, rows, channels), f32),
         ],
-        in_specs=[IN_SMEM] + whole_vmem(9),
-        out_specs=whole_vmem(6),
-        scratch_shapes=[pltpu.VMEM((PAD + rows, channels), f32)],
+        in_specs=[IN_SMEM] + whole_any(2) + whole_vmem(6),
+        out_specs=whole_vmem(5),
+        scratch_shapes=[pltpu.VMEM((PAD + rows, channels), f32), pltpu.SemaphoreType.DMA((4,))],
         compiler_params=small,
         name="prepare",
-    )(me, *held((turns, forward, inverse), pltpu.HBM), short_taps, *held(got[1:2], pltpu.VMEM), *inputs)
+    )(me, *held((forward, inverse), pltpu.HBM), short_taps, *held(got[1:2], pltpu.VMEM), *inputs)
     ready = held(ready, pltpu.VMEM)
     done = pl.pallas_call(
         layer_kernel,
-        out_shape=[pltpu.VMEM((3 * rows + 48, LANES), bf16)] * RADIX,
-        in_specs=[IN_SMEM] + whole_vmem(4 + RADIX),
+        out_shape=[pltpu.VMEM((3 * rows + HEAD, LANES), bf16)] * RADIX,
+        in_specs=[IN_SMEM] + whole_vmem(3 + RADIX),
         out_specs=whole_vmem(RADIX),
         scratch_shapes=[pltpu.VMEM((total + PAD, LANES), f32)] * 7
         + [
@@ -679,11 +683,11 @@
         + [
             pltpu.VMEM((3, RADIX, 8, LANES), f32),
             pltpu.VMEM((9, 8, LANES), f32),
-            pltpu.VMEM((48, LANES), f32),
+            pltpu.VMEM((HEAD, LANES), f32),
         ],
         compiler_params=pltpu.CompilerParams(vmem_limit_bytes=20 * 1024 * 1024),
         name="layer",
-    )(me, ready[3], *ready[:3], *held(got, pltpu.VMEM))
+    )(me, ready[2], *ready[:2], *held(got, pltpu.VMEM))
     back = held(swap_blocks(BACK, done), pltpu.VMEM)
     results = [shape((rows, channels), bf16)] * 4 + [
         shape((rows, channels), f32),
@@ -708,7 +712,7 @@
             input_output_aliases={count + 3 + n: n for n in range(len(begun))},
             compiler_params=small,
             name="finish",
-        )(me, *back[first:last], *ready[4:], *begun)
+        )(me, *back[first:last], *ready[3:], *begun)
     return tuple(begun)
 
 

time: 40.8 us -> 39.9 us (0.978)
  waiting for transfers between devices: 8.58 us -> 7.5 us
    ppermute x14, waiting for transfers between devices: 8.58 us -> 7.5 us  [swap_blocks(): lax.ppermute(block, 'ctx', [(i, i ^ k) for i in devices])]
  transfers between devices with their start and end apart: 14 -> 14, of which waited for: 8 -> 8; matrix products, arithmetic and copies ran while one was open for 0% -> 0% of each run, Pallas kernels for 13% -> 15%
where the time goes in v5:
time: 39.9 us; the launch traced here: 39.7 us
  starting transfers between devices  16.5 us (41%)
  Pallas kernels  14.2 us (36%)
  waiting for transfers between devices  7.5 us (19%)
  local copies, waits for them, and re-layouts  0.74 us (2%)
  between operations  0.71 us (2%)
    ppermute x14, starting transfers between devices, swap_blocks(): lax.ppermute(block, 'ctx', [(i, i ^ k) for i in devices])  16.5 us
    ppermute x14, waiting for transfers between devices, swap_blocks(): lax.ppermute(block, 'ctx', [(i, i ^ k) for i in devices])  7.5 us
    pallas_call x1, Pallas kernels, local_fast(): pl.pallas_call(layer_kernel, out_shape=[pltpu.VMEM((3 * rows + HEAD, LANE...  5.69 us
    pallas_call x3, Pallas kernels, local_fast(): pl.pallas_call(partial(finish_kernel, BACK[first:last], len(begun)), out_...  3.75 us
    pallas_call x1, Pallas kernels, local_fast(): pl.pallas_call(prepare_kernel, out_shape=[pltpu.VMEM(forward.shape, bf16)...  3.39 us
    pallas_call x1, Pallas kernels, pack(): pl.pallas_call(partial(pack_kernel, places), out_shape=[pltpu.VMEM((FIELD...  1.38 us
  transfers between devices with their start and end apart: 14, of which 8 were waited for; matrix products, arithmetic and copies ran while one was open for 0% of the time, Pallas kernels for 15%

profile of v5, /device:TPU:0, one launch (start us, length us, event | category | flops | bytes accessed | tf_op | source)
XLA Modules:
  0.0 39.7 jit_solution(5798932589902142797)
XLA Ops:
  0.6 1.4 %pack.1 = (bf16[640,128]{1,0:T(8,128)(2,1)S(1)}, bf16[640,128]{1,0:T(8,128)(2,1)S(1)}, bf16[640,128]{1,0:T(8,128)(2,1)S(1)}, bf16[640,128]{1,0:T(8,128)(2,1)S(1)...) custom-call(s32[1]{0:T(128)} %bitcast.me_ref, ...), custom_call_target="tpu_custom_call" | custom-call | tf_op jit(solution)/shard_map/pack/pallas_call | solution.py:637
  2.0 4.0 %collective-permute-start = (bf16[640,128]{1,0:T(8,128)(2,1)S(1)}, bf16[640,128]{1,0:T(8,128)(2,1)S(1)}, u32[]{:S(2)}, u32[]{:S(2)}) collective-permute-start(bf16[640,128]{1,0:T(8,128)(2,1)S(1)} %get-tuple-element.39), channel_id=1, source_target_pairs={{0,24},{4,28},{8,16},{12,20},{16,8},{20,12},{24,0},{28,4},{1,25},{... | collective-permute-start | bytes 491528 | tf_op jit(solution)/shard_map/ppermute | solution.py:617
  6.0 0.5 %collective-permute-start.1 = (bf16[640,128]{1,0:T(8,128)(2,1)S(1)}, bf16[640,128]{1,0:T(8,128)(2,1)S(1)}, u32[]{:S(2)}, u32[]{:S(2)}) collective-permute-start(bf16[640,128]{1,0:T(8,128)(2,1)S(1)} %get-tuple-element.44), channel_id=1, source_target_pairs={{0,8},{4,12},{8,0},{12,4},{16,24},{20,28},{24,16},{28,20},{1,9},{5... | collective-permute-start | bytes 491528 | tf_op jit(solution)/shard_map/ppermute | solution.py:617
  6.5 1.7 %collective-permute-start.3 = (bf16[640,128]{1,0:T(8,128)(2,1)S(1)}, bf16[640,128]{1,0:T(8,128)(2,1)S(1)}, u32[]{:S(2)}, u32[]{:S(2)}) collective-permute-start(bf16[640,128]{1,0:T(8,128)(2,1)S(1)} %get-tuple-element.46), channel_id=1, source_target_pairs={{0,12},{4,8},{8,4},{12,0},{16,28},{20,24},{24,20},{28,16},{1,13},{... | collective-permute-start | bytes 491528 | tf_op jit(solution)/shard_map/ppermute | solution.py:617
  8.2 1.5 %collective-permute-start.4 = (bf16[640,128]{1,0:T(8,128)(2,1)S(1)}, bf16[640,128]{1,0:T(8,128)(2,1)S(1)}, u32[]{:S(2)}, u32[]{:S(2)}) collective-permute-start(bf16[640,128]{1,0:T(8,128)(2,1)S(1)} %get-tuple-element.47), channel_id=1, source_target_pairs={{0,16},{4,20},{8,24},{12,28},{16,0},{20,4},{24,8},{28,12},{1,17},{... | collective-permute-start | bytes 491528 | tf_op jit(solution)/shard_map/ppermute | solution.py:617
  9.8 1.3 %collective-permute-done._.refs_1_ = bf16[640,128]{1,0:T(8,128)(2,1)S(1)} collective-permute-done((bf16[640,128]{1,0:T(8,128)(2,1)S(1)}, bf16[640,128]{1,0:T(8,128)(2,1)S(1)}, u32[]{:S(2)}, u32[]{:S(2)}) %collective-permute-start) | collective-permute-done | bytes 163872 | tf_op jit(solution)/shard_map/ppermute | solution.py:617
  11.0 0.4 collective-permute-start.5
  11.4 3.7 %collective-permute-done.1.refs_2_ = bf16[640,128]{1,0:T(8,128)(2,1)S(1)} collective-permute-done((bf16[640,128]{1,0:T(8,128)(2,1)S(1)}, bf16[640,128]{1,0:T(8,128)(2,1)S(1)}, u32[]{:S(2)}, u32[]{:S(2)}) %collective-permute-start.1) | collective-permute-done | bytes 163872 | tf_op jit(solution)/shard_map/ppermute | solution.py:617
  15.1 0.7 %copy-done = bf16[3,3,1024]{2,1,0:T(4,128)(2,1)S(1)} copy-done((bf16[3,3,1024]{2,1,0:T(4,128)(2,1)S(1)}, bf16[3,3,1024]{2,1,0:T(4,128)(2,1)}, u32[]{:S(2)}) %copy-start) | copy-done | bytes 18456
  15.8 3.4 %prepare.1 = (bf16[2,8,256,256]{3,2,1,0:T(8,128)(2,1)S(1)}, bf16[2,8,256,256]{3,2,1,0:T(8,128)(2,1)S(1)}, f32[16,128]{1,0:T(8,128)S(1)}, f32[16,1024]{1,0:T(8,128)S(1)}, f32[4,128,1024]{2,1,0:T(8,128)S(1)}) custom-call(s32[1]{0:T(128)} %bitcast.me_ref, bf16[2,8,256,256]{3,2,1,0:T(8,128)(2,1)} %constant.10.clone.forward_any, ...), custom_call_target="tpu_custom_call" | custom-call | tf_op jit(solution)/shard_map/prepare/pallas_call | solution.py:654
  19.3 0.7 %collective-permute-done.5.refs_6_ = bf16[640,128]{1,0:T(8,128)(2,1)S(1)} collective-permute-done((bf16[640,128]{1,0:T(8,128)(2,1)S(1)}, bf16[640,128]{1,0:T(8,128)(2,1)S(1)}, u32[]{:S(2)}, u32[]{:S(2)}) %collective-permute-start.5) | collective-permute-done | bytes 163872 | tf_op jit(solution)/shard_map/ppermute | solution.py:617
  20.0 5.7 %layer.1 = (bf16[416,128]{1,0:T(8,128)(2,1)S(1)}, bf16[416,128]{1,0:T(8,128)(2,1)S(1)}, bf16[416,128]{1,0:T(8,128)(2,1)S(1)}, bf16[416,128]{1,0:T(8,128)(2,1)S(1...) custom-call(s32[1]{0:T(128)} %bitcast.me_ref, ...), custom_call_target="tpu_custom_call" | custom-call | tf_op jit(solution)/shard_map/layer/pallas_call | solution.py:670
  25.7 2.3 %collective-permute-start.11 = (bf16[416,128]{1,0:T(8,128)(2,1)S(1)}, bf16[416,128]{1,0:T(8,128)(2,1)S(1)}, u32[]{:S(2)}, u32[]{:S(2)}) collective-permute-start(bf16[416,128]{1,0:T(8,128)(2,1)S(1)} %get-tuple-element.57), channel_id=1, source_target_pairs={{0,24},{4,28},{8,16},{12,20},{16,8},{20,12},{24,0},{28,4},{1,25},{... | collective-permute-start | bytes 319496 | tf_op jit(solution)/shard_map/ppermute | solution.py:617
  28.0 0.5 %collective-permute-start.12 = (bf16[416,128]{1,0:T(8,128)(2,1)S(1)}, bf16[416,128]{1,0:T(8,128)(2,1)S(1)}, u32[]{:S(2)}, u32[]{:S(2)}) collective-permute-start(bf16[416,128]{1,0:T(8,128)(2,1)S(1)} %get-tuple-element.58), channel_id=1, source_target_pairs={{0,8},{4,12},{8,0},{12,4},{16,24},{20,28},{24,16},{28,20},{1,9},{5... | collective-permute-start | bytes 319496 | tf_op jit(solution)/shard_map/ppermute | solution.py:617
  28.5 0.4 %collective-permute-start.13 = (bf16[416,128]{1,0:T(8,128)(2,1)S(1)}, bf16[416,128]{1,0:T(8,128)(2,1)S(1)}, u32[]{:S(2)}, u32[]{:S(2)}) collective-permute-start(bf16[416,128]{1,0:T(8,128)(2,1)S(1)} %get-tuple-element.59), channel_id=1, source_target_pairs={{0,20},{4,16},{8,28},{12,24},{16,4},{20,0},{24,12},{28,8},{1,21},{... | collective-permute-start | bytes 319496 | tf_op jit(solution)/shard_map/ppermute | solution.py:617
  28.9 1.3 %collective-permute-start.9 = (bf16[416,128]{1,0:T(8,128)(2,1)S(1)}, bf16[416,128]{1,0:T(8,128)(2,1)S(1)}, u32[]{:S(2)}, u32[]{:S(2)}) collective-permute-start(bf16[416,128]{1,0:T(8,128)(2,1)S(1)} %get-tuple-element.54), channel_id=1, source_target_pairs={{0,12},{4,8},{8,4},{12,0},{16,28},{20,24},{24,20},{28,16},{1,13},{... | collective-permute-start | bytes 319496 | tf_op jit(solution)/shard_map/ppermute | solution.py:617
  30.2 1.5 %collective-permute-start.10 = (bf16[416,128]{1,0:T(8,128)(2,1)S(1)}, bf16[416,128]{1,0:T(8,128)(2,1)S(1)}, u32[]{:S(2)}, u32[]{:S(2)}) collective-permute-start(bf16[416,128]{1,0:T(8,128)(2,1)S(1)} %get-tuple-element.55), channel_id=1, source_target_pairs={{0,16},{4,20},{8,24},{12,28},{16,0},{20,4},{24,8},{28,12},{1,17},{... | collective-permute-start | bytes 319496 | tf_op jit(solution)/shard_map/ppermute | solution.py:617
  31.7 0.7 %collective-permute-done.11.refs_1_ = bf16[416,128]{1,0:T(8,128)(2,1)S(1)} collective-permute-done((bf16[416,128]{1,0:T(8,128)(2,1)S(1)}, bf16[416,128]{1,0:T(8,128)(2,1)S(1)}, u32[]{:S(2)}, u32[]{:S(2)}) %collective-permute-start.11) | collective-permute-done | bytes 106528 | tf_op jit(solution)/shard_map/ppermute | solution.py:617
  32.4 2.1 %collective-permute-start.7 = (bf16[416,128]{1,0:T(8,128)(2,1)S(1)}, bf16[416,128]{1,0:T(8,128)(2,1)S(1)}, u32[]{:S(2)}, u32[]{:S(2)}) collective-permute-start(bf16[416,128]{1,0:T(8,128)(2,1)S(1)} %get-tuple-element.50), channel_id=1, source_target_pairs={{0,28},{4,24},{8,20},{12,16},{16,12},{20,8},{24,4},{28,0},{1,29},{... | collective-permute-start | bytes 319496 | tf_op jit(solution)/shard_map/ppermute | solution.py:617
  34.9 1.5 %finish.3 = (bf16[128,1024]{1,0:T(8,128)(2,1)}, bf16[128,1024]{1,0:T(8,128)(2,1)}, bf16[128,1024]{1,0:T(8,128)(2,1)}, bf16[128,1024]{1,0:T(8,128)(2,1)}, f32[128,1024]{1,0:T(8,128)}, /*index=5*/f32[3,3,1024]{2,1,0:T(4,128)}) custom-call(s32[1]{0:T(128)} %bitcast.me_ref, bf16[416,128]{1,0:T(8,128)(2,1)S(1)} %get-tuple-element.56.refs_0_, ...), custom_call_target="tpu_custom_call" | custom-call | tf_op jit(solution)/shard_map/finish/pallas_call | solution.py:700
  36.5 0.4 %collective-permute-done.9.refs_0_ = bf16[416,128]{1,0:T(8,128)(2,1)S(1)} collective-permute-done((bf16[416,128]{1,0:T(8,128)(2,1)S(1)}, bf16[416,128]{1,0:T(8,128)(2,1)S(1)}, u32[]{:S(2)}, u32[]{:S(2)}) %collective-permute-start.9) | collective-permute-done | bytes 106528 | tf_op jit(solution)/shard_map/ppermute | solution.py:617
  37.0 1.1 %finish.4 = (bf16[128,1024]{1,0:T(8,128)(2,1)}, bf16[128,1024]{1,0:T(8,128)(2,1)}, bf16[128,1024]{1,0:T(8,128)(2,1)}, bf16[128,1024]{1,0:T(8,128)(2,1)}, f32[128,1024]{1,0:T(8,128)}, /*index=5*/f32[3,3,1024]{2,1,0:T(4,128)}) custom-call(s32[1]{0:T(128)} %bitcast.me_ref, ...), custom_call_target="tpu_custom_call", output_to_operand_aliasing={{0}: (5, {}), {1}: (6, {}), {2}: (7, {}), {3}: (8, {}), {4}... | custom-call | tf_op jit(solution)/shard_map/finish/pallas_call | solution.py:700
  38.1 0.5 %collective-permute-done.7.refs_0_ = bf16[416,128]{1,0:T(8,128)(2,1)S(1)} collective-permute-done((bf16[416,128]{1,0:T(8,128)(2,1)S(1)}, bf16[416,128]{1,0:T(8,128)(2,1)S(1)}, u32[]{:S(2)}, u32[]{:S(2)}) %collective-permute-start.7) | collective-permute-done | bytes 106528 | tf_op jit(solution)/shard_map/ppermute | solution.py:617
  38.6 1.1 %finish.5 = (bf16[128,1024]{1,0:T(8,128)(2,1)}, bf16[128,1024]{1,0:T(8,128)(2,1)}, bf16[128,1024]{1,0:T(8,128)(2,1)}, bf16[128,1024]{1,0:T(8,128)(2,1)}, f32[128,1024]{1,0:T(8,128)}, /*index=5*/f32[3,3,1024]{2,1,0:T(4,128)}) custom-call(s32[1]{0:T(128)} %bitcast.me_ref, ...), custom_call_target="tpu_custom_call", output_to_operand_aliasing={{0}: (5, {}), {1}: (6, {}), {2}: (7, {}), {3}: (8, {}), {4}... | custom-call | tf_op jit(solution)/shard_map/finish/pallas_call | solution.py:700
  (12 shorter events, 0.6 us)
Async XLA Ops:
  2.0 9.0 %collective-permute-start = (bf16[640,128]{1,0:T(8,128)(2,1)S(1)}, bf16[640,128]{1,0:T(8,128)(2,1)S(1)}, u32[]{:S(2)}, u32[]{:S(2)}) collective-permute-start(bf16[640,128]{1,0:T(8,128)(2,1)S(1)} %get-tuple-element.39), channel_id=1, source_target_pairs={{0,24},{4,28},{8,16},{12,20},{16,8},{20,12},{24,0},{28,4},{1,25},{... | collective-permute-start | bytes 491528 | tf_op jit(solution)/shard_map/ppermute | solution.py:617
  6.0 9.1 %collective-permute-start.1 = (bf16[640,128]{1,0:T(8,128)(2,1)S(1)}, bf16[640,128]{1,0:T(8,128)(2,1)S(1)}, u32[]{:S(2)}, u32[]{:S(2)}) collective-permute-start(bf16[640,128]{1,0:T(8,128)(2,1)S(1)} %get-tuple-element.44), channel_id=1, source_target_pairs={{0,8},{4,12},{8,0},{12,4},{16,24},{20,28},{24,16},{28,20},{1,9},{5... | collective-permute-start | bytes 491528 | tf_op jit(solution)/shard_map/ppermute | solution.py:617
  6.5 12.7 %collective-permute-start.2 = (bf16[640,128]{1,0:T(8,128)(2,1)S(1)}, bf16[640,128]{1,0:T(8,128)(2,1)S(1)}, u32[]{:S(2)}, u32[]{:S(2)}) collective-permute-start(bf16[640,128]{1,0:T(8,128)(2,1)S(1)} %get-tuple-element.45), channel_id=1, source_target_pairs={{0,20},{4,16},{8,28},{12,24},{16,4},{20,0},{24,12},{28,8},{1,21},{... | collective-permute-start | bytes 491528 | tf_op jit(solution)/shard_map/ppermute | solution.py:617
  6.5 12.7 %collective-permute-start.3 = (bf16[640,128]{1,0:T(8,128)(2,1)S(1)}, bf16[640,128]{1,0:T(8,128)(2,1)S(1)}, u32[]{:S(2)}, u32[]{:S(2)}) collective-permute-start(bf16[640,128]{1,0:T(8,128)(2,1)S(1)} %get-tuple-element.46), channel_id=1, source_target_pairs={{0,12},{4,8},{8,4},{12,0},{16,28},{20,24},{24,20},{28,16},{1,13},{... | collective-permute-start | bytes 491528 | tf_op jit(solution)/shard_map/ppermute | solution.py:617
  8.2 11.0 %collective-permute-start.4 = (bf16[640,128]{1,0:T(8,128)(2,1)S(1)}, bf16[640,128]{1,0:T(8,128)(2,1)S(1)}, u32[]{:S(2)}, u32[]{:S(2)}) collective-permute-start(bf16[640,128]{1,0:T(8,128)(2,1)S(1)} %get-tuple-element.47), channel_id=1, source_target_pairs={{0,16},{4,20},{8,24},{12,28},{16,0},{20,4},{24,8},{28,12},{1,17},{... | collective-permute-start | bytes 491528 | tf_op jit(solution)/shard_map/ppermute | solution.py:617
  11.0 9.0 %collective-permute-start.5 = (bf16[640,128]{1,0:T(8,128)(2,1)S(1)}, bf16[640,128]{1,0:T(8,128)(2,1)S(1)}, u32[]{:S(2)}, u32[]{:S(2)}) collective-permute-start(bf16[640,128]{1,0:T(8,128)(2,1)S(1)} %get-tuple-element.48), channel_id=1, source_target_pairs={{0,28},{4,24},{8,20},{12,16},{16,12},{20,8},{24,4},{28,0},{1,29},{... | collective-permute-start | bytes 491528 | tf_op jit(solution)/shard_map/ppermute | solution.py:617
  15.1 4.9 %collective-permute-start.6 = (bf16[640,128]{1,0:T(8,128)(2,1)S(1)}, bf16[640,128]{1,0:T(8,128)(2,1)S(1)}, u32[]{:S(2)}, u32[]{:S(2)}) collective-permute-start(bf16[640,128]{1,0:T(8,128)(2,1)S(1)} %get-tuple-element.49), channel_id=1, source_target_pairs={{0,4},{4,0},{8,12},{12,8},{16,20},{20,16},{24,28},{28,24},{1,5},{5... | collective-permute-start | bytes 491528 | tf_op jit(solution)/shard_map/ppermute | solution.py:617
  15.1 0.7 %copy-start = (bf16[3,3,1024]{2,1,0:T(4,128)(2,1)S(1)}, bf16[3,3,1024]{2,1,0:T(4,128)(2,1)}, u32[]{:S(2)}) copy-start(bf16[3,3,1024]{2,1,0:T(4,128)(2,1)} %taps_any.1) | copy-start | bytes 55300
  25.7 6.7 %collective-permute-start.11 = (bf16[416,128]{1,0:T(8,128)(2,1)S(1)}, bf16[416,128]{1,0:T(8,128)(2,1)S(1)}, u32[]{:S(2)}, u32[]{:S(2)}) collective-permute-start(bf16[416,128]{1,0:T(8,128)(2,1)S(1)} %get-tuple-element.57), channel_id=1, source_target_pairs={{0,24},{4,28},{8,16},{12,20},{16,8},{20,12},{24,0},{28,4},{1,25},{... | collective-permute-start | bytes 319496 | tf_op jit(solution)/shard_map/ppermute | solution.py:617
  28.0 6.6 %collective-permute-start.12 = (bf16[416,128]{1,0:T(8,128)(2,1)S(1)}, bf16[416,128]{1,0:T(8,128)(2,1)S(1)}, u32[]{:S(2)}, u32[]{:S(2)}) collective-permute-start(bf16[416,128]{1,0:T(8,128)(2,1)S(1)} %get-tuple-element.58), channel_id=1, source_target_pairs={{0,8},{4,12},{8,0},{12,4},{16,24},{20,28},{24,16},{28,20},{1,9},{5... | collective-permute-start | bytes 319496 | tf_op jit(solution)/shard_map/ppermute | solution.py:617
  28.5 6.4 %collective-permute-start.13 = (bf16[416,128]{1,0:T(8,128)(2,1)S(1)}, bf16[416,128]{1,0:T(8,128)(2,1)S(1)}, u32[]{:S(2)}, u32[]{:S(2)}) collective-permute-start(bf16[416,128]{1,0:T(8,128)(2,1)S(1)} %get-tuple-element.59), channel_id=1, source_target_pairs={{0,20},{4,16},{8,28},{12,24},{16,4},{20,0},{24,12},{28,8},{1,21},{... | collective-permute-start | bytes 319496 | tf_op jit(solution)/shard_map/ppermute | solution.py:617
  28.9 8.0 %collective-permute-start.9 = (bf16[416,128]{1,0:T(8,128)(2,1)S(1)}, bf16[416,128]{1,0:T(8,128)(2,1)S(1)}, u32[]{:S(2)}, u32[]{:S(2)}) collective-permute-start(bf16[416,128]{1,0:T(8,128)(2,1)S(1)} %get-tuple-element.54), channel_id=1, source_target_pairs={{0,12},{4,8},{8,4},{12,0},{16,28},{20,24},{24,20},{28,16},{1,13},{... | collective-permute-start | bytes 319496 | tf_op jit(solution)/shard_map/ppermute | solution.py:617
  30.2 6.7 %collective-permute-start.10 = (bf16[416,128]{1,0:T(8,128)(2,1)S(1)}, bf16[416,128]{1,0:T(8,128)(2,1)S(1)}, u32[]{:S(2)}, u32[]{:S(2)}) collective-permute-start(bf16[416,128]{1,0:T(8,128)(2,1)S(1)} %get-tuple-element.55), channel_id=1, source_target_pairs={{0,16},{4,20},{8,24},{12,28},{16,0},{20,4},{24,8},{28,12},{1,17},{... | collective-permute-start | bytes 319496 | tf_op jit(solution)/shard_map/ppermute | solution.py:617
  32.4 6.2 %collective-permute-start.7 = (bf16[416,128]{1,0:T(8,128)(2,1)S(1)}, bf16[416,128]{1,0:T(8,128)(2,1)S(1)}, u32[]{:S(2)}, u32[]{:S(2)}) collective-permute-start(bf16[416,128]{1,0:T(8,128)(2,1)S(1)} %get-tuple-element.50), channel_id=1, source_target_pairs={{0,28},{4,24},{8,20},{12,16},{16,12},{20,8},{24,4},{28,0},{1,29},{... | collective-permute-start | bytes 319496 | tf_op jit(solution)/shard_map/ppermute | solution.py:617
  34.6 4.0 %collective-permute-start.8 = (bf16[416,128]{1,0:T(8,128)(2,1)S(1)}, bf16[416,128]{1,0:T(8,128)(2,1)S(1)}, u32[]{:S(2)}, u32[]{:S(2)}) collective-permute-start(bf16[416,128]{1,0:T(8,128)(2,1)S(1)} %get-tuple-element.51), channel_id=1, source_target_pairs={{0,4},{4,0},{8,12},{12,8},{16,20},{20,16},{24,28},{28,24},{1,5},{5... | collective-permute-start | bytes 319496 | tf_op jit(solution)/shard_map/ppermute | solution.py:617

commit v6 on v5

--- a/solution.py
+++ b/solution.py
@@ -205,12 +205,10 @@
 LANES = 128
 PAD = 8
 CHUNK = 16
-SENT = (0, 6, 2, 5, 3, 4, 7, 1)
-BACK = (0, 6, 2, 5, 3, 4, 7, 1)
+SENT = (0, 6, 2, 4, 5, 3, 7, 1)
+BACK = (0, 6, 5, 2, 4, 3, 7, 1)
 FINISHED = (0, 4, 6, 8)
-CURVE = 15.0
-REACH = 120.0
-SLOPE = 2.0 * REACH / math.log2(1.0 + CURVE)
+REACH = 124.0
 TINY = 1e-30
 HEAD = 32
 TAPS_AT = (10, 11, 12, 13, 14, 15, 28, 29, 30)
@@ -311,8 +309,7 @@
 
 
 def log_code(values, inverse_scale):
-    share = 1.0 + CURVE * (jnp.abs(values) * inverse_scale)
-    code = jnp.exp2(jnp.log2(share) * SLOPE - REACH)
+    code = jnp.exp2(jnp.abs(values) * (inverse_scale * (2.0 * REACH)) - REACH)
     return jnp.where(values < 0.0, -code, code).astype(jnp.bfloat16)
 
 
@@ -322,8 +319,7 @@
 
 def log_decode(code, scale):
     code = code.astype(jnp.float32)
-    share = jnp.exp2((jnp.log2(jnp.abs(code)) + REACH) * (1.0 / SLOPE)) - 1.0
-    values = share * (scale * (1.0 / CURVE))
+    values = (jnp.log2(jnp.abs(code)) + REACH) * (scale * (0.5 / REACH))
     return jnp.where(code < 0.0, -values, values)
 
 

time: 39.9 us -> 39.6 us (level)
  transfers between devices with their start and end apart: 14 -> 14, of which waited for: 8 -> 6; matrix products, arithmetic and copies ran while one was open for 0% -> 0% of each run, Pallas kernels for 15% -> 15%
where the time goes in v6:
time: 39.6 us; the launch traced here: 39.3 us
  starting transfers between devices  16.4 us (41%)
  Pallas kernels  13.9 us (35%)
  waiting for transfers between devices  7.6 us (19%)
  local copies, waits for them, and re-layouts  0.74 us (2%)
  between operations  0.71 us (2%)
    ppermute x14, starting transfers between devices, swap_blocks(): lax.ppermute(block, 'ctx', [(i, i ^ k) for i in devices])  16.4 us
    ppermute x14, waiting for transfers between devices, swap_blocks(): lax.ppermute(block, 'ctx', [(i, i ^ k) for i in devices])  7.6 us
    pallas_call x1, Pallas kernels, local_fast(): pl.pallas_call(layer_kernel, out_shape=[pltpu.VMEM((3 * rows + HEAD, LANE...  5.51 us
    pallas_call x3, Pallas kernels, local_fast(): pl.pallas_call(partial(finish_kernel, BACK[first:last], len(begun)), out_...  3.6 us
    pallas_call x1, Pallas kernels, local_fast(): pl.pallas_call(prepare_kernel, out_shape=[pltpu.VMEM(forward.shape, bf16)...  3.39 us
    pallas_call x1, Pallas kernels, pack(): pl.pallas_call(partial(pack_kernel, places), out_shape=[pltpu.VMEM((FIELD...  1.38 us
  transfers between devices with their start and end apart: 14, of which 6 were waited for; matrix products, arithmetic and copies ran while one was open for 0% of the time, Pallas kernels for 15%

profile of v6, /device:TPU:0, one launch (start us, length us, event | category | flops | bytes accessed | tf_op | source)
XLA Modules:
  0.0 39.3 jit_solution(1626969451842537387)
XLA Ops:
  0.6 1.4 %pack.1 = (bf16[640,128]{1,0:T(8,128)(2,1)S(1)}, bf16[640,128]{1,0:T(8,128)(2,1)S(1)}, bf16[640,128]{1,0:T(8,128)(2,1)S(1)}, bf16[640,128]{1,0:T(8,128)(2,1)S(1)...) custom-call(s32[1]{0:T(128)} %bitcast.me_ref, ...), custom_call_target="tpu_custom_call" | custom-call | tf_op jit(solution)/shard_map/pack/pallas_call | solution.py:633
  2.0 4.0 %collective-permute-start = (bf16[640,128]{1,0:T(8,128)(2,1)S(1)}, bf16[640,128]{1,0:T(8,128)(2,1)S(1)}, u32[]{:S(2)}, u32[]{:S(2)}) collective-permute-start(bf16[640,128]{1,0:T(8,128)(2,1)S(1)} %get-tuple-element.39), channel_id=1, source_target_pairs={{0,24},{4,28},{8,16},{12,20},{16,8},{20,12},{24,0},{28,4},{1,25},{... | collective-permute-start | bytes 491528 | tf_op jit(solution)/shard_map/ppermute | solution.py:613
  6.0 0.5 %collective-permute-start.1 = (bf16[640,128]{1,0:T(8,128)(2,1)S(1)}, bf16[640,128]{1,0:T(8,128)(2,1)S(1)}, u32[]{:S(2)}, u32[]{:S(2)}) collective-permute-start(bf16[640,128]{1,0:T(8,128)(2,1)S(1)} %get-tuple-element.44), channel_id=1, source_target_pairs={{0,8},{4,12},{8,0},{12,4},{16,24},{20,28},{24,16},{28,20},{1,9},{5... | collective-permute-start | bytes 491528 | tf_op jit(solution)/shard_map/ppermute | solution.py:613
  6.6 0.5 %collective-permute-start.3 = (bf16[640,128]{1,0:T(8,128)(2,1)S(1)}, bf16[640,128]{1,0:T(8,128)(2,1)S(1)}, u32[]{:S(2)}, u32[]{:S(2)}) collective-permute-start(bf16[640,128]{1,0:T(8,128)(2,1)S(1)} %get-tuple-element.46), channel_id=1, source_target_pairs={{0,20},{4,16},{8,28},{12,24},{16,4},{20,0},{24,12},{28,8},{1,21},{... | collective-permute-start | bytes 491528 | tf_op jit(solution)/shard_map/ppermute | solution.py:613
  7.1 2.6 %collective-permute-start.4 = (bf16[640,128]{1,0:T(8,128)(2,1)S(1)}, bf16[640,128]{1,0:T(8,128)(2,1)S(1)}, u32[]{:S(2)}, u32[]{:S(2)}) collective-permute-start(bf16[640,128]{1,0:T(8,128)(2,1)S(1)} %get-tuple-element.47), channel_id=1, source_target_pairs={{0,12},{4,8},{8,4},{12,0},{16,28},{20,24},{24,20},{28,16},{1,13},{... | collective-permute-start | bytes 491528 | tf_op jit(solution)/shard_map/ppermute | solution.py:613
  9.8 1.3 %collective-permute-done._.refs_1_ = bf16[640,128]{1,0:T(8,128)(2,1)S(1)} collective-permute-done((bf16[640,128]{1,0:T(8,128)(2,1)S(1)}, bf16[640,128]{1,0:T(8,128)(2,1)S(1)}, u32[]{:S(2)}, u32[]{:S(2)}) %collective-permute-start) | collective-permute-done | bytes 163872 | tf_op jit(solution)/shard_map/ppermute | solution.py:613
  11.0 0.4 %collective-permute-start.5 = (bf16[640,128]{1,0:T(8,128)(2,1)S(1)}, bf16[640,128]{1,0:T(8,128)(2,1)S(1)}, u32[]{:S(2)}, u32[]{:S(2)}) collective-permute-start(bf16[640,128]{1,0:T(8,128)(2,1)S(1)} %get-tuple-element.48), channel_id=1, source_target_pairs={{0,28},{4,24},{8,20},{12,16},{16,12},{20,8},{24,4},{28,0},{1,29},{... | collective-permute-start | bytes 491528 | tf_op jit(solution)/shard_map/ppermute | solution.py:613
  11.4 3.7 %collective-permute-done.1.refs_2_ = bf16[640,128]{1,0:T(8,128)(2,1)S(1)} collective-permute-done((bf16[640,128]{1,0:T(8,128)(2,1)S(1)}, bf16[640,128]{1,0:T(8,128)(2,1)S(1)}, u32[]{:S(2)}, u32[]{:S(2)}) %collective-permute-start.1) | collective-permute-done | bytes 163872 | tf_op jit(solution)/shard_map/ppermute | solution.py:613
  15.1 0.7 %copy-done = bf16[3,3,1024]{2,1,0:T(4,128)(2,1)S(1)} copy-done((bf16[3,3,1024]{2,1,0:T(4,128)(2,1)S(1)}, bf16[3,3,1024]{2,1,0:T(4,128)(2,1)}, u32[]{:S(2)}) %copy-start) | copy-done | bytes 18456
  15.9 3.4 %prepare.1 = (bf16[2,8,256,256]{3,2,1,0:T(8,128)(2,1)S(1)}, bf16[2,8,256,256]{3,2,1,0:T(8,128)(2,1)S(1)}, f32[16,128]{1,0:T(8,128)S(1)}, f32[16,1024]{1,0:T(8,128)S(1)}, f32[4,128,1024]{2,1,0:T(8,128)S(1)}) custom-call(s32[1]{0:T(128)} %bitcast.me_ref, bf16[2,8,256,256]{3,2,1,0:T(8,128)(2,1)} %constant.10.clone.forward_any, ...), custom_call_target="tpu_custom_call" | custom-call | tf_op jit(solution)/shard_map/prepare/pallas_call | solution.py:650
  19.3 0.7 %collective-permute-done.5.refs_6_ = bf16[640,128]{1,0:T(8,128)(2,1)S(1)} collective-permute-done((bf16[640,128]{1,0:T(8,128)(2,1)S(1)}, bf16[640,128]{1,0:T(8,128)(2,1)S(1)}, u32[]{:S(2)}, u32[]{:S(2)}) %collective-permute-start.5) | collective-permute-done | bytes 163872 | tf_op jit(solution)/shard_map/ppermute | solution.py:613
  20.0 5.5 %layer.1 = (bf16[416,128]{1,0:T(8,128)(2,1)S(1)}, bf16[416,128]{1,0:T(8,128)(2,1)S(1)}, bf16[416,128]{1,0:T(8,128)(2,1)S(1)}, bf16[416,128]{1,0:T(8,128)(2,1)S(1...) custom-call(s32[1]{0:T(128)} %bitcast.me_ref, ...), custom_call_target="tpu_custom_call" | custom-call | tf_op jit(solution)/shard_map/layer/pallas_call | solution.py:666
  25.5 2.3 %collective-permute-start.11 = (bf16[416,128]{1,0:T(8,128)(2,1)S(1)}, bf16[416,128]{1,0:T(8,128)(2,1)S(1)}, u32[]{:S(2)}, u32[]{:S(2)}) collective-permute-start(bf16[416,128]{1,0:T(8,128)(2,1)S(1)} %get-tuple-element.57), channel_id=1, source_target_pairs={{0,24},{4,28},{8,16},{12,20},{16,8},{20,12},{24,0},{28,4},{1,25},{... | collective-permute-start | bytes 319496 | tf_op jit(solution)/shard_map/ppermute | solution.py:613
  27.8 0.8 %collective-permute-start.12 = (bf16[416,128]{1,0:T(8,128)(2,1)S(1)}, bf16[416,128]{1,0:T(8,128)(2,1)S(1)}, u32[]{:S(2)}, u32[]{:S(2)}) collective-permute-start(bf16[416,128]{1,0:T(8,128)(2,1)S(1)} %get-tuple-element.58), channel_id=1, source_target_pairs={{0,20},{4,16},{8,28},{12,24},{16,4},{20,0},{24,12},{28,8},{1,21},{... | collective-permute-start | bytes 319496 | tf_op jit(solution)/shard_map/ppermute | solution.py:613
  28.6 0.4 %collective-permute-start.13 = (bf16[416,128]{1,0:T(8,128)(2,1)S(1)}, bf16[416,128]{1,0:T(8,128)(2,1)S(1)}, u32[]{:S(2)}, u32[]{:S(2)}) collective-permute-start(bf16[416,128]{1,0:T(8,128)(2,1)S(1)} %get-tuple-element.59), channel_id=1, source_target_pairs={{0,8},{4,12},{8,0},{12,4},{16,24},{20,28},{24,16},{28,20},{1,9},{5... | collective-permute-start | bytes 319496 | tf_op jit(solution)/shard_map/ppermute | solution.py:613
  29.0 1.6 %collective-permute-start.9 = (bf16[416,128]{1,0:T(8,128)(2,1)S(1)}, bf16[416,128]{1,0:T(8,128)(2,1)S(1)}, u32[]{:S(2)}, u32[]{:S(2)}) collective-permute-start(bf16[416,128]{1,0:T(8,128)(2,1)S(1)} %get-tuple-element.54), channel_id=1, source_target_pairs={{0,16},{4,20},{8,24},{12,28},{16,0},{20,4},{24,8},{28,12},{1,17},{... | collective-permute-start | bytes 319496 | tf_op jit(solution)/shard_map/ppermute | solution.py:613
  30.7 0.4 collective-permute-start.10
  31.0 1.0 %collective-permute-done.11.refs_1_ = bf16[416,128]{1,0:T(8,128)(2,1)S(1)} collective-permute-done((bf16[416,128]{1,0:T(8,128)(2,1)S(1)}, bf16[416,128]{1,0:T(8,128)(2,1)S(1)}, u32[]{:S(2)}, u32[]{:S(2)}) %collective-permute-start.11) | collective-permute-done | bytes 106528 | tf_op jit(solution)/shard_map/ppermute | solution.py:613
  32.0 2.3 %collective-permute-start.7 = (bf16[416,128]{1,0:T(8,128)(2,1)S(1)}, bf16[416,128]{1,0:T(8,128)(2,1)S(1)}, u32[]{:S(2)}, u32[]{:S(2)}) collective-permute-start(bf16[416,128]{1,0:T(8,128)(2,1)S(1)} %get-tuple-element.50), channel_id=1, source_target_pairs={{0,28},{4,24},{8,20},{12,16},{16,12},{20,8},{24,4},{28,0},{1,29},{... | collective-permute-start | bytes 319496 | tf_op jit(solution)/shard_map/ppermute | solution.py:613
  34.3 0.5 %collective-permute-start.8 = (bf16[416,128]{1,0:T(8,128)(2,1)S(1)}, bf16[416,128]{1,0:T(8,128)(2,1)S(1)}, u32[]{:S(2)}, u32[]{:S(2)}) collective-permute-start(bf16[416,128]{1,0:T(8,128)(2,1)S(1)} %get-tuple-element.51), channel_id=1, source_target_pairs={{0,4},{4,0},{8,12},{12,8},{16,20},{20,16},{24,28},{28,24},{1,5},{5... | collective-permute-start | bytes 319496 | tf_op jit(solution)/shard_map/ppermute | solution.py:613
  34.8 1.5 %finish.3 = (bf16[128,1024]{1,0:T(8,128)(2,1)}, bf16[128,1024]{1,0:T(8,128)(2,1)}, bf16[128,1024]{1,0:T(8,128)(2,1)}, bf16[128,1024]{1,0:T(8,128)(2,1)}, f32[128,1024]{1,0:T(8,128)}, /*index=5*/f32[3,3,1024]{2,1,0:T(4,128)}) custom-call(s32[1]{0:T(128)} %bitcast.me_ref, bf16[416,128]{1,0:T(8,128)(2,1)S(1)} %get-tuple-element.56.refs_0_, ...), custom_call_target="tpu_custom_call" | custom-call | tf_op jit(solution)/shard_map/finish/pallas_call | solution.py:696
  36.3 0.7 %collective-permute-done.9.refs_0_ = bf16[416,128]{1,0:T(8,128)(2,1)S(1)} collective-permute-done((bf16[416,128]{1,0:T(8,128)(2,1)S(1)}, bf16[416,128]{1,0:T(8,128)(2,1)S(1)}, u32[]{:S(2)}, u32[]{:S(2)}) %collective-permute-start.9) | collective-permute-done | bytes 106528 | tf_op jit(solution)/shard_map/ppermute | solution.py:613
  37.0 1.1 %finish.4 = (bf16[128,1024]{1,0:T(8,128)(2,1)}, bf16[128,1024]{1,0:T(8,128)(2,1)}, bf16[128,1024]{1,0:T(8,128)(2,1)}, bf16[128,1024]{1,0:T(8,128)(2,1)}, f32[128,1024]{1,0:T(8,128)}, /*index=5*/f32[3,3,1024]{2,1,0:T(4,128)}) custom-call(s32[1]{0:T(128)} %bitcast.me_ref, ...), custom_call_target="tpu_custom_call", output_to_operand_aliasing={{0}: (5, {}), {1}: (6, {}), {2}: (7, {}), {3}: (8, {}), {4}... | custom-call | tf_op jit(solution)/shard_map/finish/pallas_call | solution.py:696
  38.3 1.1 %finish.5 = (bf16[128,1024]{1,0:T(8,128)(2,1)}, bf16[128,1024]{1,0:T(8,128)(2,1)}, bf16[128,1024]{1,0:T(8,128)(2,1)}, bf16[128,1024]{1,0:T(8,128)(2,1)}, f32[128,1024]{1,0:T(8,128)}, /*index=5*/f32[3,3,1024]{2,1,0:T(4,128)}) custom-call(s32[1]{0:T(128)} %bitcast.me_ref, ...), custom_call_target="tpu_custom_call", output_to_operand_aliasing={{0}: (5, {}), {1}: (6, {}), {2}: (7, {}), {3}: (8, {}), {4}... | custom-call | tf_op jit(solution)/shard_map/finish/pallas_call | solution.py:696
  (12 shorter events, 0.3 us)
Async XLA Ops:
  2.0 9.0 %collective-permute-start = (bf16[640,128]{1,0:T(8,128)(2,1)S(1)}, bf16[640,128]{1,0:T(8,128)(2,1)S(1)}, u32[]{:S(2)}, u32[]{:S(2)}) collective-permute-start(bf16[640,128]{1,0:T(8,128)(2,1)S(1)} %get-tuple-element.39), channel_id=1, source_target_pairs={{0,24},{4,28},{8,16},{12,20},{16,8},{20,12},{24,0},{28,4},{1,25},{... | collective-permute-start | bytes 491528 | tf_op jit(solution)/shard_map/ppermute | solution.py:613
  6.0 9.1 %collective-permute-start.1 = (bf16[640,128]{1,0:T(8,128)(2,1)S(1)}, bf16[640,128]{1,0:T(8,128)(2,1)S(1)}, u32[]{:S(2)}, u32[]{:S(2)}) collective-permute-start(bf16[640,128]{1,0:T(8,128)(2,1)S(1)} %get-tuple-element.44), channel_id=1, source_target_pairs={{0,8},{4,12},{8,0},{12,4},{16,24},{20,28},{24,16},{28,20},{1,9},{5... | collective-permute-start | bytes 491528 | tf_op jit(solution)/shard_map/ppermute | solution.py:613
  6.5 12.8 %collective-permute-start.2 = (bf16[640,128]{1,0:T(8,128)(2,1)S(1)}, bf16[640,128]{1,0:T(8,128)(2,1)S(1)}, u32[]{:S(2)}, u32[]{:S(2)}) collective-permute-start(bf16[640,128]{1,0:T(8,128)(2,1)S(1)} %get-tuple-element.45), channel_id=1, source_target_pairs={{0,16},{4,20},{8,24},{12,28},{16,0},{20,4},{24,8},{28,12},{1,17},{... | collective-permute-start | bytes 491528 | tf_op jit(solution)/shard_map/ppermute | solution.py:613
  6.6 12.7 %collective-permute-start.3 = (bf16[640,128]{1,0:T(8,128)(2,1)S(1)}, bf16[640,128]{1,0:T(8,128)(2,1)S(1)}, u32[]{:S(2)}, u32[]{:S(2)}) collective-permute-start(bf16[640,128]{1,0:T(8,128)(2,1)S(1)} %get-tuple-element.46), channel_id=1, source_target_pairs={{0,20},{4,16},{8,28},{12,24},{16,4},{20,0},{24,12},{28,8},{1,21},{... | collective-permute-start | bytes 491528 | tf_op jit(solution)/shard_map/ppermute | solution.py:613
  7.1 12.2 %collective-permute-start.4 = (bf16[640,128]{1,0:T(8,128)(2,1)S(1)}, bf16[640,128]{1,0:T(8,128)(2,1)S(1)}, u32[]{:S(2)}, u32[]{:S(2)}) collective-permute-start(bf16[640,128]{1,0:T(8,128)(2,1)S(1)} %get-tuple-element.47), channel_id=1, source_target_pairs={{0,12},{4,8},{8,4},{12,0},{16,28},{20,24},{24,20},{28,16},{1,13},{... | collective-permute-start | bytes 491528 | tf_op jit(solution)/shard_map/ppermute | solution.py:613
  11.0 9.0 %collective-permute-start.5 = (bf16[640,128]{1,0:T(8,128)(2,1)S(1)}, bf16[640,128]{1,0:T(8,128)(2,1)S(1)}, u32[]{:S(2)}, u32[]{:S(2)}) collective-permute-start(bf16[640,128]{1,0:T(8,128)(2,1)S(1)} %get-tuple-element.48), channel_id=1, source_target_pairs={{0,28},{4,24},{8,20},{12,16},{16,12},{20,8},{24,4},{28,0},{1,29},{... | collective-permute-start | bytes 491528 | tf_op jit(solution)/shard_map/ppermute | solution.py:613
  15.1 4.9 %collective-permute-start.6 = (bf16[640,128]{1,0:T(8,128)(2,1)S(1)}, bf16[640,128]{1,0:T(8,128)(2,1)S(1)}, u32[]{:S(2)}, u32[]{:S(2)}) collective-permute-start(bf16[640,128]{1,0:T(8,128)(2,1)S(1)} %get-tuple-element.49), channel_id=1, source_target_pairs={{0,4},{4,0},{8,12},{12,8},{16,20},{20,16},{24,28},{28,24},{1,5},{5... | collective-permute-start | bytes 491528 | tf_op jit(solution)/shard_map/ppermute | solution.py:613
  15.1 0.7 %copy-start = (bf16[3,3,1024]{2,1,0:T(4,128)(2,1)S(1)}, bf16[3,3,1024]{2,1,0:T(4,128)(2,1)}, u32[]{:S(2)}) copy-start(bf16[3,3,1024]{2,1,0:T(4,128)(2,1)} %taps_any.1) | copy-start | bytes 55300
  25.5 6.5 %collective-permute-start.11 = (bf16[416,128]{1,0:T(8,128)(2,1)S(1)}, bf16[416,128]{1,0:T(8,128)(2,1)S(1)}, u32[]{:S(2)}, u32[]{:S(2)}) collective-permute-start(bf16[416,128]{1,0:T(8,128)(2,1)S(1)} %get-tuple-element.57), channel_id=1, source_target_pairs={{0,24},{4,28},{8,16},{12,20},{16,8},{20,12},{24,0},{28,4},{1,25},{... | collective-permute-start | bytes 319496 | tf_op jit(solution)/shard_map/ppermute | solution.py:613
  27.8 6.5 %collective-permute-start.12 = (bf16[416,128]{1,0:T(8,128)(2,1)S(1)}, bf16[416,128]{1,0:T(8,128)(2,1)S(1)}, u32[]{:S(2)}, u32[]{:S(2)}) collective-permute-start(bf16[416,128]{1,0:T(8,128)(2,1)S(1)} %get-tuple-element.58), channel_id=1, source_target_pairs={{0,20},{4,16},{8,28},{12,24},{16,4},{20,0},{24,12},{28,8},{1,21},{... | collective-permute-start | bytes 319496 | tf_op jit(solution)/shard_map/ppermute | solution.py:613
  28.6 6.2 %collective-permute-start.13 = (bf16[416,128]{1,0:T(8,128)(2,1)S(1)}, bf16[416,128]{1,0:T(8,128)(2,1)S(1)}, u32[]{:S(2)}, u32[]{:S(2)}) collective-permute-start(bf16[416,128]{1,0:T(8,128)(2,1)S(1)} %get-tuple-element.59), channel_id=1, source_target_pairs={{0,8},{4,12},{8,0},{12,4},{16,24},{20,28},{24,16},{28,20},{1,9},{5... | collective-permute-start | bytes 319496 | tf_op jit(solution)/shard_map/ppermute | solution.py:613
  29.0 8.0 %collective-permute-start.9 = (bf16[416,128]{1,0:T(8,128)(2,1)S(1)}, bf16[416,128]{1,0:T(8,128)(2,1)S(1)}, u32[]{:S(2)}, u32[]{:S(2)}) collective-permute-start(bf16[416,128]{1,0:T(8,128)(2,1)S(1)} %get-tuple-element.54), channel_id=1, source_target_pairs={{0,16},{4,20},{8,24},{12,28},{16,0},{20,4},{24,8},{28,12},{1,17},{... | collective-permute-start | bytes 319496 | tf_op jit(solution)/shard_map/ppermute | solution.py:613
  30.7 6.3 %collective-permute-start.10 = (bf16[416,128]{1,0:T(8,128)(2,1)S(1)}, bf16[416,128]{1,0:T(8,128)(2,1)S(1)}, u32[]{:S(2)}, u32[]{:S(2)}) collective-permute-start(bf16[416,128]{1,0:T(8,128)(2,1)S(1)} %get-tuple-element.55), channel_id=1, source_target_pairs={{0,12},{4,8},{8,4},{12,0},{16,28},{20,24},{24,20},{28,16},{1,13},{... | collective-permute-start | bytes 319496 | tf_op jit(solution)/shard_map/ppermute | solution.py:613
  32.0 6.2 %collective-permute-start.7 = (bf16[416,128]{1,0:T(8,128)(2,1)S(1)}, bf16[416,128]{1,0:T(8,128)(2,1)S(1)}, u32[]{:S(2)}, u32[]{:S(2)}) collective-permute-start(bf16[416,128]{1,0:T(8,128)(2,1)S(1)} %get-tuple-element.50), channel_id=1, source_target_pairs={{0,28},{4,24},{8,20},{12,16},{16,12},{20,8},{24,4},{28,0},{1,29},{... | collective-permute-start | bytes 319496 | tf_op jit(solution)/shard_map/ppermute | solution.py:613
  34.3 3.9 %collective-permute-start.8 = (bf16[416,128]{1,0:T(8,128)(2,1)S(1)}, bf16[416,128]{1,0:T(8,128)(2,1)S(1)}, u32[]{:S(2)}, u32[]{:S(2)}) collective-permute-start(bf16[416,128]{1,0:T(8,128)(2,1)S(1)} %get-tuple-element.51), channel_id=1, source_target_pairs={{0,4},{4,0},{8,12},{12,8},{16,20},{20,16},{24,28},{28,24},{1,5},{5... | collective-permute-start | bytes 319496 | tf_op jit(solution)/shard_map/ppermute | solution.py:613

commit v7 on v6

--- a/solution.py
+++ b/solution.py
@@ -562,10 +562,19 @@
         conv, mixed_grad, filt = [
             log_decode(got_ref[pl.ds(c * rows, rows), :], head[6 + c : 7 + c]) for c in range(3)
         ]
+
+        def store(c):
+            source = stage.at[n, c] if c < 4 else (stage_filter, stage_taps)[c - 4].at[n]
+            target = outs[c].at[:, lanes] if c < 5 else outs[c].at[:, :, lanes]
+            copies.append(pltpu.make_async_copy(source, target, sem.at[len(copies)]))
+            copies[-1].start()
+
         stage_filter[n] = filt * (1.0 / math.sqrt(RADIX * rows))
+        store(4)
         pairs = head[16:22] + head[22:28]
         for c, at in enumerate(TAPS_AT):
             stage_taps[n, c // 3, c % 3 : c % 3 + 1, :] = log_decode(head[at : at + 1], head[9:10])
+        store(5)
         line = lax.broadcasted_iota(jnp.int32, (PAD, LANES), 0)
         filtered = []
         gain = []
@@ -579,6 +588,7 @@
             )
             filtered.append(jnp.concatenate([top, early_ref[i, PAD:, lanes]], axis=0))
         stage[n, 0] = (filtered[0] * conv).astype(bf16)
+        store(0)
         inner = (
             conv * early_ref[3, :, lanes],
             mixed_grad * filtered[2],
@@ -592,11 +602,7 @@
                 + gain[i][1] * grads[i, pl.ds(1, rows), :]
                 + gain[i][2] * grads[i, pl.ds(2, rows), :]
             ).astype(bf16)
-        for c, out in enumerate(outs):
-            source = stage.at[n, c] if c < 4 else (stage_filter, stage_taps)[c - 4].at[n]
-            target = out.at[:, lanes] if c < 5 else out.at[:, :, lanes]
-            copies.append(pltpu.make_async_copy(source, target, sem.at[len(copies)]))
-            copies[-1].start()
+            store(1 + i)
     return copies
 
 

time: 39.6 us -> 39.5 us (level)
  no operation moved by 1% of the time
where the time goes in v7:
time: 39.5 us; the launch traced here: 39.3 us
  starting transfers between devices  16.4 us (42%)
  Pallas kernels  13.7 us (35%)
  waiting for transfers between devices  7.71 us (20%)
  local copies, waits for them, and re-layouts  0.74 us (2%)
  between operations  0.71 us (2%)
    ppermute x14, starting transfers between devices, swap_blocks(): lax.ppermute(block, 'ctx', [(i, i ^ k) for i in devices])  16.4 us
    ppermute x14, waiting for transfers between devices, swap_blocks(): lax.ppermute(block, 'ctx', [(i, i ^ k) for i in devices])  7.71 us
    pallas_call x1, Pallas kernels, local_fast(): pl.pallas_call(layer_kernel, out_shape=[pltpu.VMEM((3 * rows + HEAD, LANE...  5.51 us
    pallas_call x3, Pallas kernels, local_fast(): pl.pallas_call(partial(finish_kernel, BACK[first:last], len(begun)), out_...  3.44 us
    pallas_call x1, Pallas kernels, local_fast(): pl.pallas_call(prepare_kernel, out_shape=[pltpu.VMEM(forward.shape, bf16)...  3.39 us
    pallas_call x1, Pallas kernels, pack(): pl.pallas_call(partial(pack_kernel, places), out_shape=[pltpu.VMEM((FIELD...  1.38 us
  transfers between devices with their start and end apart: 14, of which 6 were waited for; matrix products, arithmetic and copies ran while one was open for 0% of the time, Pallas kernels for 15%

profile of v7, /device:TPU:0, one launch (start us, length us, event | category | flops | bytes accessed | tf_op | source)
XLA Modules:
  0.0 39.3 jit_solution(10606052653297974529)
XLA Ops:
  0.6 1.4 %pack.1 = (bf16[640,128]{1,0:T(8,128)(2,1)S(1)}, bf16[640,128]{1,0:T(8,128)(2,1)S(1)}, bf16[640,128]{1,0:T(8,128)(2,1)S(1)}, bf16[640,128]{1,0:T(8,128)(2,1)S(1)...) custom-call(s32[1]{0:T(128)} %bitcast.me_ref, ...), custom_call_target="tpu_custom_call" | custom-call | tf_op jit(solution)/shard_map/pack/pallas_call | solution.py:639
  2.0 4.0 %collective-permute-start = (bf16[640,128]{1,0:T(8,128)(2,1)S(1)}, bf16[640,128]{1,0:T(8,128)(2,1)S(1)}, u32[]{:S(2)}, u32[]{:S(2)}) collective-permute-start(bf16[640,128]{1,0:T(8,128)(2,1)S(1)} %get-tuple-element.39), channel_id=1, source_target_pairs={{0,24},{4,28},{8,16},{12,20},{16,8},{20,12},{24,0},{28,4},{1,25},{... | collective-permute-start | bytes 491528 | tf_op jit(solution)/shard_map/ppermute | solution.py:619
  6.0 0.5 %collective-permute-start.1 = (bf16[640,128]{1,0:T(8,128)(2,1)S(1)}, bf16[640,128]{1,0:T(8,128)(2,1)S(1)}, u32[]{:S(2)}, u32[]{:S(2)}) collective-permute-start(bf16[640,128]{1,0:T(8,128)(2,1)S(1)} %get-tuple-element.44), channel_id=1, source_target_pairs={{0,8},{4,12},{8,0},{12,4},{16,24},{20,28},{24,16},{28,20},{1,9},{5... | collective-permute-start | bytes 491528 | tf_op jit(solution)/shard_map/ppermute | solution.py:619
  6.6 0.5 %collective-permute-start.3 = (bf16[640,128]{1,0:T(8,128)(2,1)S(1)}, bf16[640,128]{1,0:T(8,128)(2,1)S(1)}, u32[]{:S(2)}, u32[]{:S(2)}) collective-permute-start(bf16[640,128]{1,0:T(8,128)(2,1)S(1)} %get-tuple-element.46), channel_id=1, source_target_pairs={{0,20},{4,16},{8,28},{12,24},{16,4},{20,0},{24,12},{28,8},{1,21},{... | collective-permute-start | bytes 491528 | tf_op jit(solution)/shard_map/ppermute | solution.py:619
  7.1 2.6 %collective-permute-start.4 = (bf16[640,128]{1,0:T(8,128)(2,1)S(1)}, bf16[640,128]{1,0:T(8,128)(2,1)S(1)}, u32[]{:S(2)}, u32[]{:S(2)}) collective-permute-start(bf16[640,128]{1,0:T(8,128)(2,1)S(1)} %get-tuple-element.47), channel_id=1, source_target_pairs={{0,12},{4,8},{8,4},{12,0},{16,28},{20,24},{24,20},{28,16},{1,13},{... | collective-permute-start | bytes 491528 | tf_op jit(solution)/shard_map/ppermute | solution.py:619
  9.8 1.3 %collective-permute-done._.refs_1_ = bf16[640,128]{1,0:T(8,128)(2,1)S(1)} collective-permute-done((bf16[640,128]{1,0:T(8,128)(2,1)S(1)}, bf16[640,128]{1,0:T(8,128)(2,1)S(1)}, u32[]{:S(2)}, u32[]{:S(2)}) %collective-permute-start) | collective-permute-done | bytes 163872 | tf_op jit(solution)/shard_map/ppermute | solution.py:619
  11.0 0.4 %collective-permute-start.5 = (bf16[640,128]{1,0:T(8,128)(2,1)S(1)}, bf16[640,128]{1,0:T(8,128)(2,1)S(1)}, u32[]{:S(2)}, u32[]{:S(2)}) collective-permute-start(bf16[640,128]{1,0:T(8,128)(2,1)S(1)} %get-tuple-element.48), channel_id=1, source_target_pairs={{0,28},{4,24},{8,20},{12,16},{16,12},{20,8},{24,4},{28,0},{1,29},{... | collective-permute-start | bytes 491528 | tf_op jit(solution)/shard_map/ppermute | solution.py:619
  11.4 3.7 %collective-permute-done.1.refs_2_ = bf16[640,128]{1,0:T(8,128)(2,1)S(1)} collective-permute-done((bf16[640,128]{1,0:T(8,128)(2,1)S(1)}, bf16[640,128]{1,0:T(8,128)(2,1)S(1)}, u32[]{:S(2)}, u32[]{:S(2)}) %collective-permute-start.1) | collective-permute-done | bytes 163872 | tf_op jit(solution)/shard_map/ppermute | solution.py:619
  15.1 0.7 %copy-done = bf16[3,3,1024]{2,1,0:T(4,128)(2,1)S(1)} copy-done((bf16[3,3,1024]{2,1,0:T(4,128)(2,1)S(1)}, bf16[3,3,1024]{2,1,0:T(4,128)(2,1)}, u32[]{:S(2)}) %copy-start) | copy-done | bytes 18456
  15.9 3.4 %prepare.1 = (bf16[2,8,256,256]{3,2,1,0:T(8,128)(2,1)S(1)}, bf16[2,8,256,256]{3,2,1,0:T(8,128)(2,1)S(1)}, f32[16,128]{1,0:T(8,128)S(1)}, f32[16,1024]{1,0:T(8,128)S(1)}, f32[4,128,1024]{2,1,0:T(8,128)S(1)}) custom-call(s32[1]{0:T(128)} %bitcast.me_ref, bf16[2,8,256,256]{3,2,1,0:T(8,128)(2,1)} %constant.10.clone.forward_any, ...), custom_call_target="tpu_custom_call" | custom-call | tf_op jit(solution)/shard_map/prepare/pallas_call | solution.py:656
  19.3 0.7 %collective-permute-done.5.refs_6_ = bf16[640,128]{1,0:T(8,128)(2,1)S(1)} collective-permute-done((bf16[640,128]{1,0:T(8,128)(2,1)S(1)}, bf16[640,128]{1,0:T(8,128)(2,1)S(1)}, u32[]{:S(2)}, u32[]{:S(2)}) %collective-permute-start.5) | collective-permute-done | bytes 163872 | tf_op jit(solution)/shard_map/ppermute | solution.py:619
  20.0 5.5 %layer.1 = (bf16[416,128]{1,0:T(8,128)(2,1)S(1)}, bf16[416,128]{1,0:T(8,128)(2,1)S(1)}, bf16[416,128]{1,0:T(8,128)(2,1)S(1)}, bf16[416,128]{1,0:T(8,128)(2,1)S(1...) custom-call(s32[1]{0:T(128)} %bitcast.me_ref, ...), custom_call_target="tpu_custom_call" | custom-call | tf_op jit(solution)/shard_map/layer/pallas_call | solution.py:672
  25.5 2.3 %collective-permute-start.11 = (bf16[416,128]{1,0:T(8,128)(2,1)S(1)}, bf16[416,128]{1,0:T(8,128)(2,1)S(1)}, u32[]{:S(2)}, u32[]{:S(2)}) collective-permute-start(bf16[416,128]{1,0:T(8,128)(2,1)S(1)} %get-tuple-element.57), channel_id=1, source_target_pairs={{0,24},{4,28},{8,16},{12,20},{16,8},{20,12},{24,0},{28,4},{1,25},{... | collective-permute-start | bytes 319496 | tf_op jit(solution)/shard_map/ppermute | solution.py:619
  27.8 0.8 %collective-permute-start.12 = (bf16[416,128]{1,0:T(8,128)(2,1)S(1)}, bf16[416,128]{1,0:T(8,128)(2,1)S(1)}, u32[]{:S(2)}, u32[]{:S(2)}) collective-permute-start(bf16[416,128]{1,0:T(8,128)(2,1)S(1)} %get-tuple-element.58), channel_id=1, source_target_pairs={{0,20},{4,16},{8,28},{12,24},{16,4},{20,0},{24,12},{28,8},{1,21},{... | collective-permute-start | bytes 319496 | tf_op jit(solution)/shard_map/ppermute | solution.py:619
  28.6 0.4 %collective-permute-start.13 = (bf16[416,128]{1,0:T(8,128)(2,1)S(1)}, bf16[416,128]{1,0:T(8,128)(2,1)S(1)}, u32[]{:S(2)}, u32[]{:S(2)}) collective-permute-start(bf16[416,128]{1,0:T(8,128)(2,1)S(1)} %get-tuple-element.59), channel_id=1, source_target_pairs={{0,8},{4,12},{8,0},{12,4},{16,24},{20,28},{24,16},{28,20},{1,9},{5... | collective-permute-start | bytes 319496 | tf_op jit(solution)/shard_map/ppermute | solution.py:619
  29.0 1.6 %collective-permute-start.9 = (bf16[416,128]{1,0:T(8,128)(2,1)S(1)}, bf16[416,128]{1,0:T(8,128)(2,1)S(1)}, u32[]{:S(2)}, u32[]{:S(2)}) collective-permute-start(bf16[416,128]{1,0:T(8,128)(2,1)S(1)} %get-tuple-element.54), channel_id=1, source_target_pairs={{0,16},{4,20},{8,24},{12,28},{16,0},{20,4},{24,8},{28,12},{1,17},{... | collective-permute-start | bytes 319496 | tf_op jit(solution)/shard_map/ppermute | solution.py:619
  30.7 0.4 collective-permute-start.10
  31.0 1.0 %collective-permute-done.11.refs_1_ = bf16[416,128]{1,0:T(8,128)(2,1)S(1)} collective-permute-done((bf16[416,128]{1,0:T(8,128)(2,1)S(1)}, bf16[416,128]{1,0:T(8,128)(2,1)S(1)}, u32[]{:S(2)}, u32[]{:S(2)}) %collective-permute-start.11) | collective-permute-done | bytes 106528 | tf_op jit(solution)/shard_map/ppermute | solution.py:619
  32.0 2.3 %collective-permute-start.7 = (bf16[416,128]{1,0:T(8,128)(2,1)S(1)}, bf16[416,128]{1,0:T(8,128)(2,1)S(1)}, u32[]{:S(2)}, u32[]{:S(2)}) collective-permute-start(bf16[416,128]{1,0:T(8,128)(2,1)S(1)} %get-tuple-element.50), channel_id=1, source_target_pairs={{0,28},{4,24},{8,20},{12,16},{16,12},{20,8},{24,4},{28,0},{1,29},{... | collective-permute-start | bytes 319496 | tf_op jit(solution)/shard_map/ppermute | solution.py:619
  34.3 0.5 %collective-permute-start.8 = (bf16[416,128]{1,0:T(8,128)(2,1)S(1)}, bf16[416,128]{1,0:T(8,128)(2,1)S(1)}, u32[]{:S(2)}, u32[]{:S(2)}) collective-permute-start(bf16[416,128]{1,0:T(8,128)(2,1)S(1)} %get-tuple-element.51), channel_id=1, source_target_pairs={{0,4},{4,0},{8,12},{12,8},{16,20},{20,16},{24,28},{28,24},{1,5},{5... | collective-permute-start | bytes 319496 | tf_op jit(solution)/shard_map/ppermute | solution.py:619
  34.8 1.4 %finish.3 = (bf16[128,1024]{1,0:T(8,128)(2,1)}, bf16[128,1024]{1,0:T(8,128)(2,1)}, bf16[128,1024]{1,0:T(8,128)(2,1)}, bf16[128,1024]{1,0:T(8,128)(2,1)}, f32[128,1024]{1,0:T(8,128)}, /*index=5*/f32[3,3,1024]{2,1,0:T(4,128)}) custom-call(s32[1]{0:T(128)} %bitcast.me_ref, bf16[416,128]{1,0:T(8,128)(2,1)S(1)} %get-tuple-element.56.refs_0_, ...), custom_call_target="tpu_custom_call" | custom-call | tf_op jit(solution)/shard_map/finish/pallas_call | solution.py:702
  36.2 0.8 %collective-permute-done.9.refs_0_ = bf16[416,128]{1,0:T(8,128)(2,1)S(1)} collective-permute-done((bf16[416,128]{1,0:T(8,128)(2,1)S(1)}, bf16[416,128]{1,0:T(8,128)(2,1)S(1)}, u32[]{:S(2)}, u32[]{:S(2)}) %collective-permute-start.9) | collective-permute-done | bytes 106528 | tf_op jit(solution)/shard_map/ppermute | solution.py:619
  37.0 1.0 %finish.4 = (bf16[128,1024]{1,0:T(8,128)(2,1)}, bf16[128,1024]{1,0:T(8,128)(2,1)}, bf16[128,1024]{1,0:T(8,128)(2,1)}, bf16[128,1024]{1,0:T(8,128)(2,1)}, f32[128,1024]{1,0:T(8,128)}, /*index=5*/f32[3,3,1024]{2,1,0:T(4,128)}) custom-call(s32[1]{0:T(128)} %bitcast.me_ref, ...), custom_call_target="tpu_custom_call", output_to_operand_aliasing={{0}: (5, {}), {1}: (6, {}), {2}: (7, {}), {3}: (8, {}), {4}... | custom-call | tf_op jit(solution)/shard_map/finish/pallas_call | solution.py:702
  38.3 1.0 %finish.5 = (bf16[128,1024]{1,0:T(8,128)(2,1)}, bf16[128,1024]{1,0:T(8,128)(2,1)}, bf16[128,1024]{1,0:T(8,128)(2,1)}, bf16[128,1024]{1,0:T(8,128)(2,1)}, f32[128,1024]{1,0:T(8,128)}, /*index=5*/f32[3,3,1024]{2,1,0:T(4,128)}) custom-call(s32[1]{0:T(128)} %bitcast.me_ref, ...), custom_call_target="tpu_custom_call", output_to_operand_aliasing={{0}: (5, {}), {1}: (6, {}), {2}: (7, {}), {3}: (8, {}), {4}... | custom-call | tf_op jit(solution)/shard_map/finish/pallas_call | solution.py:702
  (12 shorter events, 0.4 us)
Async XLA Ops:
  2.0 9.0 %collective-permute-start = (bf16[640,128]{1,0:T(8,128)(2,1)S(1)}, bf16[640,128]{1,0:T(8,128)(2,1)S(1)}, u32[]{:S(2)}, u32[]{:S(2)}) collective-permute-start(bf16[640,128]{1,0:T(8,128)(2,1)S(1)} %get-tuple-element.39), channel_id=1, source_target_pairs={{0,24},{4,28},{8,16},{12,20},{16,8},{20,12},{24,0},{28,4},{1,25},{... | collective-permute-start | bytes 491528 | tf_op jit(solution)/shard_map/ppermute | solution.py:619
  6.0 9.1 %collective-permute-start.1 = (bf16[640,128]{1,0:T(8,128)(2,1)S(1)}, bf16[640,128]{1,0:T(8,128)(2,1)S(1)}, u32[]{:S(2)}, u32[]{:S(2)}) collective-permute-start(bf16[640,128]{1,0:T(8,128)(2,1)S(1)} %get-tuple-element.44), channel_id=1, source_target_pairs={{0,8},{4,12},{8,0},{12,4},{16,24},{20,28},{24,16},{28,20},{1,9},{5... | collective-permute-start | bytes 491528 | tf_op jit(solution)/shard_map/ppermute | solution.py:619
  6.5 12.8 %collective-permute-start.2 = (bf16[640,128]{1,0:T(8,128)(2,1)S(1)}, bf16[640,128]{1,0:T(8,128)(2,1)S(1)}, u32[]{:S(2)}, u32[]{:S(2)}) collective-permute-start(bf16[640,128]{1,0:T(8,128)(2,1)S(1)} %get-tuple-element.45), channel_id=1, source_target_pairs={{0,16},{4,20},{8,24},{12,28},{16,0},{20,4},{24,8},{28,12},{1,17},{... | collective-permute-start | bytes 491528 | tf_op jit(solution)/shard_map/ppermute | solution.py:619
  6.6 12.7 %collective-permute-start.3 = (bf16[640,128]{1,0:T(8,128)(2,1)S(1)}, bf16[640,128]{1,0:T(8,128)(2,1)S(1)}, u32[]{:S(2)}, u32[]{:S(2)}) collective-permute-start(bf16[640,128]{1,0:T(8,128)(2,1)S(1)} %get-tuple-element.46), channel_id=1, source_target_pairs={{0,20},{4,16},{8,28},{12,24},{16,4},{20,0},{24,12},{28,8},{1,21},{... | collective-permute-start | bytes 491528 | tf_op jit(solution)/shard_map/ppermute | solution.py:619
  7.1 12.2 %collective-permute-start.4 = (bf16[640,128]{1,0:T(8,128)(2,1)S(1)}, bf16[640,128]{1,0:T(8,128)(2,1)S(1)}, u32[]{:S(2)}, u32[]{:S(2)}) collective-permute-start(bf16[640,128]{1,0:T(8,128)(2,1)S(1)} %get-tuple-element.47), channel_id=1, source_target_pairs={{0,12},{4,8},{8,4},{12,0},{16,28},{20,24},{24,20},{28,16},{1,13},{... | collective-permute-start | bytes 491528 | tf_op jit(solution)/shard_map/ppermute | solution.py:619
  11.0 9.0 %collective-permute-start.5 = (bf16[640,128]{1,0:T(8,128)(2,1)S(1)}, bf16[640,128]{1,0:T(8,128)(2,1)S(1)}, u32[]{:S(2)}, u32[]{:S(2)}) collective-permute-start(bf16[640,128]{1,0:T(8,128)(2,1)S(1)} %get-tuple-element.48), channel_id=1, source_target_pairs={{0,28},{4,24},{8,20},{12,16},{16,12},{20,8},{24,4},{28,0},{1,29},{... | collective-permute-start | bytes 491528 | tf_op jit(solution)/shard_map/ppermute | solution.py:619
  15.1 4.9 %collective-permute-start.6 = (bf16[640,128]{1,0:T(8,128)(2,1)S(1)}, bf16[640,128]{1,0:T(8,128)(2,1)S(1)}, u32[]{:S(2)}, u32[]{:S(2)}) collective-permute-start(bf16[640,128]{1,0:T(8,128)(2,1)S(1)} %get-tuple-element.49), channel_id=1, source_target_pairs={{0,4},{4,0},{8,12},{12,8},{16,20},{20,16},{24,28},{28,24},{1,5},{5... | collective-permute-start | bytes 491528 | tf_op jit(solution)/shard_map/ppermute | solution.py:619
  15.1 0.7 %copy-start = (bf16[3,3,1024]{2,1,0:T(4,128)(2,1)S(1)}, bf16[3,3,1024]{2,1,0:T(4,128)(2,1)}, u32[]{:S(2)}) copy-start(bf16[3,3,1024]{2,1,0:T(4,128)(2,1)} %taps_any.1) | copy-start | bytes 55300
  25.5 6.5 %collective-permute-start.11 = (bf16[416,128]{1,0:T(8,128)(2,1)S(1)}, bf16[416,128]{1,0:T(8,128)(2,1)S(1)}, u32[]{:S(2)}, u32[]{:S(2)}) collective-permute-start(bf16[416,128]{1,0:T(8,128)(2,1)S(1)} %get-tuple-element.57), channel_id=1, source_target_pairs={{0,24},{4,28},{8,16},{12,20},{16,8},{20,12},{24,0},{28,4},{1,25},{... | collective-permute-start | bytes 319496 | tf_op jit(solution)/shard_map/ppermute | solution.py:619
  27.8 6.5 %collective-permute-start.12 = (bf16[416,128]{1,0:T(8,128)(2,1)S(1)}, bf16[416,128]{1,0:T(8,128)(2,1)S(1)}, u32[]{:S(2)}, u32[]{:S(2)}) collective-permute-start(bf16[416,128]{1,0:T(8,128)(2,1)S(1)} %get-tuple-element.58), channel_id=1, source_target_pairs={{0,20},{4,16},{8,28},{12,24},{16,4},{20,0},{24,12},{28,8},{1,21},{... | collective-permute-start | bytes 319496 | tf_op jit(solution)/shard_map/ppermute | solution.py:619
  28.6 6.2 %collective-permute-start.13 = (bf16[416,128]{1,0:T(8,128)(2,1)S(1)}, bf16[416,128]{1,0:T(8,128)(2,1)S(1)}, u32[]{:S(2)}, u32[]{:S(2)}) collective-permute-start(bf16[416,128]{1,0:T(8,128)(2,1)S(1)} %get-tuple-element.59), channel_id=1, source_target_pairs={{0,8},{4,12},{8,0},{12,4},{16,24},{20,28},{24,16},{28,20},{1,9},{5... | collective-permute-start | bytes 319496 | tf_op jit(solution)/shard_map/ppermute | solution.py:619
  29.0 8.0 %collective-permute-start.9 = (bf16[416,128]{1,0:T(8,128)(2,1)S(1)}, bf16[416,128]{1,0:T(8,128)(2,1)S(1)}, u32[]{:S(2)}, u32[]{:S(2)}) collective-permute-start(bf16[416,128]{1,0:T(8,128)(2,1)S(1)} %get-tuple-element.54), channel_id=1, source_target_pairs={{0,16},{4,20},{8,24},{12,28},{16,0},{20,4},{24,8},{28,12},{1,17},{... | collective-permute-start | bytes 319496 | tf_op jit(solution)/shard_map/ppermute | solution.py:619
  30.7 6.3 %collective-permute-start.10 = (bf16[416,128]{1,0:T(8,128)(2,1)S(1)}, bf16[416,128]{1,0:T(8,128)(2,1)S(1)}, u32[]{:S(2)}, u32[]{:S(2)}) collective-permute-start(bf16[416,128]{1,0:T(8,128)(2,1)S(1)} %get-tuple-element.55), channel_id=1, source_target_pairs={{0,12},{4,8},{8,4},{12,0},{16,28},{20,24},{24,20},{28,16},{1,13},{... | collective-permute-start | bytes 319496 | tf_op jit(solution)/shard_map/ppermute | solution.py:619
  32.0 6.2 %collective-permute-start.7 = (bf16[416,128]{1,0:T(8,128)(2,1)S(1)}, bf16[416,128]{1,0:T(8,128)(2,1)S(1)}, u32[]{:S(2)}, u32[]{:S(2)}) collective-permute-start(bf16[416,128]{1,0:T(8,128)(2,1)S(1)} %get-tuple-element.50), channel_id=1, source_target_pairs={{0,28},{4,24},{8,20},{12,16},{16,12},{20,8},{24,4},{28,0},{1,29},{... | collective-permute-start | bytes 319496 | tf_op jit(solution)/shard_map/ppermute | solution.py:619
  34.3 3.9 %collective-permute-start.8 = (bf16[416,128]{1,0:T(8,128)(2,1)S(1)}, bf16[416,128]{1,0:T(8,128)(2,1)S(1)}, u32[]{:S(2)}, u32[]{:S(2)}) collective-permute-start(bf16[416,128]{1,0:T(8,128)(2,1)S(1)} %get-tuple-element.51), channel_id=1, source_target_pairs={{0,4},{4,0},{8,12},{12,8},{16,20},{20,16},{24,28},{28,24},{1,5},{5... | collective-permute-start | bytes 319496 | tf_op jit(solution)/shard_map/ppermute | solution.py:619

commit v8 on v7

--- a/solution.py
+++ b/solution.py
@@ -438,26 +438,27 @@
         mixed, filt = [spec_parts(spec[f], rows, c) for c in range(2)]
         grad = spec_parts(spec_grad[f], rows, 0)
         ys[f] = side_by_side([times_spec(grad, one, True, f == 0) for one in (filt, mixed)])
-    peak[...] = jnp.zeros_like(peak)
-    sums[...] = jnp.zeros_like(sums)
 
     def take(column, b0, ref, source, place):
         found = take_classes(source, place, rows, b0)
         for a, value in enumerate(found):
             ref[pl.ds(a * rows + b0, CHUNK), :] = value
             size = jnp.abs(value)
-            peak[column, a] = jnp.maximum(peak[column, a], jnp.maximum(size[:8], size[8:]))
+            top = jnp.maximum(size[:8], size[8:])
+            peak[column, a] = jnp.maximum(peak[column, a], top) if b0 else top
         return found
 
     def add(i, b0, source, values, other):
-        found = [jnp.zeros((CHUNK, LANES), f32)] * 3
+        found = [None] * 3
         for a, value in enumerate(values):
             at = a * rows + b0
             now = value * other[pl.ds(at, CHUNK), :]
             for j in range(3):
-                found[j] = found[j] + now * source[pl.ds(PAD + at - j, CHUNK), :]
+                term = now * source[pl.ds(PAD + at - j, CHUNK), :]
+                found[j] = found[j] + term if a else term
         for j in range(3):
-            sums[3 * i + j] += found[j][:8] + found[j][8:]
+            line = found[j][:8] + found[j][8:]
+            sums[3 * i + j] = sums[3 * i + j] + line if b0 else line
 
     for f, b0 in zip(classes, chunks):
         zs[f] = table_dot(inverse_ref, f, ys[f])

time: 39.5 us -> 39.5 us (level)
  no operation moved by 1% of the time
where the time goes in v8:
time: 39.5 us; the launch traced here: 39.3 us
  starting transfers between devices  16.4 us (42%)
  Pallas kernels  13.7 us (35%)
  waiting for transfers between devices  7.73 us (20%)
  local copies, waits for them, and re-layouts  0.74 us (2%)
  between operations  0.71 us (2%)
    ppermute x14, starting transfers between devices, swap_blocks(): lax.ppermute(block, 'ctx', [(i, i ^ k) for i in devices])  16.4 us
    ppermute x14, waiting for transfers between devices, swap_blocks(): lax.ppermute(block, 'ctx', [(i, i ^ k) for i in devices])  7.73 us
    pallas_call x1, Pallas kernels, local_fast(): pl.pallas_call(layer_kernel, out_shape=[pltpu.VMEM((3 * rows + HEAD, LANE...  5.49 us
    pallas_call x3, Pallas kernels, local_fast(): pl.pallas_call(partial(finish_kernel, BACK[first:last], len(begun)), out_...  3.44 us
    pallas_call x1, Pallas kernels, local_fast(): pl.pallas_call(prepare_kernel, out_shape=[pltpu.VMEM(forward.shape, bf16)...  3.39 us
    pallas_call x1, Pallas kernels, pack(): pl.pallas_call(partial(pack_kernel, places), out_shape=[pltpu.VMEM((FIELD...  1.38 us
  transfers between devices with their start and end apart: 14, of which 6 were waited for; matrix products, arithmetic and copies ran while one was open for 0% of the time, Pallas kernels for 15%

profile of v8, /device:TPU:0, one launch (start us, length us, event | category | flops | bytes accessed | tf_op | source)
XLA Modules:
  0.0 39.3 jit_solution(5892401254775850912)
XLA Ops:
  0.6 1.4 %pack.1 = (bf16[640,128]{1,0:T(8,128)(2,1)S(1)}, bf16[640,128]{1,0:T(8,128)(2,1)S(1)}, bf16[640,128]{1,0:T(8,128)(2,1)S(1)}, bf16[640,128]{1,0:T(8,128)(2,1)S(1)...) custom-call(s32[1]{0:T(128)} %bitcast.me_ref, ...), custom_call_target="tpu_custom_call" | custom-call | tf_op jit(solution)/shard_map/pack/pallas_call | solution.py:640
  2.0 4.0 %collective-permute-start = (bf16[640,128]{1,0:T(8,128)(2,1)S(1)}, bf16[640,128]{1,0:T(8,128)(2,1)S(1)}, u32[]{:S(2)}, u32[]{:S(2)}) collective-permute-start(bf16[640,128]{1,0:T(8,128)(2,1)S(1)} %get-tuple-element.39), channel_id=1, source_target_pairs={{0,24},{4,28},{8,16},{12,20},{16,8},{20,12},{24,0},{28,4},{1,25},{... | collective-permute-start | bytes 491528 | tf_op jit(solution)/shard_map/ppermute | solution.py:620
  6.0 0.5 %collective-permute-start.1 = (bf16[640,128]{1,0:T(8,128)(2,1)S(1)}, bf16[640,128]{1,0:T(8,128)(2,1)S(1)}, u32[]{:S(2)}, u32[]{:S(2)}) collective-permute-start(bf16[640,128]{1,0:T(8,128)(2,1)S(1)} %get-tuple-element.44), channel_id=1, source_target_pairs={{0,8},{4,12},{8,0},{12,4},{16,24},{20,28},{24,16},{28,20},{1,9},{5... | collective-permute-start | bytes 491528 | tf_op jit(solution)/shard_map/ppermute | solution.py:620
  6.6 0.5 %collective-permute-start.3 = (bf16[640,128]{1,0:T(8,128)(2,1)S(1)}, bf16[640,128]{1,0:T(8,128)(2,1)S(1)}, u32[]{:S(2)}, u32[]{:S(2)}) collective-permute-start(bf16[640,128]{1,0:T(8,128)(2,1)S(1)} %get-tuple-element.46), channel_id=1, source_target_pairs={{0,20},{4,16},{8,28},{12,24},{16,4},{20,0},{24,12},{28,8},{1,21},{... | collective-permute-start | bytes 491528 | tf_op jit(solution)/shard_map/ppermute | solution.py:620
  7.1 2.6 %collective-permute-start.4 = (bf16[640,128]{1,0:T(8,128)(2,1)S(1)}, bf16[640,128]{1,0:T(8,128)(2,1)S(1)}, u32[]{:S(2)}, u32[]{:S(2)}) collective-permute-start(bf16[640,128]{1,0:T(8,128)(2,1)S(1)} %get-tuple-element.47), channel_id=1, source_target_pairs={{0,12},{4,8},{8,4},{12,0},{16,28},{20,24},{24,20},{28,16},{1,13},{... | collective-permute-start | bytes 491528 | tf_op jit(solution)/shard_map/ppermute | solution.py:620
  9.8 1.3 %collective-permute-done._.refs_1_ = bf16[640,128]{1,0:T(8,128)(2,1)S(1)} collective-permute-done((bf16[640,128]{1,0:T(8,128)(2,1)S(1)}, bf16[640,128]{1,0:T(8,128)(2,1)S(1)}, u32[]{:S(2)}, u32[]{:S(2)}) %collective-permute-start) | collective-permute-done | bytes 163872 | tf_op jit(solution)/shard_map/ppermute | solution.py:620
  11.0 0.4 %collective-permute-start.5 = (bf16[640,128]{1,0:T(8,128)(2,1)S(1)}, bf16[640,128]{1,0:T(8,128)(2,1)S(1)}, u32[]{:S(2)}, u32[]{:S(2)}) collective-permute-start(bf16[640,128]{1,0:T(8,128)(2,1)S(1)} %get-tuple-element.48), channel_id=1, source_target_pairs={{0,28},{4,24},{8,20},{12,16},{16,12},{20,8},{24,4},{28,0},{1,29},{... | collective-permute-start | bytes 491528 | tf_op jit(solution)/shard_map/ppermute | solution.py:620
  11.4 3.7 %collective-permute-done.1.refs_2_ = bf16[640,128]{1,0:T(8,128)(2,1)S(1)} collective-permute-done((bf16[640,128]{1,0:T(8,128)(2,1)S(1)}, bf16[640,128]{1,0:T(8,128)(2,1)S(1)}, u32[]{:S(2)}, u32[]{:S(2)}) %collective-permute-start.1) | collective-permute-done | bytes 163872 | tf_op jit(solution)/shard_map/ppermute | solution.py:620
  15.1 0.7 %copy-done = bf16[3,3,1024]{2,1,0:T(4,128)(2,1)S(1)} copy-done((bf16[3,3,1024]{2,1,0:T(4,128)(2,1)S(1)}, bf16[3,3,1024]{2,1,0:T(4,128)(2,1)}, u32[]{:S(2)}) %copy-start) | copy-done | bytes 18456
  15.9 3.4 %prepare.1 = (bf16[2,8,256,256]{3,2,1,0:T(8,128)(2,1)S(1)}, bf16[2,8,256,256]{3,2,1,0:T(8,128)(2,1)S(1)}, f32[16,128]{1,0:T(8,128)S(1)}, f32[16,1024]{1,0:T(8,128)S(1)}, f32[4,128,1024]{2,1,0:T(8,128)S(1)}) custom-call(s32[1]{0:T(128)} %bitcast.me_ref, bf16[2,8,256,256]{3,2,1,0:T(8,128)(2,1)} %constant.10.clone.forward_any, ...), custom_call_target="tpu_custom_call" | custom-call | tf_op jit(solution)/shard_map/prepare/pallas_call | solution.py:657
  19.3 0.7 %collective-permute-done.5.refs_6_ = bf16[640,128]{1,0:T(8,128)(2,1)S(1)} collective-permute-done((bf16[640,128]{1,0:T(8,128)(2,1)S(1)}, bf16[640,128]{1,0:T(8,128)(2,1)S(1)}, u32[]{:S(2)}, u32[]{:S(2)}) %collective-permute-start.5) | collective-permute-done | bytes 163872 | tf_op jit(solution)/shard_map/ppermute | solution.py:620
  20.0 5.5 %layer.1 = (bf16[416,128]{1,0:T(8,128)(2,1)S(1)}, bf16[416,128]{1,0:T(8,128)(2,1)S(1)}, bf16[416,128]{1,0:T(8,128)(2,1)S(1)}, bf16[416,128]{1,0:T(8,128)(2,1)S(1...) custom-call(s32[1]{0:T(128)} %bitcast.me_ref, ...), custom_call_target="tpu_custom_call" | custom-call | tf_op jit(solution)/shard_map/layer/pallas_call | solution.py:673
  25.5 2.3 %collective-permute-start.11 = (bf16[416,128]{1,0:T(8,128)(2,1)S(1)}, bf16[416,128]{1,0:T(8,128)(2,1)S(1)}, u32[]{:S(2)}, u32[]{:S(2)}) collective-permute-start(bf16[416,128]{1,0:T(8,128)(2,1)S(1)} %get-tuple-element.57), channel_id=1, source_target_pairs={{0,24},{4,28},{8,16},{12,20},{16,8},{20,12},{24,0},{28,4},{1,25},{... | collective-permute-start | bytes 319496 | tf_op jit(solution)/shard_map/ppermute | solution.py:620
  27.8 0.8 %collective-permute-start.12 = (bf16[416,128]{1,0:T(8,128)(2,1)S(1)}, bf16[416,128]{1,0:T(8,128)(2,1)S(1)}, u32[]{:S(2)}, u32[]{:S(2)}) collective-permute-start(bf16[416,128]{1,0:T(8,128)(2,1)S(1)} %get-tuple-element.58), channel_id=1, source_target_pairs={{0,20},{4,16},{8,28},{12,24},{16,4},{20,0},{24,12},{28,8},{1,21},{... | collective-permute-start | bytes 319496 | tf_op jit(solution)/shard_map/ppermute | solution.py:620
  28.6 0.5 %collective-permute-start.13 = (bf16[416,128]{1,0:T(8,128)(2,1)S(1)}, bf16[416,128]{1,0:T(8,128)(2,1)S(1)}, u32[]{:S(2)}, u32[]{:S(2)}) collective-permute-start(bf16[416,128]{1,0:T(8,128)(2,1)S(1)} %get-tuple-element.59), channel_id=1, source_target_pairs={{0,8},{4,12},{8,0},{12,4},{16,24},{20,28},{24,16},{28,20},{1,9},{5... | collective-permute-start | bytes 319496 | tf_op jit(solution)/shard_map/ppermute | solution.py:620
  29.0 1.6 %collective-permute-start.9 = (bf16[416,128]{1,0:T(8,128)(2,1)S(1)}, bf16[416,128]{1,0:T(8,128)(2,1)S(1)}, u32[]{:S(2)}, u32[]{:S(2)}) collective-permute-start(bf16[416,128]{1,0:T(8,128)(2,1)S(1)} %get-tuple-element.54), channel_id=1, source_target_pairs={{0,16},{4,20},{8,24},{12,28},{16,0},{20,4},{24,8},{28,12},{1,17},{... | collective-permute-start | bytes 319496 | tf_op jit(solution)/shard_map/ppermute | solution.py:620
  30.7 0.3 collective-permute-start.10
  31.0 1.0 %collective-permute-done.11.refs_1_ = bf16[416,128]{1,0:T(8,128)(2,1)S(1)} collective-permute-done((bf16[416,128]{1,0:T(8,128)(2,1)S(1)}, bf16[416,128]{1,0:T(8,128)(2,1)S(1)}, u32[]{:S(2)}, u32[]{:S(2)}) %collective-permute-start.11) | collective-permute-done | bytes 106528 | tf_op jit(solution)/shard_map/ppermute | solution.py:620
  32.0 2.3 %collective-permute-start.7 = (bf16[416,128]{1,0:T(8,128)(2,1)S(1)}, bf16[416,128]{1,0:T(8,128)(2,1)S(1)}, u32[]{:S(2)}, u32[]{:S(2)}) collective-permute-start(bf16[416,128]{1,0:T(8,128)(2,1)S(1)} %get-tuple-element.50), channel_id=1, source_target_pairs={{0,28},{4,24},{8,20},{12,16},{16,12},{20,8},{24,4},{28,0},{1,29},{... | collective-permute-start | bytes 319496 | tf_op jit(solution)/shard_map/ppermute | solution.py:620
  34.3 0.5 %collective-permute-start.8 = (bf16[416,128]{1,0:T(8,128)(2,1)S(1)}, bf16[416,128]{1,0:T(8,128)(2,1)S(1)}, u32[]{:S(2)}, u32[]{:S(2)}) collective-permute-start(bf16[416,128]{1,0:T(8,128)(2,1)S(1)} %get-tuple-element.51), channel_id=1, source_target_pairs={{0,4},{4,0},{8,12},{12,8},{16,20},{20,16},{24,28},{28,24},{1,5},{5... | collective-permute-start | bytes 319496 | tf_op jit(solution)/shard_map/ppermute | solution.py:620
  34.8 1.4 %finish.3 = (bf16[128,1024]{1,0:T(8,128)(2,1)}, bf16[128,1024]{1,0:T(8,128)(2,1)}, bf16[128,1024]{1,0:T(8,128)(2,1)}, bf16[128,1024]{1,0:T(8,128)(2,1)}, f32[128,1024]{1,0:T(8,128)}, /*index=5*/f32[3,3,1024]{2,1,0:T(4,128)}) custom-call(s32[1]{0:T(128)} %bitcast.me_ref, bf16[416,128]{1,0:T(8,128)(2,1)S(1)} %get-tuple-element.56.refs_0_, ...), custom_call_target="tpu_custom_call" | custom-call | tf_op jit(solution)/shard_map/finish/pallas_call | solution.py:703
  36.2 0.8 %collective-permute-done.9.refs_0_ = bf16[416,128]{1,0:T(8,128)(2,1)S(1)} collective-permute-done((bf16[416,128]{1,0:T(8,128)(2,1)S(1)}, bf16[416,128]{1,0:T(8,128)(2,1)S(1)}, u32[]{:S(2)}, u32[]{:S(2)}) %collective-permute-start.9) | collective-permute-done | bytes 106528 | tf_op jit(solution)/shard_map/ppermute | solution.py:620
  37.0 1.0 %finish.4 = (bf16[128,1024]{1,0:T(8,128)(2,1)}, bf16[128,1024]{1,0:T(8,128)(2,1)}, bf16[128,1024]{1,0:T(8,128)(2,1)}, bf16[128,1024]{1,0:T(8,128)(2,1)}, f32[128,1024]{1,0:T(8,128)}, /*index=5*/f32[3,3,1024]{2,1,0:T(4,128)}) custom-call(s32[1]{0:T(128)} %bitcast.me_ref, ...), custom_call_target="tpu_custom_call", output_to_operand_aliasing={{0}: (5, {}), {1}: (6, {}), {2}: (7, {}), {3}: (8, {}), {4}... | custom-call | tf_op jit(solution)/shard_map/finish/pallas_call | solution.py:703
  38.3 1.0 %finish.5 = (bf16[128,1024]{1,0:T(8,128)(2,1)}, bf16[128,1024]{1,0:T(8,128)(2,1)}, bf16[128,1024]{1,0:T(8,128)(2,1)}, bf16[128,1024]{1,0:T(8,128)(2,1)}, f32[128,1024]{1,0:T(8,128)}, /*index=5*/f32[3,3,1024]{2,1,0:T(4,128)}) custom-call(s32[1]{0:T(128)} %bitcast.me_ref, ...), custom_call_target="tpu_custom_call", output_to_operand_aliasing={{0}: (5, {}), {1}: (6, {}), {2}: (7, {}), {3}: (8, {}), {4}... | custom-call | tf_op jit(solution)/shard_map/finish/pallas_call | solution.py:703
  (12 shorter events, 0.4 us)
Async XLA Ops:
  2.0 9.0 %collective-permute-start = (bf16[640,128]{1,0:T(8,128)(2,1)S(1)}, bf16[640,128]{1,0:T(8,128)(2,1)S(1)}, u32[]{:S(2)}, u32[]{:S(2)}) collective-permute-start(bf16[640,128]{1,0:T(8,128)(2,1)S(1)} %get-tuple-element.39), channel_id=1, source_target_pairs={{0,24},{4,28},{8,16},{12,20},{16,8},{20,12},{24,0},{28,4},{1,25},{... | collective-permute-start | bytes 491528 | tf_op jit(solution)/shard_map/ppermute | solution.py:620
  6.0 9.1 %collective-permute-start.1 = (bf16[640,128]{1,0:T(8,128)(2,1)S(1)}, bf16[640,128]{1,0:T(8,128)(2,1)S(1)}, u32[]{:S(2)}, u32[]{:S(2)}) collective-permute-start(bf16[640,128]{1,0:T(8,128)(2,1)S(1)} %get-tuple-element.44), channel_id=1, source_target_pairs={{0,8},{4,12},{8,0},{12,4},{16,24},{20,28},{24,16},{28,20},{1,9},{5... | collective-permute-start | bytes 491528 | tf_op jit(solution)/shard_map/ppermute | solution.py:620
  6.5 12.8 %collective-permute-start.2 = (bf16[640,128]{1,0:T(8,128)(2,1)S(1)}, bf16[640,128]{1,0:T(8,128)(2,1)S(1)}, u32[]{:S(2)}, u32[]{:S(2)}) collective-permute-start(bf16[640,128]{1,0:T(8,128)(2,1)S(1)} %get-tuple-element.45), channel_id=1, source_target_pairs={{0,16},{4,20},{8,24},{12,28},{16,0},{20,4},{24,8},{28,12},{1,17},{... | collective-permute-start | bytes 491528 | tf_op jit(solution)/shard_map/ppermute | solution.py:620
  6.6 12.7 %collective-permute-start.3 = (bf16[640,128]{1,0:T(8,128)(2,1)S(1)}, bf16[640,128]{1,0:T(8,128)(2,1)S(1)}, u32[]{:S(2)}, u32[]{:S(2)}) collective-permute-start(bf16[640,128]{1,0:T(8,128)(2,1)S(1)} %get-tuple-element.46), channel_id=1, source_target_pairs={{0,20},{4,16},{8,28},{12,24},{16,4},{20,0},{24,12},{28,8},{1,21},{... | collective-permute-start | bytes 491528 | tf_op jit(solution)/shard_map/ppermute | solution.py:620
  7.1 12.2 %collective-permute-start.4 = (bf16[640,128]{1,0:T(8,128)(2,1)S(1)}, bf16[640,128]{1,0:T(8,128)(2,1)S(1)}, u32[]{:S(2)}, u32[]{:S(2)}) collective-permute-start(bf16[640,128]{1,0:T(8,128)(2,1)S(1)} %get-tuple-element.47), channel_id=1, source_target_pairs={{0,12},{4,8},{8,4},{12,0},{16,28},{20,24},{24,20},{28,16},{1,13},{... | collective-permute-start | bytes 491528 | tf_op jit(solution)/shard_map/ppermute | solution.py:620
  11.0 9.0 %collective-permute-start.5 = (bf16[640,128]{1,0:T(8,128)(2,1)S(1)}, bf16[640,128]{1,0:T(8,128)(2,1)S(1)}, u32[]{:S(2)}, u32[]{:S(2)}) collective-permute-start(bf16[640,128]{1,0:T(8,128)(2,1)S(1)} %get-tuple-element.48), channel_id=1, source_target_pairs={{0,28},{4,24},{8,20},{12,16},{16,12},{20,8},{24,4},{28,0},{1,29},{... | collective-permute-start | bytes 491528 | tf_op jit(solution)/shard_map/ppermute | solution.py:620
  15.1 4.9 %collective-permute-start.6 = (bf16[640,128]{1,0:T(8,128)(2,1)S(1)}, bf16[640,128]{1,0:T(8,128)(2,1)S(1)}, u32[]{:S(2)}, u32[]{:S(2)}) collective-permute-start(bf16[640,128]{1,0:T(8,128)(2,1)S(1)} %get-tuple-element.49), channel_id=1, source_target_pairs={{0,4},{4,0},{8,12},{12,8},{16,20},{20,16},{24,28},{28,24},{1,5},{5... | collective-permute-start | bytes 491528 | tf_op jit(solution)/shard_map/ppermute | solution.py:620
  15.1 0.7 %copy-start = (bf16[3,3,1024]{2,1,0:T(4,128)(2,1)S(1)}, bf16[3,3,1024]{2,1,0:T(4,128)(2,1)}, u32[]{:S(2)}) copy-start(bf16[3,3,1024]{2,1,0:T(4,128)(2,1)} %taps_any.1) | copy-start | bytes 55300
  25.5 6.5 %collective-permute-start.11 = (bf16[416,128]{1,0:T(8,128)(2,1)S(1)}, bf16[416,128]{1,0:T(8,128)(2,1)S(1)}, u32[]{:S(2)}, u32[]{:S(2)}) collective-permute-start(bf16[416,128]{1,0:T(8,128)(2,1)S(1)} %get-tuple-element.57), channel_id=1, source_target_pairs={{0,24},{4,28},{8,16},{12,20},{16,8},{20,12},{24,0},{28,4},{1,25},{... | collective-permute-start | bytes 319496 | tf_op jit(solution)/shard_map/ppermute | solution.py:620
  27.8 6.5 %collective-permute-start.12 = (bf16[416,128]{1,0:T(8,128)(2,1)S(1)}, bf16[416,128]{1,0:T(8,128)(2,1)S(1)}, u32[]{:S(2)}, u32[]{:S(2)}) collective-permute-start(bf16[416,128]{1,0:T(8,128)(2,1)S(1)} %get-tuple-element.58), channel_id=1, source_target_pairs={{0,20},{4,16},{8,28},{12,24},{16,4},{20,0},{24,12},{28,8},{1,21},{... | collective-permute-start | bytes 319496 | tf_op jit(solution)/shard_map/ppermute | solution.py:620
  28.6 6.2 %collective-permute-start.13 = (bf16[416,128]{1,0:T(8,128)(2,1)S(1)}, bf16[416,128]{1,0:T(8,128)(2,1)S(1)}, u32[]{:S(2)}, u32[]{:S(2)}) collective-permute-start(bf16[416,128]{1,0:T(8,128)(2,1)S(1)} %get-tuple-element.59), channel_id=1, source_target_pairs={{0,8},{4,12},{8,0},{12,4},{16,24},{20,28},{24,16},{28,20},{1,9},{5... | collective-permute-start | bytes 319496 | tf_op jit(solution)/shard_map/ppermute | solution.py:620
  29.0 8.0 %collective-permute-start.9 = (bf16[416,128]{1,0:T(8,128)(2,1)S(1)}, bf16[416,128]{1,0:T(8,128)(2,1)S(1)}, u32[]{:S(2)}, u32[]{:S(2)}) collective-permute-start(bf16[416,128]{1,0:T(8,128)(2,1)S(1)} %get-tuple-element.54), channel_id=1, source_target_pairs={{0,16},{4,20},{8,24},{12,28},{16,0},{20,4},{24,8},{28,12},{1,17},{... | collective-permute-start | bytes 319496 | tf_op jit(solution)/shard_map/ppermute | solution.py:620
  30.7 6.3 %collective-permute-start.10 = (bf16[416,128]{1,0:T(8,128)(2,1)S(1)}, bf16[416,128]{1,0:T(8,128)(2,1)S(1)}, u32[]{:S(2)}, u32[]{:S(2)}) collective-permute-start(bf16[416,128]{1,0:T(8,128)(2,1)S(1)} %get-tuple-element.55), channel_id=1, source_target_pairs={{0,12},{4,8},{8,4},{12,0},{16,28},{20,24},{24,20},{28,16},{1,13},{... | collective-permute-start | bytes 319496 | tf_op jit(solution)/shard_map/ppermute | solution.py:620
  32.0 6.2 %collective-permute-start.7 = (bf16[416,128]{1,0:T(8,128)(2,1)S(1)}, bf16[416,128]{1,0:T(8,128)(2,1)S(1)}, u32[]{:S(2)}, u32[]{:S(2)}) collective-permute-start(bf16[416,128]{1,0:T(8,128)(2,1)S(1)} %get-tuple-element.50), channel_id=1, source_target_pairs={{0,28},{4,24},{8,20},{12,16},{16,12},{20,8},{24,4},{28,0},{1,29},{... | collective-permute-start | bytes 319496 | tf_op jit(solution)/shard_map/ppermute | solution.py:620
  34.3 3.9 %collective-permute-start.8 = (bf16[416,128]{1,0:T(8,128)(2,1)S(1)}, bf16[416,128]{1,0:T(8,128)(2,1)S(1)}, u32[]{:S(2)}, u32[]{:S(2)}) collective-permute-start(bf16[416,128]{1,0:T(8,128)(2,1)S(1)} %get-tuple-element.51), channel_id=1, source_target_pairs={{0,4},{4,0},{8,12},{12,8},{16,20},{20,16},{24,28},{28,24},{1,5},{5... | collective-permute-start | bytes 319496 | tf_op jit(solution)/shard_map/ppermute | solution.py:620
